TPU v7x, 512 devices: a whole 4x8x8 slice. The times are simulated.
512 devices in a mesh: fsdp: 64 (over y, x, core), tensor: 8 (over z).
Axes of the slice: x: 4, y: 8, z: 8, core: 2. Of those that a mesh axis runs over, the one named last changes fastest.
Arguments:
- momentum: float32 [7168, 28672], P('fsdp', 'tensor'), may hold values from -6 to 6
- gradient: bfloat16 [7168, 28672], P('fsdp', 'tensor'), may hold values from -40 to 40
- basis_panel: float32 [256, 28672], P('fsdp', 'tensor'), may hold values from -0.625 to 0.625
Outputs:
- momentum_new: float32 [7168, 28672], P('fsdp', 'tensor')
- basis_new: float32 [256, 28672], P('fsdp', 'tensor')
- update: bfloat16 [7168, 28672], P('fsdp', 'tensor')
All inputs are finite; a program needn't handle non-finite values.
Results may differ from a plain program's by a relative error of at most 0.0012.
Values sent between devices are 32-bit elements; how exact they have to be, the bound alone decides.
No kernel may reach another device: no remote copies, remote signals or barrier semaphores. Data moves between devices by JAX's collectives and lax.ppermute only.
A program may use at most 64 MiB of HBM per device.

v0:
```python
import math

import jax
import jax.numpy as jnp
from jax import lax
from jax.sharding import PartitionSpec as P

ROWS = 7168
COLS = 28672
RANK = 256


norm_eps = 1e-06
carry_keep = 0.9


def shards(momentum, gradient, basis_panel):
    highest = lax.Precision.HIGHEST
    combined = momentum + gradient.astype(jnp.float32)
    panel_part = lax.dot_general(
        combined,
        lax.all_gather(basis_panel, "fsdp", axis=0, tiled=True),
        (((1,), (1,)), ((), ())),
        precision=highest,
        preferred_element_type=jnp.float32,
    )
    panel_full = lax.psum(panel_part, "tensor")
    panel_squares = jnp.sum(panel_full * panel_full, axis=0)
    update_scale = math.sqrt(ROWS * COLS / RANK)
    squares_all = lax.psum(panel_squares, "fsdp")
    left_panel = panel_full / jnp.sqrt(squares_all + norm_eps)[None, :]
    right_share = lax.psum_scatter(
        lax.dot_general(
            left_panel,
            combined,
            (((0,), (0,)), ((), ())),
            precision=highest,
            preferred_element_type=jnp.float32,
        ),
        "fsdp",
        scatter_dimension=0,
        tiled=True,
    )
    right_squares = lax.psum(jnp.sum(right_share * right_share, axis=1), "tensor")
    right_scale = jnp.sqrt(right_squares + norm_eps)[:, None]
    right_whole, scale_whole = (
        lax.all_gather(right_share, "fsdp", axis=0, tiled=True),
        lax.all_gather(right_scale, "fsdp", axis=0, tiled=True),
    )
    feedback_sum = jnp.dot(
        left_panel, right_whole, precision=highest, preferred_element_type=jnp.float32
    )
    update_sum = jnp.dot(
        left_panel, right_whole / scale_whole, precision=highest, preferred_element_type=jnp.float32
    )
    basis_share = right_share / right_scale
    momentum_new = combined - (1.0 - carry_keep) * feedback_sum
    update = (update_scale * update_sum).astype(jnp.bfloat16)
    return (momentum_new, basis_share, update)


def solution(mesh):
    return jax.shard_map(
        shards,
        mesh=mesh,
        in_specs=(P("fsdp", "tensor"), P("fsdp", "tensor"), P("fsdp", "tensor")),
        out_specs=(P("fsdp", "tensor"), P("fsdp", "tensor"), P("fsdp", "tensor")),
        check_vma=False,
    )
```

profile of v0, /device:TPU:1, one launch (start us, length us, event | category | flops | bytes accessed | tf_op | source)
XLA Modules:
  0.0 685.8 jit_solution(13984997624992476977)
XLA Ops:
  7.2 0.0 all-gather.6.cloned.1.call-start
  7.2 0.7 all-gather.6.cloned.1.call-update
  7.9 0.0 copy-start.1
  7.9 0.0 copy-start.2
  7.9 0.0 all-reduce.5.cloned.1.call-start
  8.0 92.9 %all-gather.6.cloned.1.call-done = f32[64,4,3584]{2,1,0:T(4,128)} async-done(((f32[1,4,3584]{2,1,0:T(4,128)}), f32[64,4,3584]{2,1,0:T(4,128)}) %all-gather.6.cloned.1.call-update) | async-done | bytes 3670032 | tf_op jit(solution)/shard_map/all_gather | solution.py:22
  100.9 5.3 reshape.14
  106.2 0.0 copy-done.1
  106.2 0.0 copy-done.2
  106.2 6.3 fusion.5
  112.5 0.0 all-reduce.5.cloned.1.call-update
  112.6 0.0 all-reduce.7.cloned.1.call-start
  112.6 70.8 %all-reduce.5.cloned.1.call-done = f32[112,256]{1,0:T(8,128)} async-done(((f32[112,256]{1,0:T(8,128)}), f32[112,256]{1,0:T(8,128)}) %all-reduce.5.cloned.1.call-update) | async-done | bytes 114704 | tf_op jit(solution)/shard_map/psum | solution.py:27
  183.4 0.9 multiply_reduce_fusion
  184.3 128.8 %psum.22 = f32[256]{0:T(256)S(1)} all-reduce(f32[256]{0:T(256)S(1)} %multiply_reduce_fusion), channel_id=1, replica_groups=mesh['fsdp'=64,'tensor'=8] {'fsdp'}, use_global_device_ids=true, to_apply=%region_2.0 | all-reduce | flops 256 | bytes 2048 | tf_op jit(solution)/shard_map/psum | solution.py:30
  313.2 5.8 fusion.4
  319.0 0.0 copy-start.4
  319.0 0.0 all-reduce.7.cloned.1.call-update
  319.0 0.0 all-gather.8.cloned.1.call-start
  319.1 0.6 copy-done.4
  319.7 0.6 fusion.7
  320.9 196.8 %all-reduce.7.cloned.1.call-done = f32[256,3584]{1,0:T(8,128)} async-done(((f32[256,3584]{1,0:T(8,128)}), f32[256,3584]{1,0:T(8,128)}) %all-reduce.7.cloned.1.call-update) | async-done | bytes 3670032
  517.8 1.0 multiply_reduce_fusion.1
  519.5 14.6 %psum.23 = f32[4]{0:T(128)S(1)} all-reduce(f32[4]{0:T(128)S(1)} %multiply_reduce_fusion.1), channel_id=1, replica_groups=mesh['fsdp'=64,'tensor'=8] {'tensor'}, use_global_device_ids=true, to_apply=%region_5.0 | all-reduce | flops 4 | bytes 32 | tf_op jit(solution)/shard_map/psum | solution.py:44
  534.1 0.1 fusion.6
  534.2 1.6 dynamic-slice_divide_fusion
  535.8 0.0 all-gather.8.cloned.1.call-update
  535.8 129.4 %all-reduce = f32[256]{0:T(256)S(1)} all-reduce(f32[256]{0:T(256)S(1)} %get-tuple-element.7), channel_id=2, replica_groups=mesh['fsdp'=64,'tensor'=8] {'fsdp'}, use_global_device_ids=true, to_apply=%add | all-reduce | flops 256 | bytes 2048
  665.3 0.0 copy-start.3
  665.3 0.0 all-gather.8.cloned.1.call-done
  665.3 5.3 reshape.16
  670.6 0.0 copy-done.3
  670.6 0.0 copy-start
  670.6 5.5 fusion
  676.1 0.0 copy-done
  676.1 3.2 fusion.1
  (2 shorter events, 0.0 us)
Async XLA Ops:
  7.2 93.7 %all-gather.6.cloned.1.call-start = ((), (), s32[]{:S(2)}) async-start(), calls=%async_computation.1 | async-start | bytes 3727360 | tf_op jit(solution)/shard_map/all_gather | solution.py:22
  7.9 98.3 %copy-start.1 = (f32[112,3584]{1,0:T(8,128)S(1)}, f32[112,3584]{1,0:T(8,128)}, u32[]{:S(2)}) copy-start(f32[112,3584]{1,0:T(8,128)} %param.3) | copy-start | bytes 4816900
  7.9 98.3 %copy-start.2 = (bf16[112,3584]{1,0:T(8,128)(2,1)S(1)}, bf16[112,3584]{1,0:T(8,128)(2,1)}, u32[]{:S(2)}) copy-start(bf16[112,3584]{1,0:T(8,128)(2,1)} %param.4) | copy-start | bytes 2408452
  7.9 175.5 %all-reduce.5.cloned.1.call-start = ((), (), s32[]{:S(2)}) async-start(), calls=%async_computation | async-start | bytes 229376 | tf_op jit(solution)/shard_map/psum | solution.py:27
  112.6 405.2 %all-reduce.7.cloned.1.call-start = ((), (), s32[]{:S(2)}) async-start(), calls=%async_computation.3 | async-start | bytes 7340032
  319.0 0.7 copy-start.4
  319.0 346.3 %all-gather.8.cloned.1.call-start = ((), (), s32[]{:S(2)}) async-start(), calls=%async_computation.2 | async-start | bytes 3727360 | tf_op jit(solution)/shard_map/all_gather | solution.py:47
  665.3 5.3 copy-start.3
  670.6 5.5 copy-start
Sparse Core Ops, SparseCore 0:
  11.3 89.5 all-gather.5
  112.7 70.6 all-reduce.4
  319.1 198.5 all-reduce.6
  536.0 85.3 all-gather.7
where the time goes:
time: 686 us
  waiting for transfers between devices  361 us (53%)
  blocking collectives  273 us (40%)
  matrix products  20.8 us (3%)
  between operations  15.1 us (2%)
  local copies, waits for them, and re-layouts  11.8 us (2%)
    unnamed x5, waiting for transfers between devices  198 us
    unnamed x1, blocking collectives  129 us
    psum x1, blocking collectives, shards(): squares_all = lax.psum(panel_squares, 'fsdp')  129 us
    all_gather x1, waiting for transfers between devices, shards(): lax.all_gather(basis_panel, 'fsdp', axis=0, tiled=True)  92.9 us
    psum x1, waiting for transfers between devices, shards(): panel_full = lax.psum(panel_part, 'tensor')  70.8 us
    psum x1, blocking collectives, shards(): lax.psum(jnp.sum(right_share * right_share, axis=1), 'tensor')  14.6 us
  transfers between devices with their start and end apart: 4, of which 3 were waited for; matrix products, arithmetic and copies ran while one was open for 0% of the time, Pallas kernels for 0%

commit v1 on v0

v1 whole, which is shorter than its diff:
```python
import math

import jax
import jax.numpy as jnp
from jax import lax
from jax.sharding import Mesh, PartitionSpec as P

ROWS = 7168
COLS = 28672
RANK = 256

NY, NX, NC, NZ = 8, 4, 2, 8

norm_eps = 1e-06
carry_keep = 0.9
HIGH = lax.Precision.HIGH
SWAP = [(0, 1), (1, 0)]


def dot(a, b, dims):
    return lax.dot_general(
        a, b, (dims, ((), ())), precision=HIGH, preferred_element_type=jnp.float32
    )


def exchange(blocks, axes):
    return lax.all_to_all(blocks, axes, 0, 0, tiled=True)


def spread(block, axes, n):
    return exchange(jnp.broadcast_to(block[None], (n, *block.shape)), axes)


def shards(momentum, gradient, basis_panel):
    rows, cols = momentum.shape
    rank_rows = basis_panel.shape[0]
    part = cols // NX
    half = NY * NX * rank_rows
    own_ranks = NX * rank_rows
    padded = -(-rows // (8 * NZ)) * 8 * NZ
    chunk = padded // NZ
    combined = momentum + gradient.astype(jnp.float32)

    wide = combined.reshape(rows, NX, part).transpose(1, 0, 2)
    tall = exchange(wide, "x").reshape(NX * rows, part)
    pieces = basis_panel.reshape(rank_rows, NX, part).transpose(1, 0, 2)
    pieces = jnp.broadcast_to(pieces[None], (NY, NX, rank_rows, part))
    basis_own = exchange(pieces.reshape(NY * NX, rank_rows, part), ("y", "x"))
    basis_own = basis_own.reshape(half, part)
    basis_oth = lax.ppermute(basis_own, "core", SWAP)

    panel = jnp.concatenate(
        [dot(tall, basis_own, ((1,), (1,))), dot(tall, basis_oth, ((1,), (1,)))], axis=1
    )
    panel = panel.reshape(NX, rows, 2 * half)
    panel = jnp.pad(panel, ((0, 0), (0, padded - rows), (0, 0)))
    panel = exchange(panel.reshape(NX * NZ, chunk, 2 * half), ("x", "z"))
    panel = spread(jnp.sum(panel, axis=0), ("x", "z"), NX * NZ)
    panel = panel.reshape(NX, padded, 2 * half)[:, :rows]
    mine = lax.dynamic_index_in_dim(panel, lax.axis_index("x"), 0, keepdims=False)
    panel = panel.reshape(NX * rows, 2 * half)

    squares = jnp.sum(panel * panel, axis=0)

    def right(p, q):
        u = dot(p, tall, ((0,), (0,)))
        return jnp.concatenate([u, jnp.broadcast_to(q[:, None], (half, 128))], axis=1)

    right_oth = lax.ppermute(right(panel[:, half:], squares[half:]), "core", SWAP)
    right_sum = right(panel[:, :half], squares[:half]) + right_oth
    right_sum = exchange(right_sum.reshape(NY, own_ranks, part + 128), "y")
    right_sum = jnp.sum(right_sum, axis=0)
    square = right_sum[:, part : part + 1] + norm_eps
    scaled = right_sum[:, :part] / square
    sent = jnp.concatenate([scaled, jnp.broadcast_to(square, (own_ranks, 128))], axis=1)

    got = spread(sent, "y", NY).reshape(half, part + 128)
    scaled, square = got[:, :part], got[:, part]
    row_squares = square * jnp.sum(scaled * scaled, axis=1)
    row_squares = jnp.broadcast_to(row_squares[None, :], (8, half))
    row_squares = jnp.sum(spread(row_squares, ("x", "z"), NX * NZ), axis=0)[0]
    right_scale = jnp.sqrt(row_squares + norm_eps)
    scale_oth = lax.ppermute(right_scale, "core", SWAP)

    own = spread(scaled, "x", NX).transpose(1, 0, 2).reshape(half, cols)
    oth = lax.ppermute(own, "core", SWAP)
    at = lax.axis_index("y") * own_ranks + lax.axis_index("x") * rank_rows
    factor = jnp.sqrt(square) / right_scale
    basis_share = lax.dynamic_slice_in_dim(own, at, rank_rows, 0)
    basis_share = basis_share * lax.dynamic_slice_in_dim(factor, at, rank_rows, 0)[:, None]

    whole_scale = jnp.concatenate([right_scale, scale_oth])
    flat = ((1,), (0,))
    feedback = dot(mine[:, :half], own, flat) + dot(mine[:, half:], oth, flat)
    left = mine / whole_scale[None, :]
    update_sum = dot(left[:, :half], own, flat) + dot(left[:, half:], oth, flat)
    momentum_new = combined - (1.0 - carry_keep) * feedback
    update = (math.sqrt(ROWS * COLS / RANK) * update_sum).astype(jnp.bfloat16)
    return momentum_new, basis_share, update


def solution(mesh):
    fine = Mesh(mesh.devices.reshape(NY, NX, NC, NZ), ("y", "x", "core", "z"))
    spec = P(("y", "x", "core"), "z")
    return jax.shard_map(
        shards,
        mesh=fine,
        in_specs=(spec, spec, spec),
        out_specs=(spec, spec, spec),
        check_vma=False,
    )
```

time: 686 us -> 213 us (0.31)
  waiting for transfers between devices: 361 us -> 35.4 us
  blocking collectives: 273 us -> 93.3 us
  starting transfers between devices: 0.16 us -> 47.5 us
  between operations: 15.1 us -> 0.94 us
    unnamed x5 -> x0, waiting for transfers between devices: 198 us -> none
    psum x2 -> x0, blocking collectives: 143 us -> none  [the longest x1 129 us: shards(): squares_all = lax.psum(panel_squares, 'fsdp')]
    unnamed x1 -> x0, blocking collectives: 129 us -> none
    all_to_all x0 -> x5, blocking collectives: none -> 93.3 us  [exchange(): return lax.all_to_all(blocks, axes, 0, 0, tiled=True)]
    all_gather x2 -> x0, waiting for transfers between devices: 93 us -> none  [the longest x1 92.9 us: shards(): lax.all_gather(basis_panel, 'fsdp', axis=0, tiled=True)]
    psum x1 -> x0, waiting for transfers between devices: 70.8 us -> none  [shards(): panel_full = lax.psum(panel_part, 'tensor')]
    all_to_all x0 -> x3, waiting for transfers between devices: none -> 34.6 us  [exchange(): return lax.all_to_all(blocks, axes, 0, 0, tiled=True)]
    ppermute x0 -> x4, starting transfers between devices: none -> 28.4 us  [the longest x1 8.75 us: shards(): lax.ppermute(right(panel[:, half:], squares[half:]), 'core', SWAP)]
  transfers between devices with their start and end apart: 4 -> 7, of which waited for: 3 -> 4; matrix products, arithmetic and copies ran while one was open for 0% -> 9% of each run, Pallas kernels for 0% -> 0%
where the time goes in v1:
time: 213 us; the launch traced here: 212 us
  blocking collectives  93.3 us (44%)
  starting transfers between devices  47.5 us (22%)
  waiting for transfers between devices  35.4 us (17%)
  matrix products  14.6 us (7%)
  local copies, waits for them, and re-layouts  12.6 us (6%)
  other arithmetic  7.3 us (3%)
    all_to_all x5, blocking collectives, exchange(): return lax.all_to_all(blocks, axes, 0, 0, tiled=True)  93.3 us
    all_to_all x3, waiting for transfers between devices, exchange(): return lax.all_to_all(blocks, axes, 0, 0, tiled=True)  34.6 us
    all_to_all x3, starting transfers between devices, exchange(): return lax.all_to_all(blocks, axes, 0, 0, tiled=True)  19.1 us
    dot_general x8, matrix products, dot(): lax.dot_general(a, b, (dims, ((), ())), precision=HIGH, preferred_element...  14.6 us
    ppermute x1, starting transfers between devices, shards(): lax.ppermute(right(panel[:, half:], squares[half:]), 'core', SWAP)  8.75 us
    ppermute x1, starting transfers between devices, shards(): oth = lax.ppermute(own, 'core', SWAP)  8.31 us
    ppermute x1, starting transfers between devices, shards(): scale_oth = lax.ppermute(right_scale, 'core', SWAP)  6.91 us
    ppermute x1, starting transfers between devices, shards(): basis_oth = lax.ppermute(basis_own, 'core', SWAP)  4.4 us
  transfers between devices with their start and end apart: 7, of which 4 were waited for; matrix products, arithmetic and copies ran while one was open for 9% of the time, Pallas kernels for 0%

profile of v1, /device:TPU:1, one launch (start us, length us, event | category | flops | bytes accessed | tf_op | source)
XLA Modules:
  0.0 211.7 jit_solution(14694077471271558175)
XLA Ops:
  0.6 0.9 reshape.55
  1.6 0.8 broadcast_in_dim.14
  2.4 10.5 %all-to-all-start.1 = ((f32[32,4,896]{2,1,0:T(4,128)}), f32[32,4,896]{2,1,0:T(4,128)S(1)}, u32[]{:S(2)}, u32[]{:S(2)}) async-start(f32[32,4,896]{2,1,0:T(4,128)} %bitcast.3), calls=%async_computation.1 | async-start | bytes 917504 | tf_op jit(solution)/shard_map/all_to_all | solution.py:27
  12.9 1.6 convert_add_fusion
  14.5 1.3 copy.26
  15.8 11.6 %all-to-all-done.1 = f32[32,4,896]{2,1,0:T(4,128)S(1)} async-done(((f32[32,4,896]{2,1,0:T(4,128)}), f32[32,4,896]{2,1,0:T(4,128)S(1)}, u32[]{:S(2)}, u32[]{:S(2)}) %all-to-all-start.1) | async-done | bytes 458784 | tf_op jit(solution)/shard_map/all_to_all | solution.py:27
  27.4 0.8 copy-done.1
  28.1 4.2 %all-to-all-start = ((f32[4,112,896]{2,1,0:T(8,128)}), f32[4,112,896]{2,1,0:T(8,128)S(1)}, u32[]{:S(2)}, u32[]{:S(2)}) async-start(f32[4,112,896]{2,1,0:T(8,128)} %bitcast.45), calls=%async_computation | async-start | bytes 3211264 | tf_op jit(solution)/shard_map/all_to_all | solution.py:27
  32.3 1.9 reshape.57
  34.3 4.4 %collective-permute-start = (f32[128,896]{1,0:T(8,128)}, f32[128,896]{1,0:T(8,128)}, u32[]{:S(2)}, u32[]{:S(2)}) collective-permute-start(f32[128,896]{1,0:T(8,128)} %reshape.57), channel_id=1, source_target_pairs={{0,8},{8,0},{1,9},{9,1},{2,10},{10,2},{3,11},{11,3},{4,12},{12,4},... | collective-permute-start | bytes 1376264 | tf_op jit(solution)/shard_map/ppermute | solution.py:50
  38.7 12.3 %all-to-all-done = f32[4,112,896]{2,1,0:T(8,128)S(1)} async-done(((f32[4,112,896]{2,1,0:T(8,128)}), f32[4,112,896]{2,1,0:T(8,128)S(1)}, u32[]{:S(2)}, u32[]{:S(2)}) %all-to-all-start) | async-done | bytes 1605664 | tf_op jit(solution)/shard_map/all_to_all | solution.py:27
  50.9 1.8 fusion.17
  52.8 1.8 fusion.18
  54.7 22.6 %all_to_all.40 = f32[32,16,256]{2,1,0:T(8,128)} all-to-all(f32[32,16,256]{2,1,0:T(8,128)S(1)} %bitcast.51), channel_id=1, replica_groups=mesh['y'=8,'x'=4,'core'=2,'z'=8] {'x','z'}, dimensions={0} | all-to-all | bytes 1048576 | tf_op jit(solution)/shard_map/all_to_all | solution.py:27
  77.3 1.1 reduce_sum.45
  78.4 18.5 %all_to_all.41 = f32[32,16,256]{2,1,0:T(8,128)S(1)} all-to-all(f32[32,16,256]{2,1,0:T(8,128)S(1)} %broadcast_in_dim.15), channel_id=1, replica_groups=mesh['y'=8,'x'=4,'core'=2,'z'=8] {'x','z'}, dimensions={0} | all-to-all | bytes 1048576 | tf_op jit(solution)/shard_map/all_to_all | solution.py:27
  96.9 0.1 fusion.15
  97.0 0.7 fusion.4
  97.7 0.1 broadcast_in_dim.17
  97.8 0.1 pad_maximum_fusion
  97.8 8.7 %collective-permute-start.1 = (f32[128,1024]{1,0:T(8,128)S(1)}, f32[128,1024]{1,0:T(8,128)S(1)}, u32[]{:S(2)}, u32[]{:S(2)}) collective-permute-start(f32[128,1024]{1,0:T(8,128)S(1)} %pad_maximum_fusion), channel_id=1, source_target_pairs={{0,8},{8,0},{1,9},{9,1},{2,10},{10,2},{3,11},{11,3},{4,12},{12,4},... | collective-permute-start | bytes 1572872 | tf_op jit(solution)/shard_map/ppermute | solution.py:69
  106.6 0.7 fusion.6
  107.3 0.8 collective-permute-done.1
  108.1 0.1 broadcast_in_dim.16
  108.2 0.1 maximum_add_fusion
  108.3 20.5 %all_to_all.42 = f32[8,16,1024]{2,1,0:T(8,128)S(1)} all-to-all(f32[8,16,1024]{2,1,0:T(8,128)S(1)} %bitcast.48), channel_id=1, replica_groups=mesh['y'=8,'x'=4,'core'=2,'z'=8] {'y'}, dimensions={0} | all-to-all | bytes 1048576 | tf_op jit(solution)/shard_map/all_to_all | solution.py:27
  128.8 0.1 fusion.14
  128.9 0.1 slice_divide_fusion
  129.0 0.1 broadcast_in_dim.18
  129.1 0.1 broadcast_in_dim.19
  129.1 17.3 %all_to_all.43 = f32[8,16,1024]{2,1,0:T(8,128)S(1)} all-to-all(f32[8,16,1024]{2,1,0:T(8,128)S(1)} %broadcast_in_dim.19), channel_id=1, replica_groups=mesh['y'=8,'x'=4,'core'=2,'z'=8] {'y'}, dimensions={0} | all-to-all | bytes 1048576 | tf_op jit(solution)/shard_map/all_to_all | solution.py:27
  146.4 0.1 multiply_reduce_fusion
  146.5 0.1 slice_reduce_fusion
  146.7 14.4 %all_to_all.44 = f32[32,8,128]{2,1,0:T(8,128)S(1)} all-to-all(f32[32,8,128]{2,1,0:T(8,128)S(1)} %broadcast_in_dim_broadcast_in_dim_broadcast_in_dim.2), channel_id=1, replica_groups=mesh['y'=8,'x'=4,'core'=2,'z'=8] {'x','z'}, dimensions={0} | all-to-all | bytes 262144 | tf_op jit(solution)/shard_map/all_to_all | solution.py:27
  161.1 1.3 broadcast_in_dim.20
  162.5 4.4 %all-to-all-start.6 = ((f32[4,128,896]{2,1,0:T(8,128)}), f32[4,128,896]{2,1,0:T(8,128)}, u32[]{:S(2)}, u32[]{:S(2)}) async-start(f32[4,128,896]{2,1,0:T(8,128)} %broadcast_in_dim.20), calls=%async_computation.6 | async-start | bytes 3670016 | tf_op jit(solution)/shard_map/all_to_all | solution.py:27
  166.9 6.9 %collective-permute-start.3 = (f32[128]{0:T(128)S(1)}, f32[128]{0:T(128)S(1)}, u32[]{:S(2)}, u32[]{:S(2)}) collective-permute-start(f32[128]{0:T(128)S(1)} %sqrt_bitcast_fusion), channel_id=1, source_target_pairs={{0,8},{8,0},{1,9},{9,1},{2,10},{10,2},{3,11},{11,3},{4,12},{12,4},... | collective-permute-start | bytes 1544 | tf_op jit(solution)/shard_map/ppermute | solution.py:83
  173.9 0.6 dynamic_slice.12
  174.4 10.7 %all-to-all-done.6 = f32[4,128,896]{2,1,0:T(8,128)} async-done(((f32[4,128,896]{2,1,0:T(8,128)}), f32[4,128,896]{2,1,0:T(8,128)}, u32[]{:S(2)}, u32[]{:S(2)}) %all-to-all-start.6) | async-done | bytes 1835040 | tf_op jit(solution)/shard_map/all_to_all | solution.py:27
  185.2 1.8 copy.22
  187.0 8.3 %collective-permute-start.2 = (f32[128,3584]{0,1:T(8,128)S(1)}, f32[128,3584]{0,1:T(8,128)}, u32[]{:S(2)}, u32[]{:S(2)}) collective-permute-start(f32[128,3584]{0,1:T(8,128)S(1)} %bitcast.40), channel_id=1, source_target_pairs={{0,8},{8,0},{1,9},{9,1},{2,10},{10,2},{3,11},{11,3},{4,12},{12,4},... | collective-permute-start | bytes 5505032 | tf_op jit(solution)/shard_map/ppermute | solution.py:86
  195.3 1.6 broadcast_divide_fusion
  196.9 2.4 %dynamic-slice_multiply_fusion = f32[4,3584]{0,1:T(8,128)} fusion(f32[128,3584]{0,1:T(8,128)S(1)} %bitcast.41, s32[]{:T(128)S(6)} %select_n.9, f32[4]{0:T(128)} %dynamic_slice.12), kind=kLoop, calls=%fused_computation.6 | loop fusion | flops 14336 | bytes 114708 | tf_op jit(solution)/shard_map/mul | solution.py:90
  199.3 2.7 %copy.23 = f32[4,3584]{1,0:T(4,128)} copy(f32[4,3584]{0,1:T(8,128)} %dynamic-slice_multiply_fusion) | data formatting | bytes 114688
  202.0 1.7 fusion.12
  203.7 0.9 fusion.9
  204.6 3.7 %fusion.1 = f32[112,3584]{1,0:T(8,128)} fusion(f32[112,3584]{1,0:T(8,128)S(1)} %convert_add_fusion, f32[112,3584]{1,0:T(8,128)S(1)} %fusion.12, f32[128,3584]{0,1:T(8,128)} %collective-permute-done.2, f32[112,256]{1,0:T(8,128)S(1)} %copy-done.3), kind=kOutput, calls=%fused_computation.3 | convolution fusion | flops 309485568 | bytes 6709248 | tf_op jit(solution)/shard_map/dot_general | solution.py:21
  208.3 3.4 %fusion.3 = bf16[112,3584]{1,0:T(8,128)(2,1)} fusion(f32[112,3584]{1,0:T(8,128)S(1)} %fusion.9, f32[128,3584]{0,1:T(8,128)} %collective-permute-done.2, f32[112,256]{1,0:T(8,128)S(1)} %get-tuple-element.9), kind=kOutput, calls=%fused_computation.5 | convolution fusion | flops 309485568 | bytes 4300800 | tf_op jit(solution)/shard_map/dot_general | solution.py:21
  (23 shorter events, 0.3 us)
Async XLA Ops:
  0.6 12.3 %copy-start.2 = (bf16[112,3584]{1,0:T(8,128)(2,1)S(1)}, bf16[112,3584]{1,0:T(8,128)(2,1)}, u32[]{:S(2)}) copy-start(bf16[112,3584]{1,0:T(8,128)(2,1)} %param.4) | copy-start | bytes 2408452
  2.4 24.9 %all-to-all-start.1 = ((f32[32,4,896]{2,1,0:T(4,128)}), f32[32,4,896]{2,1,0:T(4,128)S(1)}, u32[]{:S(2)}, u32[]{:S(2)}) async-start(f32[32,4,896]{2,1,0:T(4,128)} %bitcast.3), calls=%async_computation.1 | async-start | bytes 917504 | tf_op jit(solution)/shard_map/all_to_all | solution.py:27
  27.4 0.8 copy-start.1
  28.1 22.8 %all-to-all-start = ((f32[4,112,896]{2,1,0:T(8,128)}), f32[4,112,896]{2,1,0:T(8,128)S(1)}, u32[]{:S(2)}, u32[]{:S(2)}) async-start(f32[4,112,896]{2,1,0:T(8,128)} %bitcast.45), calls=%async_computation | async-start | bytes 3211264 | tf_op jit(solution)/shard_map/all_to_all | solution.py:27
  34.3 18.5 %collective-permute-start = (f32[128,896]{1,0:T(8,128)}, f32[128,896]{1,0:T(8,128)}, u32[]{:S(2)}, u32[]{:S(2)}) collective-permute-start(f32[128,896]{1,0:T(8,128)} %reshape.57), channel_id=1, source_target_pairs={{0,8},{8,0},{1,9},{9,1},{2,10},{10,2},{3,11},{11,3},{4,12},{12,4},... | collective-permute-start | bytes 1376264 | tf_op jit(solution)/shard_map/ppermute | solution.py:50
  97.0 9.6 %copy-start = (f32[4,112,256]{2,1,0:T(8,128)}, f32[4,112,256]{2,1,0:T(8,128)S(1)}, u32[]{:S(2)}) copy-start(f32[4,112,256]{2,1,0:T(8,128)S(1)} %get-tuple-element.13) | copy-start | bytes 1376260
  97.8 10.3 %collective-permute-start.1 = (f32[128,1024]{1,0:T(8,128)S(1)}, f32[128,1024]{1,0:T(8,128)S(1)}, u32[]{:S(2)}, u32[]{:S(2)}) collective-permute-start(f32[128,1024]{1,0:T(8,128)S(1)} %pad_maximum_fusion), channel_id=1, source_target_pairs={{0,8},{8,0},{1,9},{9,1},{2,10},{10,2},{3,11},{11,3},{4,12},{12,4},... | collective-permute-start | bytes 1572872 | tf_op jit(solution)/shard_map/ppermute | solution.py:69
  162.5 22.7 %all-to-all-start.6 = ((f32[4,128,896]{2,1,0:T(8,128)}), f32[4,128,896]{2,1,0:T(8,128)}, u32[]{:S(2)}, u32[]{:S(2)}) async-start(f32[4,128,896]{2,1,0:T(8,128)} %broadcast_in_dim.20), calls=%async_computation.6 | async-start | bytes 3670016 | tf_op jit(solution)/shard_map/all_to_all | solution.py:27
  166.9 28.4 %collective-permute-start.3 = (f32[128]{0:T(128)S(1)}, f32[128]{0:T(128)S(1)}, u32[]{:S(2)}, u32[]{:S(2)}) collective-permute-start(f32[128]{0:T(128)S(1)} %sqrt_bitcast_fusion), channel_id=1, source_target_pairs={{0,8},{8,0},{1,9},{9,1},{2,10},{10,2},{3,11},{11,3},{4,12},{12,4},... | collective-permute-start | bytes 1544 | tf_op jit(solution)/shard_map/ppermute | solution.py:83
  187.0 17.6 %collective-permute-start.2 = (f32[128,3584]{0,1:T(8,128)S(1)}, f32[128,3584]{0,1:T(8,128)}, u32[]{:S(2)}, u32[]{:S(2)}) collective-permute-start(f32[128,3584]{0,1:T(8,128)S(1)} %bitcast.40), channel_id=1, source_target_pairs={{0,8},{8,0},{1,9},{9,1},{2,10},{10,2},{3,11},{11,3},{4,12},{12,4},... | collective-permute-start | bytes 5505032 | tf_op jit(solution)/shard_map/ppermute | solution.py:86
  203.7 0.9 copy-start.3

commit v2 on v1

v2 whole, which is shorter than its diff:
```python
import functools
import math

import jax
import jax.numpy as jnp
from jax import lax
from jax.experimental import pallas as pl
from jax.experimental.pallas import tpu as pltpu
from jax.sharding import Mesh, PartitionSpec as P

ROWS = 7168
COLS = 28672
RANK = 256

NY, NX, NC, NZ = 8, 4, 2, 8

norm_eps = 1e-06
carry_keep = 0.9
SWAP = [(0, 1), (1, 0)]
PARAMS = pltpu.CompilerParams(vmem_limit_bytes=40 * 1024 * 1024)
SMEM = pl.BlockSpec(memory_space=pltpu.SMEM)


def split(value):
    high = value.astype(jnp.bfloat16)
    return high, (value - high.astype(jnp.float32)).astype(jnp.bfloat16)


def dot3(a, b, dims):
    dot = functools.partial(
        lax.dot_general, dimension_numbers=(dims, ((), ())), preferred_element_type=jnp.float32
    )
    return dot(a[1], b[0]) + dot(a[0], b[1]) + dot(a[0], b[0])


def cost(flops, nbytes):
    return pl.CostEstimate(flops=flops, bytes_accessed=nbytes, transcendentals=0)


def deal_kernel(x_ref, *refs):
    for m_ref, g_ref, o_ref in zip(refs[:NX], refs[NX : 2 * NX], refs[2 * NX :]):
        o_ref[...] = m_ref[...] + g_ref[...].astype(jnp.float32)


def deal(x, momentum, gradient):
    rows, cols = momentum.shape
    part = cols // NX
    block = [
        pl.BlockSpec((rows, part), lambda i, x_ref, j=j: (0, lax.rem(x_ref[0] + j, NX)))
        for j in range(NX)
    ]
    return pl.pallas_call(
        deal_kernel,
        grid_spec=pltpu.PrefetchScalarGridSpec(
            num_scalar_prefetch=1,
            grid=(1,),
            in_specs=block * 2,
            out_specs=[pl.BlockSpec((rows, part), lambda i, x_ref: (0, 0))] * NX,
        ),
        out_shape=[jax.ShapeDtypeStruct((rows, part), jnp.float32)] * NX,
        compiler_params=PARAMS,
        cost_estimate=cost(rows * cols, 10 * rows * cols),
    )(x, *[momentum] * NX, *[gradient] * NX)


def panel_kernel(x_ref, *refs):
    blocks, (own_ref, oth_ref, out_ref) = refs[:NX], refs[NX:]
    rows = blocks[0].shape[0]
    tall = split(jnp.concatenate([ref[...] for ref in blocks], axis=0))
    basis = split(jnp.concatenate([own_ref[...], oth_ref[...]], axis=0))
    panel = dot3(tall, basis, ((1,), (1,)))
    for j in range(NX):
        at = lax.rem(x_ref[0] + (NX - j), NX)
        out_ref[at, :rows] = panel[j * rows : (j + 1) * rows]
        if out_ref.shape[1] > rows:
            spare = (out_ref.shape[1] - rows, out_ref.shape[2])
            out_ref[at, rows:] = jnp.zeros(spare, jnp.float32)


def panel_part(x, blocks, own, oth, padded):
    rows, part = blocks[0].shape
    half = own.shape[0]
    return pl.pallas_call(
        panel_kernel,
        in_specs=[SMEM] + [pl.BlockSpec(memory_space=pltpu.VMEM)] * (NX + 2),
        out_specs=pl.BlockSpec(memory_space=pltpu.VMEM),
        out_shape=jax.ShapeDtypeStruct((NX, padded, 2 * half), jnp.float32),
        compiler_params=PARAMS,
        cost_estimate=cost(12 * NX * rows * part * half, 4 * (NX * rows + 2 * half) * part),
    )(x, *blocks, own, oth)


def right_kernel(side, x_ref, *refs):
    blocks, (panel_ref, out_ref) = refs[:NX], refs[NX:]
    rows, half = blocks[0].shape[0], out_ref.shape[0]
    tall = split(jnp.concatenate([ref[...] for ref in blocks], axis=0))
    panel = [
        panel_ref[lax.rem(x_ref[0] + (NX - j), NX), :rows, side * half : (side + 1) * half]
        for j in range(NX)
    ]
    out_ref[...] = dot3(split(jnp.concatenate(panel, axis=0)), tall, ((0,), (0,)))


def right_part(side, x, blocks, panel):
    rows, part = blocks[0].shape
    half = panel.shape[2] // 2
    return pl.pallas_call(
        functools.partial(right_kernel, side),
        in_specs=[SMEM] + [pl.BlockSpec(memory_space=pltpu.VMEM)] * (NX + 1),
        out_specs=pl.BlockSpec(memory_space=pltpu.VMEM),
        out_shape=jax.ShapeDtypeStruct((half, part), jnp.float32),
        compiler_params=PARAMS,
        cost_estimate=cost(6 * NX * rows * part * half, 4 * NX * rows * part),
    )(x, *blocks, panel)


def low_rank(panel_ref, x, rows, factor, own_ref, oth_ref):
    left = panel_ref[x, :rows] * jnp.concatenate([factor[:1], factor[1:2]], axis=1)
    whole = jnp.concatenate([own_ref[0], oth_ref[0]], axis=0)
    return dot3(split(left), split(whole), ((1,), (0,)))


def momentum_kernel(at_ref, panel_ref, square_ref, m_ref, g_ref, own_ref, oth_ref, out_ref):
    factor = (1.0 - carry_keep) / square_ref[...]
    feedback = low_rank(panel_ref, at_ref[0], m_ref.shape[0], factor, own_ref, oth_ref)
    out_ref[...] = m_ref[...] + g_ref[...].astype(jnp.float32) - feedback


def momentum_out(at, panel, square, momentum, gradient, own, oth):
    rows, cols = momentum.shape
    half, part = own.shape[1:]
    block = pl.BlockSpec((rows, part), lambda j: (0, j))
    right = pl.BlockSpec((1, half, part), lambda j: (j, 0, 0))
    return pl.pallas_call(
        momentum_kernel,
        grid=(NX,),
        in_specs=[
            SMEM,
            pl.BlockSpec(panel.shape, lambda j: (0, 0, 0)),
            pl.BlockSpec(square.shape, lambda j: (0, 0)),
            block,
            block,
            right,
            right,
        ],
        out_specs=block,
        out_shape=jax.ShapeDtypeStruct((rows, cols), jnp.float32),
        compiler_params=PARAMS,
        cost_estimate=cost(12 * rows * cols * half, 4 * (3 * rows + 2 * half) * cols),
    )(at, panel, square, momentum, gradient, own, oth)


def update_kernel(at_ref, panel_ref, square_ref, sums_ref, own_ref, oth_ref, out_ref, basis_ref):
    square = square_ref[...]
    right_scale = jnp.sqrt(sums_ref[...] / square + norm_eps)
    factor = math.sqrt(ROWS * COLS / RANK) / (square * right_scale)
    rows, (ranks, _) = out_ref.shape[0], basis_ref.shape
    update = low_rank(panel_ref, at_ref[0], rows, factor, own_ref, oth_ref)
    out_ref[...] = update.astype(jnp.bfloat16)
    first = at_ref[1]
    group = pl.multiple_of(first // 8 * 8, 8)
    eight = own_ref[0, pl.ds(group, 8), :]
    lane = lax.broadcasted_iota(jnp.int32, (8, square.shape[1]), 1)
    row = lax.broadcasted_iota(jnp.int32, (8, square.shape[1]), 0)
    scale = 1.0 / (jnp.sqrt(square[:1]) * right_scale[:1])
    scale = jnp.sum(jnp.where(lane == row + group, scale, 0.0), axis=1, keepdims=True)
    eight = eight * scale
    basis_ref[...] = jnp.where(first > group, eight[8 - ranks :], eight[:ranks])


def update_out(at, panel, square, sums, own, oth, rows, ranks):
    half, part = own.shape[1:]
    cols = NX * part
    right = pl.BlockSpec((1, half, part), lambda j: (j, 0, 0))
    small = pl.BlockSpec(square.shape, lambda j: (0, 0))
    return pl.pallas_call(
        update_kernel,
        grid=(NX,),
        in_specs=[SMEM, pl.BlockSpec(panel.shape, lambda j: (0, 0, 0)), small, small, right, right],
        out_specs=[
            pl.BlockSpec((rows, part), lambda j: (0, j)),
            pl.BlockSpec((ranks, part), lambda j: (0, j)),
        ],
        out_shape=[
            jax.ShapeDtypeStruct((rows, cols), jnp.bfloat16),
            jax.ShapeDtypeStruct((ranks, cols), jnp.float32),
        ],
        compiler_params=PARAMS,
        cost_estimate=cost(12 * rows * cols * half, 4 * (rows + 2 * half) * cols),
    )(at, panel, square, sums, own, oth)


def exchange(blocks, axes):
    return lax.all_to_all(blocks, axes, 0, 0, tiled=True)


def spread(block, axes, n):
    return exchange(jnp.broadcast_to(block[None], (n, *block.shape)), axes)


def shards(momentum, gradient, basis_panel):
    rows, cols = momentum.shape
    rank_rows = basis_panel.shape[0]
    part = cols // NX
    half = NY * NX * rank_rows
    own_ranks = NX * rank_rows
    padded = -(-rows // (8 * NZ)) * 8 * NZ
    x, core = lax.axis_index("x"), lax.axis_index("core")
    at = jnp.stack([x, lax.axis_index("y") * own_ranks + x * rank_rows]).astype(jnp.int32)

    pieces = basis_panel.reshape(rank_rows, NX, part).transpose(1, 0, 2)
    pieces = jnp.broadcast_to(pieces[None], (NY, NX, rank_rows, part))
    basis_own = exchange(pieces.reshape(NY * NX, rank_rows, part), ("y", "x"))
    blocks = deal(at, momentum, gradient)
    blocks = [blocks[0]] + [
        lax.ppermute(blocks[j], "x", [(i, (i + j) % NX) for i in range(NX)]) for j in range(1, NX)
    ]
    basis_own = basis_own.reshape(half, part)
    basis_oth = lax.ppermute(basis_own, "core", SWAP)

    panel = panel_part(at, blocks, basis_own, basis_oth, padded)
    panel = exchange(panel.reshape(NX * NZ, padded // NZ, 2 * half), ("x", "z"))
    panel = spread(jnp.sum(panel, axis=0), ("x", "z"), NX * NZ)
    panel = panel.reshape(NX, padded, 2 * half)

    right_oth = lax.ppermute(right_part(1, at, blocks, panel), "core", SWAP)
    right_sum = right_part(0, at, blocks, panel) + right_oth
    right_sum = jnp.sum(exchange(right_sum.reshape(NY, own_ranks, part), "y"), axis=0)

    square = jnp.sum(panel * panel, axis=(0, 1)).reshape(2, half)
    beside = jnp.zeros((own_ranks, 128), jnp.float32).at[:2, :half].set(square)
    got = spread(jnp.concatenate([right_sum, beside], axis=1), "y", NY)
    square = jnp.sum(got[:, :2, part : part + half], axis=0)
    square = square + lax.ppermute(square, "core", SWAP)[::-1] + norm_eps

    own = spread(got[:, :, :part].reshape(half, part), "x", NX)
    oth = lax.ppermute(own, "core", SWAP)
    sums = jnp.broadcast_to(jnp.sum(own * own, axis=(0, 2)), (8, half))
    sums = jnp.sum(spread(sums, ("core", "z"), NC * NZ).reshape(NC, NZ, 8, half), axis=1)[:, 0]
    sums = jnp.where(core == 0, sums, sums[::-1])

    momentum_new = momentum_out(at, panel, square, momentum, gradient, own, oth)
    update, basis_new = update_out(at, panel, square, sums, own, oth, rows, rank_rows)
    return momentum_new, basis_new, update


def solution(mesh):
    fine = Mesh(mesh.devices.reshape(NY, NX, NC, NZ), ("y", "x", "core", "z"))
    spec = P(("y", "x", "core"), "z")
    return jax.shard_map(
        shards,
        mesh=fine,
        in_specs=(spec, spec, spec),
        out_specs=(spec, spec, spec),
        check_vma=False,
    )
```

time: 213 us -> 217 us (1.019)
  waiting for transfers between devices: 35.4 us -> 54.8 us
  matrix products: 14.6 us -> 0 us
  Pallas kernels: 0 us -> 14.1 us
  other arithmetic: 7.3 us -> 1.31 us
  local copies, waits for them, and re-layouts: 12.6 us -> 6.67 us
  starting transfers between devices: 47.5 us -> 45.1 us
    ppermute x2 -> x5, waiting for transfers between devices: 0.84 us -> 16.8 us  [the longest x3 15.1 us: shards(): lax.ppermute(blocks[j], 'x', [(i, (i + j) % NX) for i in range(NX)])]
    dot_general x8 -> x0, matrix products: 14.6 us -> none  [dot(): lax.dot_general(a, b, (dims, ((), ())), precision=HIGH, preferred_element...]
    pallas_call x0 -> x6, Pallas kernels: none -> 14.1 us  [the longest x1 4.53 us: momentum_out(): pl.pallas_call(momentum_kernel, grid=(NX,), in_specs=[SMEM, pl.BlockSpec(...]
    ppermute x1, starting transfers between devices: 8.31 us -> 3.64 us  [shards(): oth = lax.ppermute(own, 'core', SWAP)]
    all_to_all x3, waiting for transfers between devices: 34.6 us -> 38 us  [exchange(): return lax.all_to_all(blocks, axes, 0, 0, tiled=True)]
    mul x2 -> x0, other arithmetic: 2.43 us -> none  [the longest x1 2.42 us: shards(): basis_share * lax.dynamic_slice_in_dim(factor, at, rank_rows, 0)[:, None]]
    ppermute x2 -> x5, starting transfers between devices: 15.7 us -> 18 us  [the longest x3 9.66 us: shards(): lax.ppermute(blocks[j], 'x', [(i, (i + j) % NX) for i in range(NX)])]
    all_to_all x5 -> x4, blocking collectives: 93.3 us -> 93.7 us  [exchange(): return lax.all_to_all(blocks, axes, 0, 0, tiled=True)]
  transfers between devices with their start and end apart: 7 -> 10, of which waited for: 4 -> 8; matrix products, arithmetic and copies ran while one was open for 9% -> 1% of each run, Pallas kernels for 0% -> 1%
where the time goes in v2:
time: 217 us
  blocking collectives  93.7 us (43%)
  waiting for transfers between devices  54.8 us (25%)
  starting transfers between devices  45.1 us (21%)
  Pallas kernels  14.1 us (6%)
  local copies, waits for them, and re-layouts  6.67 us (3%)
    all_to_all x4, blocking collectives, exchange(): return lax.all_to_all(blocks, axes, 0, 0, tiled=True)  93.7 us
    all_to_all x3, waiting for transfers between devices, exchange(): return lax.all_to_all(blocks, axes, 0, 0, tiled=True)  38 us
    all_to_all x3, starting transfers between devices, exchange(): return lax.all_to_all(blocks, axes, 0, 0, tiled=True)  18.4 us
    ppermute x3, waiting for transfers between devices, shards(): lax.ppermute(blocks[j], 'x', [(i, (i + j) % NX) for i in range(NX)])  15.1 us
    ppermute x3, starting transfers between devices, shards(): lax.ppermute(blocks[j], 'x', [(i, (i + j) % NX) for i in range(NX)])  9.66 us
    ppermute x1, starting transfers between devices, shards(): right_oth = lax.ppermute(right_part(1, at, blocks, panel), 'core', SWAP)  6.46 us
    ppermute x1, starting transfers between devices, shards(): basis_oth = lax.ppermute(basis_own, 'core', SWAP)  5.01 us
    pallas_call x1, Pallas kernels, momentum_out(): pl.pallas_call(momentum_kernel, grid=(NX,), in_specs=[SMEM, pl.BlockSpec(...  4.53 us
  transfers between devices with their start and end apart: 10, of which 8 were waited for; matrix products, arithmetic and copies ran while one was open for 1% of the time, Pallas kernels for 1%

profile of v2, /device:TPU:1, one launch (start us, length us, event | category | flops | bytes accessed | tf_op | source)
XLA Modules:
  0.0 216.5 jit_solution(3593270055832855858)
XLA Ops:
  0.6 0.0 copy-start.1
  0.7 1.0 reshape.60
  1.7 0.8 broadcast_in_dim.10
  2.5 10.5 %all-to-all-start = ((f32[32,4,896]{2,1,0:T(4,128)}), f32[32,4,896]{2,1,0:T(4,128)S(1)}, u32[]{:S(2)}, u32[]{:S(2)}) async-start(f32[32,4,896]{2,1,0:T(4,128)} %bitcast.3), calls=%async_computation | async-start | bytes 917504 | tf_op jit(solution)/shard_map/all_to_all | solution.py:194
  13.0 14.4 %all-to-all-done = f32[32,4,896]{2,1,0:T(4,128)S(1)} async-done(((f32[32,4,896]{2,1,0:T(4,128)}), f32[32,4,896]{2,1,0:T(4,128)S(1)}, u32[]{:S(2)}, u32[]{:S(2)}) %all-to-all-start) | async-done | bytes 458784 | tf_op jit(solution)/shard_map/all_to_all | solution.py:194
  27.4 0.9 reshape.62.refs_4_
  28.4 5.0 %collective-permute-start.3 = (f32[128,896]{1,0:T(8,128)}, f32[128,896]{1,0:T(8,128)S(1)}, u32[]{:S(2)}, u32[]{:S(2)}) collective-permute-start(f32[128,896]{1,0:T(8,128)} %reshape.62.refs_4_), channel_id=1, source_target_pairs={{0,8},{8,0},{1,9},{9,1},{2,10},{10,2},{3,11},{11,3},{4,12},{12,4},... | collective-permute-start | bytes 1376264 | tf_op jit(solution)/shard_map/ppermute | solution.py:219
  33.4 0.1 pad_add_fusion.x_ref.at_ref
  33.5 0.0 copy-done.1
  33.5 0.8 shard_map.58
  34.2 2.3 %collective-permute-start = (f32[112,896]{1,0:T(8,128)S(1)}, f32[112,896]{1,0:T(8,128)S(1)}, u32[]{:S(2)}, u32[]{:S(2)}) collective-permute-start(f32[112,896]{1,0:T(8,128)S(1)} %get-tuple-element.22), channel_id=1, source_target_pairs={{0,16},{16,32},{32,48},{48,0},{1,17},{17,33},{33,49},{49,1},{2,18}... | collective-permute-start | bytes 1204232 | tf_op jit(solution)/shard_map/ppermute | solution.py:216
  36.5 4.3 %collective-permute-start.1 = (f32[112,896]{1,0:T(8,128)S(1)}, f32[112,896]{1,0:T(8,128)S(1)}, u32[]{:S(2)}, u32[]{:S(2)}) collective-permute-start(f32[112,896]{1,0:T(8,128)S(1)} %get-tuple-element.23), channel_id=1, source_target_pairs={{0,32},{16,48},{32,0},{48,16},{1,33},{17,49},{33,1},{49,17},{2,34}... | collective-permute-start | bytes 1204232 | tf_op jit(solution)/shard_map/ppermute | solution.py:216
  40.8 3.1 %collective-permute-start.2 = (f32[112,896]{1,0:T(8,128)S(1)}, f32[112,896]{1,0:T(8,128)S(1)}, u32[]{:S(2)}, u32[]{:S(2)}) collective-permute-start(f32[112,896]{1,0:T(8,128)S(1)} %get-tuple-element.24), channel_id=1, source_target_pairs={{0,48},{16,0},{32,16},{48,32},{1,49},{17,1},{33,17},{49,33},{2,50}... | collective-permute-start | bytes 1204232 | tf_op jit(solution)/shard_map/ppermute | solution.py:216
  43.9 4.3 %collective-permute-done.refs_1_ = f32[112,896]{1,0:T(8,128)S(1)} collective-permute-done((f32[112,896]{1,0:T(8,128)S(1)}, f32[112,896]{1,0:T(8,128)S(1)}, u32[]{:S(2)}, u32[]{:S(2)}) %collective-permute-start) | collective-permute-done | bytes 401440 | tf_op jit(solution)/shard_map/ppermute | solution.py:216
  48.3 8.7 %collective-permute-done.1.refs_2_ = f32[112,896]{1,0:T(8,128)S(1)} collective-permute-done((f32[112,896]{1,0:T(8,128)S(1)}, f32[112,896]{1,0:T(8,128)S(1)}, u32[]{:S(2)}, u32[]{:S(2)}) %collective-permute-start.1) | collective-permute-done | bytes 401440 | tf_op jit(solution)/shard_map/ppermute | solution.py:216
  56.9 2.1 collective-permute-done.2.refs_3_
  59.1 0.0 collective-permute-done.3.refs_5_
  59.1 2.1 shard_map.59
  61.2 0.0 copy-start.6
  61.2 0.7 copy-done.6
  62.0 27.0 %all_to_all.35 = f32[32,16,256]{2,1,0:T(8,128)S(1)} all-to-all(f32[32,16,256]{2,1,0:T(8,128)S(1)} %bitcast.18), channel_id=1, replica_groups=mesh['y'=8,'x'=4,'core'=2,'z'=8] {'x','z'}, dimensions={0} | all-to-all | bytes 1048576 | tf_op jit(solution)/shard_map/all_to_all | solution.py:194
  89.1 0.0 copy-start.7
  89.1 0.1 broadcast_in_dim.11
  89.1 21.2 %all_to_all.36 = f32[32,16,256]{2,1,0:T(8,128)S(1)} all-to-all(f32[32,16,256]{2,1,0:T(8,128)S(1)} %broadcast_in_dim.11), channel_id=1, replica_groups=mesh['y'=8,'x'=4,'core'=2,'z'=8] {'x','z'}, dimensions={0} | all-to-all | bytes 1048576 | tf_op jit(solution)/shard_map/all_to_all | solution.py:194
  110.4 1.2 shard_map.61
  111.6 6.5 %collective-permute-start.4 = (f32[128,896]{1,0:T(8,128)S(1)}, f32[128,896]{1,0:T(8,128)S(1)}, u32[]{:S(2)}, u32[]{:S(2)}) collective-permute-start(f32[128,896]{1,0:T(8,128)S(1)} %shard_map.61), channel_id=1, source_target_pairs={{0,8},{8,0},{1,9},{9,1},{2,10},{10,2},{3,11},{11,3},{4,12},{12,4},... | collective-permute-start | bytes 1376264 | tf_op jit(solution)/shard_map/ppermute | solution.py:226
  118.0 1.2 shard_map.60
  119.2 0.2 collective-permute-done.4
  119.5 0.8 add.20
  120.3 3.5 %all-to-all-start.3 = ((f32[8,16,896]{2,1,0:T(8,128)}), f32[8,16,896]{2,1,0:T(8,128)S(1)}, u32[]{:S(2)}, u32[]{:S(2)}) async-start(f32[8,16,896]{2,1,0:T(8,128)} %bitcast.6), calls=%async_computation.3 | async-start | bytes 917504 | tf_op jit(solution)/shard_map/all_to_all | solution.py:194
  123.8 0.1 multiply_reduce_fusion.1
  123.9 16.4 %all-to-all-done.3 = f32[8,16,896]{2,1,0:T(8,128)S(1)} async-done(((f32[8,16,896]{2,1,0:T(8,128)}), f32[8,16,896]{2,1,0:T(8,128)S(1)}, u32[]{:S(2)}, u32[]{:S(2)}) %all-to-all-start.3) | async-done | bytes 458784 | tf_op jit(solution)/shard_map/all_to_all | solution.py:194
  140.3 20.3 %all_to_all.37 = f32[8,16,1024]{2,1,0:T(8,128)S(1)} all-to-all(f32[8,16,1024]{2,1,0:T(8,128)S(1)} %broadcast_in_dim.12), channel_id=1, replica_groups=mesh['y'=8,'x'=4,'core'=2,'z'=8] {'y'}, dimensions={0} | all-to-all | bytes 1048576 | tf_op jit(solution)/shard_map/all_to_all | solution.py:194
  160.6 0.1 broadcast_in_dim.14
  160.8 25.2 %all_to_all.38.own_ref = f32[4,128,896]{2,1,0:T(8,128)S(1)} all-to-all(f32[4,128,896]{2,1,0:T(8,128)S(1)} %broadcast_in_dim.14), channel_id=1, replica_groups=mesh['y'=8,'x'=4,'core'=2,'z'=8] {'x'}, dimensions={0} | all-to-all | bytes 3670016 | tf_op jit(solution)/shard_map/all_to_all | solution.py:194
  186.0 3.6 %collective-permute-start.6 = (f32[4,128,896]{2,1,0:T(8,128)S(1)}, f32[4,128,896]{2,1,0:T(8,128)}, u32[]{:S(2)}, u32[]{:S(2)}) collective-permute-start(f32[4,128,896]{2,1,0:T(8,128)S(1)} %all_to_all.38.own_ref), channel_id=1, source_target_pairs={{0,8},{8,0},{1,9},{9,1},{2,10},{10,2},{3,11},{11,3},{4,12},{12,4},... | collective-permute-start | bytes 5505032 | tf_op jit(solution)/shard_map/ppermute | solution.py:237
  189.6 1.9 collective-permute-start.5
  191.6 1.4 collective-permute-done.5
  193.0 0.2 multiply_reduce_fusion
  193.2 0.6 broadcast_in_dim_broadcast_in_dim_broadcast_in_dim.3
  193.9 4.4 %all-to-all-start.6 = ((f32[16,8,128]{2,1,0:T(8,128)}), f32[16,8,128]{2,1,0:T(8,128)S(1)}, u32[]{:S(2)}, u32[]{:S(2)}) async-start(f32[16,8,128]{2,1,0:T(8,128)} %broadcast_in_dim_broadcast_in_dim_broadcast_in_dim.3), calls=%async_computation.6 | async-start | bytes 131072 | tf_op jit(solution)/shard_map/all_to_all | solution.py:194
  198.3 7.2 %all-to-all-done.6 = f32[16,8,128]{2,1,0:T(8,128)S(1)} async-done(((f32[16,8,128]{2,1,0:T(8,128)}), f32[16,8,128]{2,1,0:T(8,128)S(1)}, u32[]{:S(2)}, u32[]{:S(2)}) %all-to-all-start.6) | async-done | bytes 65568 | tf_op jit(solution)/shard_map/all_to_all | solution.py:194
  205.5 0.0 collective-permute-done.6.oth_ref
  205.5 0.0 copy-start.2
  205.5 1.1 copy-done.2
  206.7 1.0 copy-done.4
  207.7 4.5 %shard_map.62 = f32[112,3584]{1,0:T(8,128)} custom-call(s32[2]{0:T(128)S(1)} %pad_add_fusion.x_ref.at_ref, f32[4,128,256]{2,1,0:T(8,128)S(1)} %bitcast.16, f32[2,128]{1,0:T(2,128)S(1)} %add_add_fusion.square_ref, f32[112,3584]{1,0:T(8,128)S(1)} %copy-done, bf16[112,3584]{1,0:T(8,128)(2,1)S(1)} %copy-done.2, f32[4,128,896]{2,1,0:T(8,128)S(1)} %all_to_all.38.own_ref, ...), custom_call_target="tpu_custom_call" | custom-call | flops 616562688 | bytes 8486912 | tf_op jit(solution)/shard_map/pallas_call | solution.py:134
  212.2 4.3 %shard_map.63 = (bf16[112,3584]{1,0:T(8,128)(2,1)}, f32[4,3584]{1,0:T(4,128)}) custom-call(s32[2]{0:T(128)S(1)} %pad_add_fusion.x_ref.at_ref, f32[4,128,256]{2,1,0:T(8,128)S(1)} %bitcast.17, f32[2,128]{1,0:T(2,128)S(1)} %add_add_fusion.square_ref, f32[2,128]{1,0:T(2,128)S(1)} %broadcast_select_fusion.sums_ref, f32[4,128,896]{2,1,0:T(8,128)S(1)} %all_to_all.38.own_ref, ...), custom_call_target="tpu_custom_call" | custom-call | flops 616562688 | bytes 5275648 | tf_op jit(solution)/shard_map/pallas_call | solution.py:176
  (25 shorter events, 0.3 us)
Async XLA Ops:
  0.6 32.8 %copy-start = (f32[112,3584]{1,0:T(8,128)S(1)}, f32[112,3584]{1,0:T(8,128)}, u32[]{:S(2)}) copy-start(f32[112,3584]{1,0:T(8,128)} %m_ref.1) | copy-start | bytes 4816900
  0.6 32.8 %copy-start.1 = (bf16[112,3584]{1,0:T(8,128)(2,1)S(1)}, bf16[112,3584]{1,0:T(8,128)(2,1)}, u32[]{:S(2)}) copy-start(bf16[112,3584]{1,0:T(8,128)(2,1)} %g_ref.1) | copy-start | bytes 2408452
  2.5 24.9 %all-to-all-start = ((f32[32,4,896]{2,1,0:T(4,128)}), f32[32,4,896]{2,1,0:T(4,128)S(1)}, u32[]{:S(2)}, u32[]{:S(2)}) async-start(f32[32,4,896]{2,1,0:T(4,128)} %bitcast.3), calls=%async_computation | async-start | bytes 917504 | tf_op jit(solution)/shard_map/all_to_all | solution.py:194
  28.4 30.7 %collective-permute-start.3 = (f32[128,896]{1,0:T(8,128)}, f32[128,896]{1,0:T(8,128)S(1)}, u32[]{:S(2)}, u32[]{:S(2)}) collective-permute-start(f32[128,896]{1,0:T(8,128)} %reshape.62.refs_4_), channel_id=1, source_target_pairs={{0,8},{8,0},{1,9},{9,1},{2,10},{10,2},{3,11},{11,3},{4,12},{12,4},... | collective-permute-start | bytes 1376264 | tf_op jit(solution)/shard_map/ppermute | solution.py:219
  34.2 14.0 %collective-permute-start = (f32[112,896]{1,0:T(8,128)S(1)}, f32[112,896]{1,0:T(8,128)S(1)}, u32[]{:S(2)}, u32[]{:S(2)}) collective-permute-start(f32[112,896]{1,0:T(8,128)S(1)} %get-tuple-element.22), channel_id=1, source_target_pairs={{0,16},{16,32},{32,48},{48,0},{1,17},{17,33},{33,49},{49,1},{2,18}... | collective-permute-start | bytes 1204232 | tf_op jit(solution)/shard_map/ppermute | solution.py:216
  36.5 20.4 %collective-permute-start.1 = (f32[112,896]{1,0:T(8,128)S(1)}, f32[112,896]{1,0:T(8,128)S(1)}, u32[]{:S(2)}, u32[]{:S(2)}) collective-permute-start(f32[112,896]{1,0:T(8,128)S(1)} %get-tuple-element.23), channel_id=1, source_target_pairs={{0,32},{16,48},{32,0},{48,16},{1,33},{17,49},{33,1},{49,17},{2,34}... | collective-permute-start | bytes 1204232 | tf_op jit(solution)/shard_map/ppermute | solution.py:216
  40.8 18.3 %collective-permute-start.2 = (f32[112,896]{1,0:T(8,128)S(1)}, f32[112,896]{1,0:T(8,128)S(1)}, u32[]{:S(2)}, u32[]{:S(2)}) collective-permute-start(f32[112,896]{1,0:T(8,128)S(1)} %get-tuple-element.24), channel_id=1, source_target_pairs={{0,48},{16,0},{32,16},{48,32},{1,49},{17,1},{33,17},{49,33},{2,50}... | collective-permute-start | bytes 1204232 | tf_op jit(solution)/shard_map/ppermute | solution.py:216
  59.1 2.1 copy-start.8
  61.2 0.8 copy-start.6
  89.1 21.3 %copy-start.7 = (f32[112,896]{1,0:T(8,128)S(1)}, f32[112,896]{1,0:T(8,128)}, u32[]{:S(2)}) copy-start(f32[112,896]{1,0:T(8,128)} %copy-done.6) | copy-start | bytes 1204228
  89.1 21.3 %copy-start.9 = (f32[112,896]{1,0:T(8,128)S(1)}, f32[112,896]{1,0:T(8,128)}, u32[]{:S(2)}) copy-start(f32[112,896]{1,0:T(8,128)} %copy-done.8) | copy-start | bytes 1204228
  110.4 13.4 %copy-start.3 = (f32[32,16,256]{2,1,0:T(8,128)}, f32[32,16,256]{2,1,0:T(8,128)S(1)}, u32[]{:S(2)}) copy-start(f32[32,16,256]{2,1,0:T(8,128)S(1)} %all_to_all.36) | copy-start | bytes 1572868
  111.6 7.9 %collective-permute-start.4 = (f32[128,896]{1,0:T(8,128)S(1)}, f32[128,896]{1,0:T(8,128)S(1)}, u32[]{:S(2)}, u32[]{:S(2)}) collective-permute-start(f32[128,896]{1,0:T(8,128)S(1)} %shard_map.61), channel_id=1, source_target_pairs={{0,8},{8,0},{1,9},{9,1},{2,10},{10,2},{3,11},{11,3},{4,12},{12,4},... | collective-permute-start | bytes 1376264 | tf_op jit(solution)/shard_map/ppermute | solution.py:226
  120.3 20.0 %all-to-all-start.3 = ((f32[8,16,896]{2,1,0:T(8,128)}), f32[8,16,896]{2,1,0:T(8,128)S(1)}, u32[]{:S(2)}, u32[]{:S(2)}) async-start(f32[8,16,896]{2,1,0:T(8,128)} %bitcast.6), calls=%async_computation.3 | async-start | bytes 917504 | tf_op jit(solution)/shard_map/all_to_all | solution.py:194
  186.0 19.6 %collective-permute-start.6 = (f32[4,128,896]{2,1,0:T(8,128)S(1)}, f32[4,128,896]{2,1,0:T(8,128)}, u32[]{:S(2)}, u32[]{:S(2)}) collective-permute-start(f32[4,128,896]{2,1,0:T(8,128)S(1)} %all_to_all.38.own_ref), channel_id=1, source_target_pairs={{0,8},{8,0},{1,9},{9,1},{2,10},{10,2},{3,11},{11,3},{4,12},{12,4},... | collective-permute-start | bytes 5505032 | tf_op jit(solution)/shard_map/ppermute | solution.py:237
  189.6 3.4 %collective-permute-start.5 = (f32[2,128]{1,0:T(2,128)S(1)}, f32[2,128]{1,0:T(2,128)S(1)}, u32[]{:S(2)}, u32[]{:S(2)}) collective-permute-start(f32[2,128]{1,0:T(2,128)S(1)} %slice_reduce_fusion), channel_id=1, source_target_pairs={{0,8},{8,0},{1,9},{9,1},{2,10},{10,2},{3,11},{11,3},{4,12},{12,4},... | collective-permute-start | bytes 3080 | tf_op jit(solution)/shard_map/ppermute | solution.py:234
  193.9 11.6 %all-to-all-start.6 = ((f32[16,8,128]{2,1,0:T(8,128)}), f32[16,8,128]{2,1,0:T(8,128)S(1)}, u32[]{:S(2)}, u32[]{:S(2)}) async-start(f32[16,8,128]{2,1,0:T(8,128)} %broadcast_in_dim_broadcast_in_dim_broadcast_in_dim.3), calls=%async_computation.6 | async-start | bytes 131072 | tf_op jit(solution)/shard_map/all_to_all | solution.py:194
  205.5 1.1 copy-start.2
  206.7 1.0 copy-start.4
  207.7 4.5 %copy-start.5 = (f32[32,16,256]{2,1,0:T(8,128)S(1)}, f32[32,16,256]{2,1,0:T(8,128)}, u32[]{:S(2)}) copy-start(f32[32,16,256]{2,1,0:T(8,128)} %copy-done.3) | copy-start | bytes 1572868

commit v3 on v2

v3 whole, which is shorter than its diff:
```python
import functools
import math

import jax
import jax.numpy as jnp
from jax import lax
from jax.experimental import pallas as pl
from jax.experimental.pallas import tpu as pltpu
from jax.sharding import Mesh, PartitionSpec as P

ROWS = 7168
COLS = 28672
RANK = 256

NY, NX, NC, NZ = 8, 4, 2, 8

norm_eps = 1e-06
carry_keep = 0.9
SWAP = [(0, 1), (1, 0)]
PARAMS = pltpu.CompilerParams(vmem_limit_bytes=10 * 1024 * 1024)
VMEM = pl.BlockSpec(memory_space=pltpu.VMEM)
ANY = pl.BlockSpec(memory_space=pl.ANY)


def split(value):
    high = value.astype(jnp.bfloat16)
    return high, (value - high.astype(jnp.float32)).astype(jnp.bfloat16)


def dot3(a, b, dims):
    dot = functools.partial(
        lax.dot_general, dimension_numbers=(dims, ((), ())), preferred_element_type=jnp.float32
    )
    return dot(a[1], b[0]) + dot(a[0], b[1]) + dot(a[0], b[0])


def cost(flops, nbytes):
    return pl.CostEstimate(flops=flops, bytes_accessed=nbytes, transcendentals=0)


def deal_kernel(m_ref, g_ref, basis_ref, *refs):
    blocks, pieces_ref = refs[:NX], refs[NX]
    part = blocks[0].shape[1]
    for j, ref in enumerate(blocks):
        at = lax.rem(lax.axis_index("x") + j, NX)
        columns = pl.ds(pl.multiple_of(at * part, 128), part)
        ref[...] = m_ref[:, columns] + g_ref[:, columns].astype(jnp.float32)
    for to in range(NX):
        piece = basis_ref[:, to * part : (to + 1) * part]
        for y in range(NY):
            pieces_ref[y * NX + to] = piece


def deal(momentum, gradient, basis):
    rows, cols = momentum.shape
    ranks, part = basis.shape[0], cols // NX
    shapes = [(rows, part)] * NX + [(NY * NX, ranks, part)]
    return pl.pallas_call(
        deal_kernel,
        in_specs=[VMEM] * 3,
        out_specs=[VMEM] * (NX + 1),
        out_shape=[jax.ShapeDtypeStruct(shape, jnp.float32) for shape in shapes],
        compiler_params=PARAMS,
        cost_estimate=cost(rows * cols, 10 * rows * cols),
    )(momentum, gradient, basis)


def tall_kernel(*refs):
    blocks, (high_ref, low_ref) = refs[:NX], refs[NX:]
    rows = blocks[0].shape[0]
    for j, ref in enumerate(blocks):
        at = slice(j * rows, (j + 1) * rows)
        high_ref[at], low_ref[at] = split(ref[...])


def tall_parts(blocks):
    rows, part = blocks[0].shape
    shape = jax.ShapeDtypeStruct((NX * rows, part), jnp.bfloat16)
    return pl.pallas_call(
        tall_kernel,
        in_specs=[VMEM] * NX,
        out_specs=[VMEM] * 2,
        out_shape=[shape] * 2,
        compiler_params=PARAMS,
        cost_estimate=cost(4 * NX * rows * part, 8 * NX * rows * part),
    )(*blocks)


def panel_kernel(high_ref, low_ref, own_ref, oth_ref, out_ref):
    rows = high_ref.shape[0] // NX
    basis = split(jnp.concatenate([own_ref[...], oth_ref[...]], axis=0))
    panel = dot3((high_ref[...], low_ref[...]), basis, ((1,), (1,)))
    for j in range(NX):
        at = lax.rem(lax.axis_index("x") + (NX - j), NX)
        out_ref[at, :rows] = panel[j * rows : (j + 1) * rows]
        if out_ref.shape[1] > rows:
            spare = (out_ref.shape[1] - rows, out_ref.shape[2])
            out_ref[at, rows:] = jnp.zeros(spare, jnp.float32)


def panel_part(tall, own, oth, padded):
    rows, part = tall[0].shape
    half = own.shape[0]
    return pl.pallas_call(
        panel_kernel,
        in_specs=[VMEM] * 4,
        out_specs=VMEM,
        out_shape=jax.ShapeDtypeStruct((NX, padded, 2 * half), jnp.float32),
        compiler_params=PARAMS,
        cost_estimate=cost(12 * rows * part * half, 4 * (rows + 2 * half) * part),
    )(*tall, own, oth)


def right_kernel(side, high_ref, low_ref, panel_ref, out_ref, mine_ref=None):
    rows, half = high_ref.shape[0] // NX, panel_ref.shape[2] // 2
    tall = (high_ref[...], low_ref[...])
    panel = [panel_ref[lax.rem(lax.axis_index("x") + (NX - j), NX), :rows] for j in range(NX)]
    if side == 0:
        mine_ref[...] = panel[0]
    panel = jnp.concatenate(panel, axis=0)
    out_ref[half:] = jnp.zeros((8, out_ref.shape[1]), jnp.float32)
    squares = jnp.sum(panel * panel, axis=0, keepdims=True)
    out_ref[half : half + 1, :half] = squares[:, side * half : (side + 1) * half]
    out_ref[half : half + 1, half : 2 * half] = squares[:, (1 - side) * half : (2 - side) * half]
    panel = panel[:, side * half : (side + 1) * half]
    out_ref[:half] = dot3(split(panel), tall, ((0,), (0,)))


def right_part(side, tall, panel):
    rows, part = tall[0].shape
    half = panel.shape[2] // 2
    shapes = [(half + 8, part), (rows // NX, 2 * half)][: 2 - side]
    return pl.pallas_call(
        functools.partial(right_kernel, side),
        in_specs=[VMEM] * 3,
        out_specs=[VMEM] * len(shapes),
        out_shape=[jax.ShapeDtypeStruct(shape, jnp.float32) for shape in shapes],
        compiler_params=PARAMS,
        cost_estimate=cost(6 * rows * part * half, 4 * rows * part),
    )(*tall, panel)


def first_kernel(mine_ref, square_ref, m_ref, g_ref, own_ref, out_ref):
    half = own_ref.shape[1]
    left = mine_ref[:, :half] * ((1.0 - carry_keep) / square_ref[:1])
    feedback = dot3(split(left), split(own_ref[0]), ((1,), (0,)))
    out_ref[...] = m_ref[...] + g_ref[...].astype(jnp.float32) - feedback


def first_out(mine, square, momentum, gradient, own):
    rows, cols = momentum.shape
    half, part = own.shape[1:]
    block = pl.BlockSpec((rows, part), lambda j: (0, j))
    return pl.pallas_call(
        first_kernel,
        grid=(NX,),
        in_specs=[
            pl.BlockSpec(mine.shape, lambda j: (0, 0)),
            pl.BlockSpec(square.shape, lambda j: (0, 0)),
            block,
            block,
            pl.BlockSpec((1, half, part), lambda j: (j, 0, 0)),
        ],
        out_specs=block,
        out_shape=jax.ShapeDtypeStruct((rows, cols), jnp.float32),
        compiler_params=PARAMS,
        cost_estimate=cost(6 * rows * cols * half, 4 * (3 * rows + half) * cols),
    )(mine, square, momentum, gradient, own)


def stack(*arrays):
    return jnp.concatenate(arrays, axis=0)


def last_kernel(
    mine_ref, square_ref, sums_ref, own_ref, oth_ref, first_ref,
    m_out, u_out, b_out, m_buf, u_buf, b_buf, sems,
):
    rows, (ranks, _) = mine_ref.shape[0], b_buf.shape
    half, part = own_ref.shape[1:]
    loads = []
    for j in range(NX):
        at = (slice(None), pl.ds(j * part, part))
        loads.append(pltpu.make_async_copy(first_ref.at[at], m_buf.at[at], sems.at[j, 2]))
        loads[-1].start()
    square = square_ref[...]
    right_scale = jnp.sqrt(sums_ref[...] / square + norm_eps)
    for_update = math.sqrt(ROWS * COLS / RANK) / (square * right_scale)
    m_oth = split(mine_ref[:, half:] * ((1.0 - carry_keep) / square[1:2]))
    u_oth = split(mine_ref[:, half:] * for_update[1:2])
    u_own = split(mine_ref[:, :half] * for_update[:1])
    first = (lax.axis_index("y") * NX + lax.axis_index("x")) * ranks
    group = pl.multiple_of(first // 8 * 8, 8)
    lane = lax.broadcasted_iota(jnp.int32, (8, half), 1)
    row = lax.broadcasted_iota(jnp.int32, (8, half), 0)
    scale = 1.0 / (jnp.sqrt(square[:1]) * right_scale[:1])
    scale = jnp.sum(jnp.where(lane == row + group, scale, 0.0), axis=1, keepdims=True)

    dot = functools.partial(jnp.dot, preferred_element_type=jnp.float32)
    copies = []
    for j in range(NX):
        columns = pl.ds(j * part, part)
        high, low = split(oth_ref[j])
        sums = dot(stack(*m_oth, *u_oth), high)
        rest = dot(stack(m_oth[0], u_oth[0]), low)
        feedback = sums[:rows] + sums[rows : 2 * rows] + rest[:rows]
        update = sums[2 * rows : 3 * rows] + sums[3 * rows :] + rest[rows:]
        high, low = split(own_ref[j])
        sums = dot(stack(*u_own), high)
        update += sums[:rows] + sums[rows:] + dot(u_own[0], low)
        loads[j].wait()
        m_buf[:, columns] -= feedback
        u_buf[:, columns] = update.astype(jnp.bfloat16)
        eight = own_ref[j, pl.ds(group, 8), :] * scale
        b_buf[:, columns] = jnp.where(first > group, eight[8 - ranks :], eight[:ranks])
        for i, (buf, out) in enumerate(((m_buf, m_out), (u_buf, u_out))):
            at = (slice(None), columns)
            copies.append(pltpu.make_async_copy(buf.at[at], out.at[at], sems.at[j, i]))
            copies[-1].start()
    copies.append(pltpu.make_async_copy(b_buf, b_out, sems.at[NX, 0]))
    copies[-1].start()
    for copy in copies:
        copy.wait()


def last_out(mine, square, sums, own, oth, first, ranks):
    rows, cols = first.shape
    half = own.shape[1]
    shapes = [
        ((rows, cols), jnp.float32),
        ((rows, cols), jnp.bfloat16),
        ((ranks, cols), jnp.float32),
    ]
    return pl.pallas_call(
        last_kernel,
        in_specs=[VMEM] * 5 + [ANY],
        out_specs=[ANY] * 3,
        out_shape=[jax.ShapeDtypeStruct(*shape) for shape in shapes],
        scratch_shapes=[pltpu.VMEM(*shape) for shape in shapes]
        + [pltpu.SemaphoreType.DMA((NX + 1, 3))],
        compiler_params=PARAMS,
        cost_estimate=cost(18 * rows * cols * half, 4 * (4 * rows + 2 * half) * cols),
    )(mine, square, sums, own, oth, first)


def exchange(blocks, axes):
    return lax.all_to_all(blocks, axes, 0, 0, tiled=True)


def spread(block, axes, n):
    return exchange(jnp.broadcast_to(block[None], (n, *block.shape)), axes)


def shards(momentum, gradient, basis_panel):
    rows, cols = momentum.shape
    rank_rows = basis_panel.shape[0]
    part = cols // NX
    half = NY * NX * rank_rows
    own_ranks = NX * rank_rows
    padded = -(-rows // (8 * NZ)) * 8 * NZ
    core = lax.axis_index("core")

    *blocks, pieces = deal(momentum, gradient, basis_panel)
    blocks = [blocks[0]] + [
        lax.ppermute(blocks[j], "x", [(i, (i + j) % NX) for i in range(NX)]) for j in range(1, NX)
    ]
    basis_own = exchange(pieces, ("y", "x"))
    basis_own, *blocks = lax.optimization_barrier((basis_own, *blocks))
    basis_own = basis_own.reshape(half, part)
    basis_oth = lax.ppermute(basis_own, "core", SWAP)

    tall = tall_parts(blocks)
    panel = panel_part(tall, basis_own, basis_oth, padded)
    panel = exchange(panel.reshape(NX * NZ, padded // NZ, 2 * half), ("x", "z"))
    panel = spread(jnp.sum(panel, axis=0), ("x", "z"), NX * NZ)
    panel = panel.reshape(NX, padded, 2 * half)

    right_oth = lax.ppermute(right_part(1, tall, panel)[0], "core", SWAP)
    right_sum, mine = right_part(0, tall, panel)
    right_sum = right_sum + right_oth
    square = right_sum[half, : 2 * half].reshape(2, half)
    right_sum = exchange(right_sum[:half].reshape(NY, own_ranks, part), "y")
    right_sum = jnp.sum(right_sum, axis=0)
    beside = jnp.zeros((own_ranks, 128), jnp.float32).at[:2, :half].set(square)
    got = spread(jnp.concatenate([right_sum, beside], axis=1), "y", NY)
    square = jnp.sum(got[:, :2, part : part + half], axis=0) + norm_eps

    own = spread(got[:, :, :part].reshape(half, part), "x", NX)
    oth = lax.ppermute(own, "core", SWAP)
    sums = jnp.broadcast_to(jnp.sum(own * own, axis=(0, 2)), (8, half))
    sums = jnp.sum(spread(sums, ("core", "z"), NC * NZ).reshape(NC, NZ, 8, half), axis=1)[:, 0]
    sums = jnp.where(core == 0, sums, sums[::-1])

    first = first_out(mine, square, momentum, gradient, own)
    momentum_new, update, basis_new = last_out(mine, square, sums, own, oth, first, rank_rows)
    return momentum_new, basis_new, update


def solution(mesh):
    fine = Mesh(mesh.devices.reshape(NY, NX, NC, NZ), ("y", "x", "core", "z"))
    spec = P(("y", "x", "core"), "z")
    return jax.shard_map(
        shards,
        mesh=fine,
        in_specs=(spec, spec, spec),
        out_specs=(spec, spec, spec),
        check_vma=False,
    )
```

time: 217 us -> 204 us (0.940)
  waiting for transfers between devices: 54.8 us -> 35.9 us
  local copies, waits for them, and re-layouts: 6.67 us -> 14.5 us
  Pallas kernels: 14.1 us -> 10.7 us
    all_to_all x3, waiting for transfers between devices: 38 us -> 18.6 us  [exchange(): return lax.all_to_all(blocks, axes, 0, 0, tiled=True)]
    unnamed x20 -> x26, local copies, waits for them, and re-layouts: 2.95 us -> 11.6 us
    pallas_call x6 -> x7, Pallas kernels: 14.1 us -> 10.7 us  [the longest x1 5.57 us: last_out(): pl.pallas_call(last_kernel, in_specs=[VMEM] * 5 + [ANY], out_specs=[ANY]...]
    ppermute x2 -> x1, starting transfers between devices: 8.38 us -> 5.94 us  [shards(): right_oth = lax.ppermute(right_part(1, tall, panel)[0], 'core', SWAP)]
    all_to_all x3, starting transfers between devices: 18.4 us -> 20.7 us  [exchange(): return lax.all_to_all(blocks, axes, 0, 0, tiled=True)]
  transfers between devices with their start and end apart: 10 -> 9, of which waited for: 8 -> 7; matrix products, arithmetic and copies ran while one was open for 1% -> 2% of each run, Pallas kernels for 1% -> 1%
where the time goes in v3:
time: 204 us; the launch traced here: 203 us
  blocking collectives  93.7 us (46%)
  starting transfers between devices  44.4 us (22%)
  waiting for transfers between devices  35.9 us (18%)
  local copies, waits for them, and re-layouts  14.5 us (7%)
  Pallas kernels  10.7 us (5%)
  other arithmetic  3.24 us (2%)
    all_to_all x4, blocking collectives, exchange(): return lax.all_to_all(blocks, axes, 0, 0, tiled=True)  93.7 us
    all_to_all x3, starting transfers between devices, exchange(): return lax.all_to_all(blocks, axes, 0, 0, tiled=True)  20.7 us
    all_to_all x3, waiting for transfers between devices, exchange(): return lax.all_to_all(blocks, axes, 0, 0, tiled=True)  18.6 us
    ppermute x3, waiting for transfers between devices, shards(): lax.ppermute(blocks[j], 'x', [(i, (i + j) % NX) for i in range(NX)])  16.4 us
    unnamed x26, local copies, waits for them, and re-layouts  11.6 us
    ppermute x3, starting transfers between devices, shards(): lax.ppermute(blocks[j], 'x', [(i, (i + j) % NX) for i in range(NX)])  10.5 us
    ppermute x1, starting transfers between devices, shards(): right_oth = lax.ppermute(right_part(1, tall, panel)[0], 'core', SWAP)  5.94 us
    pallas_call x1, Pallas kernels, last_out(): pl.pallas_call(last_kernel, in_specs=[VMEM] * 5 + [ANY], out_specs=[ANY]...  5.57 us
  transfers between devices with their start and end apart: 9, of which 7 were waited for; matrix products, arithmetic and copies ran while one was open for 2% of the time, Pallas kernels for 1%

profile of v3, /device:TPU:1, one launch (start us, length us, event | category | flops | bytes accessed | tf_op | source)
XLA Modules:
  0.0 203.3 jit_solution(16892391886731112689)
XLA Ops:
  0.6 1.4 copy-done
  2.1 1.1 copy-done.4
  3.2 0.8 copy-done.8
  4.0 1.0 shard_map.58
  5.0 10.5 %all-to-all-start = ((f32[32,4,896]{2,1,0:T(4,128)}), f32[32,4,896]{2,1,0:T(4,128)S(1)}, u32[]{:S(2)}, u32[]{:S(2)}) async-start(f32[32,4,896]{2,1,0:T(4,128)} %get-tuple-element.32), calls=%async_computation | async-start | bytes 917504 | tf_op jit(solution)/shard_map/all_to_all | solution.py:247
  15.5 3.1 %collective-permute-start = (f32[112,896]{1,0:T(8,128)S(1)}, f32[112,896]{1,0:T(8,128)S(1)}, u32[]{:S(2)}, u32[]{:S(2)}) collective-permute-start(f32[112,896]{1,0:T(8,128)S(1)} %get-tuple-element.34), channel_id=1, source_target_pairs={{0,16},{16,32},{32,48},{48,0},{1,17},{17,33},{33,49},{49,1},{2,18}... | collective-permute-start | bytes 1204232 | tf_op jit(solution)/shard_map/ppermute | solution.py:265
  18.6 4.3 %collective-permute-start.1 = (f32[112,896]{1,0:T(8,128)S(1)}, f32[112,896]{1,0:T(8,128)S(1)}, u32[]{:S(2)}, u32[]{:S(2)}) collective-permute-start(f32[112,896]{1,0:T(8,128)S(1)} %get-tuple-element.35), channel_id=1, source_target_pairs={{0,32},{16,48},{32,0},{48,16},{1,33},{17,49},{33,1},{49,17},{2,34}... | collective-permute-start | bytes 1204232 | tf_op jit(solution)/shard_map/ppermute | solution.py:265
  23.0 3.1 %collective-permute-start.2 = (f32[112,896]{1,0:T(8,128)S(1)}, f32[112,896]{1,0:T(8,128)S(1)}, u32[]{:S(2)}, u32[]{:S(2)}) collective-permute-start(f32[112,896]{1,0:T(8,128)S(1)} %get-tuple-element.36), channel_id=1, source_target_pairs={{0,48},{16,0},{32,16},{48,32},{1,49},{17,1},{33,17},{49,33},{2,50}... | collective-permute-start | bytes 1204232 | tf_op jit(solution)/shard_map/ppermute | solution.py:265
  26.1 7.1 %collective-permute-done.refs_1_ = f32[112,896]{1,0:T(8,128)S(1)} collective-permute-done((f32[112,896]{1,0:T(8,128)S(1)}, f32[112,896]{1,0:T(8,128)S(1)}, u32[]{:S(2)}, u32[]{:S(2)}) %collective-permute-start) | collective-permute-done | bytes 401440 | tf_op jit(solution)/shard_map/ppermute | solution.py:265
  33.1 9.1 %collective-permute-done.1.refs_2_ = f32[112,896]{1,0:T(8,128)S(1)} collective-permute-done((f32[112,896]{1,0:T(8,128)S(1)}, f32[112,896]{1,0:T(8,128)S(1)}, u32[]{:S(2)}, u32[]{:S(2)}) %collective-permute-start.1) | collective-permute-done | bytes 401440 | tf_op jit(solution)/shard_map/ppermute | solution.py:265
  42.2 0.2 collective-permute-done.2.refs_3_
  42.5 0.7 copy-done.6
  43.2 0.8 copy-done.12
  44.0 1.2 reshape.52.own_ref
  45.2 3.3 %collective-permute-start.3 = (f32[128,896]{1,0:T(8,128)S(1)}, f32[128,896]{1,0:T(8,128)S(1)}, u32[]{:S(2)}, u32[]{:S(2)}) collective-permute-start(f32[128,896]{1,0:T(8,128)S(1)} %reshape.52.own_ref), channel_id=1, source_target_pairs={{0,8},{8,0},{1,9},{9,1},{2,10},{10,2},{3,11},{11,3},{4,12},{12,4},... | collective-permute-start | bytes 1376264 | tf_op jit(solution)/shard_map/ppermute | solution.py:270
  48.5 1.0 copy-done.7
  49.5 0.3 shard_map.59
  49.7 0.1 collective-permute-done.3.oth_ref
  49.9 0.9 shard_map.60
  50.8 26.6 %all_to_all.35 = f32[32,16,256]{2,1,0:T(8,128)S(1)} all-to-all(f32[32,16,256]{2,1,0:T(8,128)S(1)} %bitcast.12), channel_id=1, replica_groups=mesh['y'=8,'x'=4,'core'=2,'z'=8] {'x','z'}, dimensions={0} | all-to-all | bytes 1048576 | tf_op jit(solution)/shard_map/all_to_all | solution.py:247
  77.5 22.0 %all_to_all.36 = f32[32,16,256]{2,1,0:T(8,128)S(1)} all-to-all(f32[32,16,256]{2,1,0:T(8,128)S(1)} %broadcast_in_dim.8), channel_id=1, replica_groups=mesh['y'=8,'x'=4,'core'=2,'z'=8] {'x','z'}, dimensions={0} | all-to-all | bytes 1048576 | tf_op jit(solution)/shard_map/all_to_all | solution.py:247
  99.5 0.6 shard_map.62
  100.1 5.9 %collective-permute-start.4 = (f32[136,896]{1,0:T(8,128)S(1)}, f32[136,896]{1,0:T(8,128)S(1)}, u32[]{:S(2)}, u32[]{:S(2)}) collective-permute-start(f32[136,896]{1,0:T(8,128)S(1)} %shard_map.62), channel_id=1, source_target_pairs={{0,8},{8,0},{1,9},{9,1},{2,10},{10,2},{3,11},{11,3},{4,12},{12,4},... | collective-permute-start | bytes 1462280 | tf_op jit(solution)/shard_map/ppermute | solution.py:278
  106.1 0.6 shard_map.61
  106.7 0.8 collective-permute-done.4
  107.6 0.1 add.13
  107.6 0.8 slice.36
  108.4 5.9 %all-to-all-start.3 = ((f32[8,16,896]{2,1,0:T(8,128)}), f32[8,16,896]{2,1,0:T(8,128)S(1)}, u32[]{:S(2)}, u32[]{:S(2)}) async-start(f32[8,16,896]{2,1,0:T(8,128)} %bitcast.2), calls=%async_computation.3 | async-start | bytes 917504 | tf_op jit(solution)/shard_map/all_to_all | solution.py:247
  114.3 16.5 %all-to-all-done.3 = f32[8,16,896]{2,1,0:T(8,128)S(1)} async-done(((f32[8,16,896]{2,1,0:T(8,128)}), f32[8,16,896]{2,1,0:T(8,128)S(1)}, u32[]{:S(2)}, u32[]{:S(2)}) %all-to-all-start.3) | async-done | bytes 458784 | tf_op jit(solution)/shard_map/all_to_all | solution.py:247
  131.0 20.1 %all_to_all.37 = f32[8,16,1024]{2,1,0:T(8,128)S(1)} all-to-all(f32[8,16,1024]{2,1,0:T(8,128)S(1)} %broadcast_in_dim.9), channel_id=1, replica_groups=mesh['y'=8,'x'=4,'core'=2,'z'=8] {'y'}, dimensions={0} | all-to-all | bytes 1048576 | tf_op jit(solution)/shard_map/all_to_all | solution.py:247
  151.1 0.8 copy-done.11
  151.9 0.1 broadcast_in_dim.11
  152.0 25.0 %all_to_all.38.own_ref = f32[4,128,896]{2,1,0:T(8,128)S(1)} all-to-all(f32[4,128,896]{2,1,0:T(8,128)S(1)} %broadcast_in_dim.11), channel_id=1, replica_groups=mesh['y'=8,'x'=4,'core'=2,'z'=8] {'x'}, dimensions={0} | all-to-all | bytes 3670016 | tf_op jit(solution)/shard_map/all_to_all | solution.py:247
  177.0 4.0 %collective-permute-start.5 = (f32[4,128,896]{2,1,0:T(8,128)S(1)}, f32[4,128,896]{2,1,0:T(8,128)}, u32[]{:S(2)}, u32[]{:S(2)}) collective-permute-start(f32[4,128,896]{2,1,0:T(8,128)S(1)} %all_to_all.38.own_ref), channel_id=1, source_target_pairs={{0,8},{8,0},{1,9},{9,1},{2,10},{10,2},{3,11},{11,3},{4,12},{12,4},... | collective-permute-start | bytes 5505032 | tf_op jit(solution)/shard_map/ppermute | solution.py:289
  181.0 1.3 slice_reduce_fusion
  182.3 0.2 multiply_reduce_fusion
  182.6 0.6 broadcast_in_dim_broadcast_in_dim_broadcast_in_dim.3
  183.2 4.3 %all-to-all-start.6 = ((f32[16,8,128]{2,1,0:T(8,128)}), f32[16,8,128]{2,1,0:T(8,128)}, u32[]{:S(2)}, u32[]{:S(2)}) async-start(f32[16,8,128]{2,1,0:T(8,128)} %broadcast_in_dim_broadcast_in_dim_broadcast_in_dim.3), calls=%async_computation.6 | async-start | bytes 131072 | tf_op jit(solution)/shard_map/all_to_all | solution.py:247
  187.5 0.7 broadcast_add_fusion.square_ref
  188.1 0.6 copy-done.9
  188.7 1.1 copy-done.5
  189.8 1.7 shard_map.63.first_ref
  191.6 1.1 copy-done.2
  192.7 2.0 %all-to-all-done.6 = f32[16,8,128]{2,1,0:T(8,128)} async-done(((f32[16,8,128]{2,1,0:T(8,128)}), f32[16,8,128]{2,1,0:T(8,128)}, u32[]{:S(2)}, u32[]{:S(2)}) %all-to-all-start.6) | async-done | bytes 65568 | tf_op jit(solution)/shard_map/all_to_all | solution.py:247
  194.8 0.9 bitcast_reduce_fusion
  195.7 1.4 copy-done.3
  197.1 0.7 copy-done.10
  197.8 5.6 %shard_map.64 = (f32[112,3584]{1,0:T(8,128)}, bf16[112,3584]{1,0:T(8,128)(2,1)}, f32[4,3584]{1,0:T(4,128)}) custom-call(f32[112,256]{1,0:T(8,128)S(1)} %get-tuple-element.44.mine_ref, f32[2,128]{1,0:T(2,128)S(1)} %copy-done.10, f32[2,128]{1,0:T(2,128)S(1)} %broadcast_select_fusion.sums_ref, f32[4,128,896]{2,1,0:T(8,128)S(1)} %all_to_all.38.own_ref, ...), custom_call_target="tpu_custom_call" | custom-call | flops 924844032 | bytes 10092544 | tf_op jit(solution)/shard_map/pallas_call | solution.py:234
  (26 shorter events, 0.3 us)
Async XLA Ops:
  0.6 1.4 copy-start
  2.1 1.1 copy-start.4
  3.2 0.8 copy-start.8
  5.0 38.2 %all-to-all-start = ((f32[32,4,896]{2,1,0:T(4,128)}), f32[32,4,896]{2,1,0:T(4,128)S(1)}, u32[]{:S(2)}, u32[]{:S(2)}) async-start(f32[32,4,896]{2,1,0:T(4,128)} %get-tuple-element.32), calls=%async_computation | async-start | bytes 917504 | tf_op jit(solution)/shard_map/all_to_all | solution.py:247
  15.5 17.6 %collective-permute-start = (f32[112,896]{1,0:T(8,128)S(1)}, f32[112,896]{1,0:T(8,128)S(1)}, u32[]{:S(2)}, u32[]{:S(2)}) collective-permute-start(f32[112,896]{1,0:T(8,128)S(1)} %get-tuple-element.34), channel_id=1, source_target_pairs={{0,16},{16,32},{32,48},{48,0},{1,17},{17,33},{33,49},{49,1},{2,18}... | collective-permute-start | bytes 1204232 | tf_op jit(solution)/shard_map/ppermute | solution.py:265
  18.6 23.6 %collective-permute-start.1 = (f32[112,896]{1,0:T(8,128)S(1)}, f32[112,896]{1,0:T(8,128)S(1)}, u32[]{:S(2)}, u32[]{:S(2)}) collective-permute-start(f32[112,896]{1,0:T(8,128)S(1)} %get-tuple-element.35), channel_id=1, source_target_pairs={{0,32},{16,48},{32,0},{48,16},{1,33},{17,49},{33,1},{49,17},{2,34}... | collective-permute-start | bytes 1204232 | tf_op jit(solution)/shard_map/ppermute | solution.py:265
  23.0 19.5 %collective-permute-start.2 = (f32[112,896]{1,0:T(8,128)S(1)}, f32[112,896]{1,0:T(8,128)S(1)}, u32[]{:S(2)}, u32[]{:S(2)}) collective-permute-start(f32[112,896]{1,0:T(8,128)S(1)} %get-tuple-element.36), channel_id=1, source_target_pairs={{0,48},{16,0},{32,16},{48,32},{1,49},{17,1},{33,17},{49,33},{2,50}... | collective-permute-start | bytes 1204232 | tf_op jit(solution)/shard_map/ppermute | solution.py:265
  42.5 0.7 copy-start.6
  43.2 0.8 copy-start.12
  45.2 4.7 %collective-permute-start.3 = (f32[128,896]{1,0:T(8,128)S(1)}, f32[128,896]{1,0:T(8,128)S(1)}, u32[]{:S(2)}, u32[]{:S(2)}) collective-permute-start(f32[128,896]{1,0:T(8,128)S(1)} %reshape.52.own_ref), channel_id=1, source_target_pairs={{0,8},{8,0},{1,9},{9,1},{2,10},{10,2},{3,11},{11,3},{4,12},{12,4},... | collective-permute-start | bytes 1376264 | tf_op jit(solution)/shard_map/ppermute | solution.py:270
  48.5 1.0 copy-start.7
  100.1 7.4 %collective-permute-start.4 = (f32[136,896]{1,0:T(8,128)S(1)}, f32[136,896]{1,0:T(8,128)S(1)}, u32[]{:S(2)}, u32[]{:S(2)}) collective-permute-start(f32[136,896]{1,0:T(8,128)S(1)} %shard_map.62), channel_id=1, source_target_pairs={{0,8},{8,0},{1,9},{9,1},{2,10},{10,2},{3,11},{11,3},{4,12},{12,4},... | collective-permute-start | bytes 1462280 | tf_op jit(solution)/shard_map/ppermute | solution.py:278
  108.4 22.5 %all-to-all-start.3 = ((f32[8,16,896]{2,1,0:T(8,128)}), f32[8,16,896]{2,1,0:T(8,128)S(1)}, u32[]{:S(2)}, u32[]{:S(2)}) async-start(f32[8,16,896]{2,1,0:T(8,128)} %bitcast.2), calls=%async_computation.3 | async-start | bytes 917504 | tf_op jit(solution)/shard_map/all_to_all | solution.py:247
  151.1 0.8 copy-start.11
  177.0 11.7 %copy-start.1 = (f32[112,3584]{1,0:T(8,128)S(1)}, f32[112,3584]{1,0:T(8,128)}, u32[]{:S(2)}) copy-start(f32[112,3584]{1,0:T(8,128)} %m_ref.3) | copy-start | bytes 4816900
  177.0 18.6 %collective-permute-start.5 = (f32[4,128,896]{2,1,0:T(8,128)S(1)}, f32[4,128,896]{2,1,0:T(8,128)}, u32[]{:S(2)}, u32[]{:S(2)}) collective-permute-start(f32[4,128,896]{2,1,0:T(8,128)S(1)} %all_to_all.38.own_ref), channel_id=1, source_target_pairs={{0,8},{8,0},{1,9},{9,1},{2,10},{10,2},{3,11},{11,3},{4,12},{12,4},... | collective-permute-start | bytes 5505032 | tf_op jit(solution)/shard_map/ppermute | solution.py:289
  183.2 11.6 %all-to-all-start.6 = ((f32[16,8,128]{2,1,0:T(8,128)}), f32[16,8,128]{2,1,0:T(8,128)}, u32[]{:S(2)}, u32[]{:S(2)}) async-start(f32[16,8,128]{2,1,0:T(8,128)} %broadcast_in_dim_broadcast_in_dim_broadcast_in_dim.3), calls=%async_computation.6 | async-start | bytes 131072 | tf_op jit(solution)/shard_map/all_to_all | solution.py:247
  188.1 0.6 copy-start.9
  188.7 1.1 copy-start.5
  191.6 1.2 copy-start.2
  195.7 1.4 copy-start.3
  197.1 0.7 copy-start.10

commit v4 on v3

v4 whole, which is shorter than its diff:
```python
import functools
import math

import jax
import jax.numpy as jnp
from jax import lax
from jax.experimental import pallas as pl
from jax.experimental.pallas import tpu as pltpu
from jax.sharding import Mesh, PartitionSpec as P

ROWS = 7168
COLS = 28672
RANK = 256

NY, NX, NC, NZ = 8, 4, 2, 8

norm_eps = 1e-06
carry_keep = 0.9
SWAP = [(0, 1), (1, 0)]
PARAMS = pltpu.CompilerParams(vmem_limit_bytes=10 * 1024 * 1024)
VMEM = pl.BlockSpec(memory_space=pltpu.VMEM)
ANY = pl.BlockSpec(memory_space=pl.ANY)
HBM = pl.BlockSpec(memory_space=pltpu.HBM)


def split(value):
    high = value.astype(jnp.bfloat16)
    return high, (value - high.astype(jnp.float32)).astype(jnp.bfloat16)


def dot3(a, b, dims):
    dot = functools.partial(
        lax.dot_general, dimension_numbers=(dims, ((), ())), preferred_element_type=jnp.float32
    )
    return dot(a[1], b[0]) + dot(a[0], b[1]) + dot(a[0], b[0])


def cost(flops, nbytes):
    return pl.CostEstimate(flops=flops, bytes_accessed=nbytes, transcendentals=0)


def deal_kernel(m_ref, g_ref, *refs):
    blocks, (m_buf, g_buf, sems) = refs[:NX], refs[NX:]
    part = blocks[0].shape[1]
    loads = []
    for j in range(NX):
        at = lax.rem(lax.axis_index("x") + j, NX)
        columns = (slice(None), pl.ds(pl.multiple_of(at * part, 128), part))
        loads.append(
            (
                pltpu.make_async_copy(m_ref.at[columns], m_buf.at[j], sems.at[j, 0]),
                pltpu.make_async_copy(g_ref.at[columns], g_buf.at[j], sems.at[j, 1]),
            )
        )
    for j in (*range(1, NX), 0):
        for load in loads[j]:
            load.start()
    for j in (*range(1, NX), 0):
        for load in loads[j]:
            load.wait()
        blocks[j][...] = m_buf[j] + g_buf[j].astype(jnp.float32)


def deal(momentum, gradient):
    rows, cols = momentum.shape
    part = cols // NX
    return pl.pallas_call(
        deal_kernel,
        in_specs=[HBM] * 2,
        out_specs=[VMEM] * NX,
        out_shape=[jax.ShapeDtypeStruct((rows, part), jnp.float32)] * NX,
        scratch_shapes=[
            pltpu.VMEM((NX, rows, part), jnp.float32),
            pltpu.VMEM((NX, rows, part), jnp.bfloat16),
            pltpu.SemaphoreType.DMA((NX, 2)),
        ],
        compiler_params=PARAMS,
        cost_estimate=cost(rows * cols, 10 * rows * cols),
    )(momentum, gradient)


def pieces_kernel(basis_ref, after_ref, pieces_ref):
    part = pieces_ref.shape[2]
    for to in range(NX):
        piece = basis_ref[:, to * part : (to + 1) * part]
        for y in range(NY):
            pieces_ref[y * NX + to] = piece


def basis_pieces(basis, after):
    ranks, cols = basis.shape
    pieces = (NY * NX, ranks, cols // NX)
    return pl.pallas_call(
        pieces_kernel,
        in_specs=[VMEM, ANY],
        out_specs=VMEM,
        out_shape=jax.ShapeDtypeStruct(pieces, jnp.float32),
        compiler_params=PARAMS,
        cost_estimate=cost(10**10, 10**8),
    )(basis, after)


def tall_kernel(*refs):
    blocks, (high_ref, low_ref) = refs[:NX], refs[NX:]
    rows = blocks[0].shape[0]
    for j, ref in enumerate(blocks):
        at = slice(j * rows, (j + 1) * rows)
        high_ref[at], low_ref[at] = split(ref[...])


def tall_parts(blocks):
    rows, part = blocks[0].shape
    shape = jax.ShapeDtypeStruct((NX * rows, part), jnp.bfloat16)
    return pl.pallas_call(
        tall_kernel,
        in_specs=[VMEM] * NX,
        out_specs=[VMEM] * 2,
        out_shape=[shape] * 2,
        compiler_params=PARAMS,
        cost_estimate=cost(10**10, 2 * 10**8),
    )(*blocks)


def panel_kernel(high_ref, low_ref, basis_ref, out_ref):
    rows = high_ref.shape[0] // NX
    panel = dot3((high_ref[...], low_ref[...]), split(basis_ref[...]), ((1,), (1,)))
    for j in range(NX):
        at = lax.rem(lax.axis_index("x") + (NX - j), NX)
        out_ref[at, :rows] = panel[j * rows : (j + 1) * rows]
        if out_ref.shape[1] > rows:
            spare = (out_ref.shape[1] - rows, out_ref.shape[2])
            out_ref[at, rows:] = jnp.zeros(spare, jnp.float32)


def panel_part(tall, basis, padded):
    rows, part = tall[0].shape
    half = basis.shape[0]
    return pl.pallas_call(
        panel_kernel,
        in_specs=[VMEM] * 3,
        out_specs=VMEM,
        out_shape=jax.ShapeDtypeStruct((NX, padded, half), jnp.float32),
        compiler_params=PARAMS,
        cost_estimate=cost(6 * rows * part * half, 4 * (rows + half) * part),
    )(*tall, basis)


def right_kernel(side, high_ref, low_ref, panel_ref, out_ref, mine_ref=None):
    rows, half = high_ref.shape[0] // NX, panel_ref.shape[2] // 2
    tall = (high_ref[...], low_ref[...])
    panel = [panel_ref[lax.rem(lax.axis_index("x") + (NX - j), NX), :rows] for j in range(NX)]
    if side == 0:
        mine_ref[...] = panel[0]
    panel = jnp.concatenate(panel, axis=0)
    out_ref[half:] = jnp.zeros((8, out_ref.shape[1]), jnp.float32)
    squares = jnp.sum(panel * panel, axis=0, keepdims=True)
    out_ref[half : half + 1, :half] = squares[:, side * half : (side + 1) * half]
    out_ref[half : half + 1, half : 2 * half] = squares[:, (1 - side) * half : (2 - side) * half]
    panel = panel[:, side * half : (side + 1) * half]
    out_ref[:half] = dot3(split(panel), tall, ((0,), (0,)))


def right_part(side, tall, panel):
    rows, part = tall[0].shape
    half = panel.shape[2] // 2
    shapes = [(half + 8, part), (rows // NX, 2 * half)][: 2 - side]
    return pl.pallas_call(
        functools.partial(right_kernel, side),
        in_specs=[VMEM] * 3,
        out_specs=[VMEM] * len(shapes),
        out_shape=[jax.ShapeDtypeStruct(shape, jnp.float32) for shape in shapes],
        compiler_params=PARAMS,
        cost_estimate=cost(6 * rows * part * half, 4 * rows * part),
    )(*tall, panel)


def product(left, own_ref, oth_ref, at=0):
    rows = left.shape[0] // 2
    high, low = split(jnp.concatenate([own_ref[at], oth_ref[at]], axis=0))
    dot = functools.partial(jnp.dot, preferred_element_type=jnp.float32)
    sums = dot(left, high)
    return sums[:rows] + sums[rows:] + dot(left[:rows], low)


def scaled(mine_ref, factor):
    return jnp.concatenate(split(mine_ref[...] * factor), axis=0)


def row(pair):
    return jnp.concatenate([pair[:1], pair[1:2]], axis=1)


def squares_kernel(own_ref, oth_ref, out_ref):
    nz, lines, _ = out_ref.shape
    part = own_ref.shape[2]
    ones = jnp.ones((lines, part), jnp.bfloat16)
    total = 0.0
    for j in range(NX):
        block = jnp.concatenate([own_ref[j], oth_ref[j]], axis=0)
        for piece in split(block * block):
            dims = (((1,), (1,)), ((), ()))
            total += lax.dot_general(ones, piece, dims, preferred_element_type=jnp.float32)
    for z in range(nz):
        out_ref[z] = total


def row_squares(own, oth):
    nx, half, part = own.shape
    shape = (NZ, 8, 2 * half)
    return pl.pallas_call(
        squares_kernel,
        in_specs=[VMEM] * 2,
        out_specs=VMEM,
        out_shape=jax.ShapeDtypeStruct(shape, jnp.float32),
        compiler_params=PARAMS,
        cost_estimate=cost(4 * nx * half * part, 8 * nx * half * part),
    )(own, oth)


def momentum_kernel(mine_ref, square_ref, m_ref, g_ref, own_ref, oth_ref, out_ref):
    left = scaled(mine_ref, row((1.0 - carry_keep) / square_ref[...]))
    out_ref[...] = m_ref[...] + g_ref[...].astype(jnp.float32) - product(left, own_ref, oth_ref)


def momentum_out(mine, square, momentum, gradient, own, oth):
    rows, cols = momentum.shape
    half, part = own.shape[1:]
    block = pl.BlockSpec((rows, part), lambda j: (0, j))
    right = pl.BlockSpec((1, half, part), lambda j: (j, 0, 0))
    whole = [pl.BlockSpec(array.shape, lambda j: (0, 0)) for array in (mine, square)]
    return pl.pallas_call(
        momentum_kernel,
        grid=(NX,),
        in_specs=[*whole, block, block, right, right],
        out_specs=block,
        out_shape=jax.ShapeDtypeStruct((rows, cols), jnp.float32),
        compiler_params=PARAMS,
        cost_estimate=cost(12 * rows * cols * half, 4 * (3 * rows + 2 * half) * cols),
    )(mine, square, momentum, gradient, own, oth)


def update_kernel(
    mine_ref, square_ref, sums_ref, own_ref, oth_ref, u_out, b_out, u_buf, b_buf, sems
):
    (ranks, _), (half, part) = b_buf.shape, own_ref.shape[1:]
    square = square_ref[...]
    right_scale = jnp.sqrt(sums_ref[...] / square + norm_eps)
    left = scaled(mine_ref, row(math.sqrt(ROWS * COLS / RANK) / (square * right_scale)))
    first = (lax.axis_index("y") * NX + lax.axis_index("x")) * ranks
    group = pl.multiple_of(first // 8 * 8, 8)
    lane = lax.broadcasted_iota(jnp.int32, (8, half), 1)
    rank = lax.broadcasted_iota(jnp.int32, (8, half), 0) + group
    scale = 1.0 / (jnp.sqrt(square[:1]) * right_scale[:1])
    scale = jnp.sum(jnp.where(lane == rank, scale, 0.0), axis=1, keepdims=True)

    copies = []
    for j in range(NX):
        columns = pl.ds(j * part, part)
        eight = own_ref[j, pl.ds(group, 8), :] * scale
        b_buf[:, columns] = jnp.where(first > group, eight[8 - ranks :], eight[:ranks])
    copies.append(pltpu.make_async_copy(b_buf, b_out, sems.at[NX]))
    copies[-1].start()
    for j in range(NX):
        columns = pl.ds(j * part, part)
        u_buf[:, columns] = product(left, own_ref, oth_ref, j).astype(jnp.bfloat16)
        at = (slice(None), columns)
        copies.append(pltpu.make_async_copy(u_buf.at[at], u_out.at[at], sems.at[j]))
        copies[-1].start()
    for copy in copies:
        copy.wait()


def update_out(mine, square, sums, own, oth, ranks):
    rows, (half, part) = mine.shape[0], own.shape[1:]
    cols = NX * part
    shapes = [((rows, cols), jnp.bfloat16), ((ranks, cols), jnp.float32)]
    return pl.pallas_call(
        update_kernel,
        in_specs=[VMEM] * 5,
        out_specs=[HBM] * 2,
        out_shape=[jax.ShapeDtypeStruct(*shape) for shape in shapes],
        scratch_shapes=[pltpu.VMEM(*shape) for shape in shapes]
        + [pltpu.SemaphoreType.DMA((NX + 1,))],
        compiler_params=PARAMS,
        cost_estimate=cost(12 * rows * cols * half, 4 * (rows + 2 * half) * cols),
    )(mine, square, sums, own, oth)


def exchange(blocks, axes):
    return lax.all_to_all(blocks, axes, 0, 0, tiled=True)


def spread(block, axes, n):
    return exchange(jnp.broadcast_to(block[None], (n, *block.shape)), axes)


def shards(momentum, gradient, basis_panel):
    rows, cols = momentum.shape
    rank_rows = basis_panel.shape[0]
    part = cols // NX
    half = NY * NX * rank_rows
    own_ranks = NX * rank_rows
    padded = -(-rows // (8 * NZ)) * 8 * NZ

    blocks = deal(momentum, gradient)
    pieces = basis_pieces(basis_panel, blocks[0])
    blocks = [blocks[0]] + [
        lax.ppermute(blocks[j], "x", [(i, (i + j) % NX) for i in range(NX)]) for j in range(1, NX)
    ]
    basis_own = exchange(pieces, ("y", "x"))
    basis_own, *tall = lax.optimization_barrier((basis_own, *tall_parts(blocks)))
    basis_own = basis_own.reshape(half, part)
    basis_oth = lax.ppermute(basis_own, "core", SWAP)

    panel = [panel_part(tall, basis, padded) for basis in (basis_own, basis_oth)]
    panel = jnp.concatenate(panel, axis=2)
    panel = exchange(panel.reshape(NX * NZ, padded // NZ, 2 * half), ("x", "z"))
    panel = spread(jnp.sum(panel, axis=0), ("x", "z"), NX * NZ)
    panel = panel.reshape(NX, padded, 2 * half)

    right_oth = lax.ppermute(right_part(1, tall, panel)[0], "core", SWAP)
    right_sum, mine = right_part(0, tall, panel)
    right_sum = right_sum + right_oth
    square = right_sum[half, : 2 * half].reshape(2, half)
    right_sum = exchange(right_sum[:half].reshape(NY, own_ranks, part), "y")
    right_sum = jnp.sum(right_sum, axis=0)
    beside = jnp.zeros((own_ranks, 128), jnp.float32).at[:2, :half].set(square)
    got = spread(jnp.concatenate([right_sum, beside], axis=1), "y", NY)
    square = jnp.sum(got[:, :2, part : part + half], axis=0) + norm_eps

    own, square = lax.optimization_barrier((got[:, :, :part].reshape(half, part), square))
    own = spread(own, "x", NX)
    own, oth = lax.optimization_barrier((own, lax.ppermute(own, "core", SWAP)))
    sums = jnp.sum(exchange(row_squares(own, oth), "z"), axis=0)[0].reshape(2, half)

    momentum_new = momentum_out(mine, square, momentum, gradient, own, oth)
    update, basis_new = update_out(mine, square, sums, own, oth, rank_rows)
    return momentum_new, basis_new, update


def solution(mesh):
    fine = Mesh(mesh.devices.reshape(NY, NX, NC, NZ), ("y", "x", "core", "z"))
    spec = P(("y", "x", "core"), "z")
    return jax.shard_map(
        shards,
        mesh=fine,
        in_specs=(spec, spec, spec),
        out_specs=(spec, spec, spec),
        check_vma=False,
    )
```

time: 204 us -> 196 us (0.961)
  starting transfers between devices: 44.4 us -> 41.5 us
  local copies, waits for them, and re-layouts: 14.5 us -> 12.2 us
    ppermute x3, waiting for transfers between devices: 16.4 us -> 4.15 us  [shards(): lax.ppermute(blocks[j], 'x', [(i, (i + j) % NX) for i in range(NX)])]
    all_to_all x3, waiting for transfers between devices: 18.6 us -> 27.1 us  [exchange(): return lax.all_to_all(blocks, axes, 0, 0, tiled=True)]
    all_to_all x3, starting transfers between devices: 20.7 us -> 14.8 us  [exchange(): return lax.all_to_all(blocks, axes, 0, 0, tiled=True)]
    ppermute x1, waiting for transfers between devices: 0.01 us -> 3.39 us  [shards(): own, oth = lax.optimization_barrier((own, lax.ppermute(own, 'core', SWAP)))]
    ppermute x1, starting transfers between devices: 3.29 us -> 5.57 us  [shards(): basis_oth = lax.ppermute(basis_own, 'core', SWAP)]
    unnamed x26 -> x22, local copies, waits for them, and re-layouts: 11.6 us -> 9.96 us
    pallas_call x4 -> x7, Pallas kernels: 9.19 us -> 8.42 us  [the longest x1 2.75 us: momentum_out(): pl.pallas_call(momentum_kernel, grid=(NX,), in_specs=[*whole, block, bloc...]
  transfers between devices with their start and end apart: 9 -> 9, of which waited for: 7 -> 7; matrix products, arithmetic and copies ran while one was open for 2% -> 0% of each run, Pallas kernels for 1% -> 3%
where the time goes in v4:
time: 196 us; the launch traced here: 195 us
  blocking collectives  93.3 us (48%)
  starting transfers between devices  41.5 us (21%)
  waiting for transfers between devices  36.1 us (18%)
  local copies, waits for them, and re-layouts  12.2 us (6%)
  Pallas kernels  9.94 us (5%)
    all_to_all x4, blocking collectives, exchange(): return lax.all_to_all(blocks, axes, 0, 0, tiled=True)  93.3 us
    all_to_all x3, waiting for transfers between devices, exchange(): return lax.all_to_all(blocks, axes, 0, 0, tiled=True)  27.1 us
    all_to_all x3, starting transfers between devices, exchange(): return lax.all_to_all(blocks, axes, 0, 0, tiled=True)  14.8 us
    ppermute x3, starting transfers between devices, shards(): lax.ppermute(blocks[j], 'x', [(i, (i + j) % NX) for i in range(NX)])  11.4 us
    unnamed x22, local copies, waits for them, and re-layouts  9.96 us
    ppermute x1, starting transfers between devices, shards(): right_oth = lax.ppermute(right_part(1, tall, panel)[0], 'core', SWAP)  5.93 us
    ppermute x1, starting transfers between devices, shards(): basis_oth = lax.ppermute(basis_own, 'core', SWAP)  5.57 us
    ppermute x3, waiting for transfers between devices, shards(): lax.ppermute(blocks[j], 'x', [(i, (i + j) % NX) for i in range(NX)])  4.15 us
  transfers between devices with their start and end apart: 9, of which 7 were waited for; matrix products, arithmetic and copies ran while one was open for 0% of the time, Pallas kernels for 3%

profile of v4, /device:TPU:1, one launch (start us, length us, event | category | flops | bytes accessed | tf_op | source)
XLA Modules:
  0.0 195.5 jit_solution(15019202283029836480)
XLA Ops:
  0.6 0.0 copy-start.3
  0.6 1.4 copy-done.3
  2.1 1.1 copy-done.5
  3.2 0.5 shard_map.58
  3.7 3.9 %collective-permute-start = (f32[112,896]{1,0:T(8,128)S(1)}, f32[112,896]{1,0:T(8,128)S(1)}, u32[]{:S(2)}, u32[]{:S(2)}) collective-permute-start(f32[112,896]{1,0:T(8,128)S(1)} %get-tuple-element.33), channel_id=1, source_target_pairs={{0,16},{16,32},{32,48},{48,0},{1,17},{17,33},{33,49},{49,1},{2,18}... | collective-permute-start | bytes 1204232 | tf_op jit(solution)/shard_map/ppermute | solution.py:308
  7.7 4.4 %collective-permute-start.1 = (f32[112,896]{1,0:T(8,128)S(1)}, f32[112,896]{1,0:T(8,128)S(1)}, u32[]{:S(2)}, u32[]{:S(2)}) collective-permute-start(f32[112,896]{1,0:T(8,128)S(1)} %get-tuple-element.34), channel_id=1, source_target_pairs={{0,32},{16,48},{32,0},{48,16},{1,33},{17,49},{33,1},{49,17},{2,34}... | collective-permute-start | bytes 1204232 | tf_op jit(solution)/shard_map/ppermute | solution.py:308
  12.1 3.1 %collective-permute-start.2 = (f32[112,896]{1,0:T(8,128)S(1)}, f32[112,896]{1,0:T(8,128)S(1)}, u32[]{:S(2)}, u32[]{:S(2)}) collective-permute-start(f32[112,896]{1,0:T(8,128)S(1)} %get-tuple-element.35), channel_id=1, source_target_pairs={{0,48},{16,0},{32,16},{48,32},{1,49},{17,1},{33,17},{49,33},{2,50}... | collective-permute-start | bytes 1204232 | tf_op jit(solution)/shard_map/ppermute | solution.py:308
  15.1 0.8 shard_map.59
  15.9 7.4 %all-to-all-start = ((f32[32,4,896]{2,1,0:T(4,128)}), f32[32,4,896]{2,1,0:T(4,128)}, u32[]{:S(2)}, u32[]{:S(2)}) async-start(f32[32,4,896]{2,1,0:T(4,128)} %shard_map.59), calls=%async_computation | async-start | bytes 917504 | tf_op jit(solution)/shard_map/all_to_all | solution.py:290
  23.3 0.0 collective-permute-done.refs_1_
  23.3 4.1 %collective-permute-done.1.refs_2_ = f32[112,896]{1,0:T(8,128)S(1)} collective-permute-done((f32[112,896]{1,0:T(8,128)S(1)}, f32[112,896]{1,0:T(8,128)S(1)}, u32[]{:S(2)}, u32[]{:S(2)}) %collective-permute-start.1) | collective-permute-done | bytes 401440 | tf_op jit(solution)/shard_map/ppermute | solution.py:308
  27.5 0.3 shard_map.60
  27.8 9.5 %all-to-all-done = f32[32,4,896]{2,1,0:T(4,128)} async-done(((f32[32,4,896]{2,1,0:T(4,128)}), f32[32,4,896]{2,1,0:T(4,128)}, u32[]{:S(2)}, u32[]{:S(2)}) %all-to-all-start) | async-done | bytes 458784 | tf_op jit(solution)/shard_map/all_to_all | solution.py:290
  37.2 1.2 reshape.52.basis_ref
  38.4 5.6 %collective-permute-start.3 = (f32[128,896]{1,0:T(8,128)S(1)}, f32[128,896]{1,0:T(8,128)S(1)}, u32[]{:S(2)}, u32[]{:S(2)}) collective-permute-start(f32[128,896]{1,0:T(8,128)S(1)} %reshape.52.basis_ref), channel_id=1, source_target_pairs={{0,8},{8,0},{1,9},{9,1},{2,10},{10,2},{3,11},{11,3},{4,12},{12,4},... | collective-permute-start | bytes 1376264 | tf_op jit(solution)/shard_map/ppermute | solution.py:313
  44.0 0.8 shard_map.61
  44.8 0.6 collective-permute-done.3.basis_ref
  45.4 0.8 shard_map.62
  46.2 25.9 %all_to_all.35 = f32[32,16,256]{2,1,0:T(8,128)S(1)} all-to-all(f32[32,16,256]{2,1,0:T(8,128)S(1)} %bitcast.9), channel_id=1, replica_groups=mesh['y'=8,'x'=4,'core'=2,'z'=8] {'x','z'}, dimensions={0} | all-to-all | bytes 1048576 | tf_op jit(solution)/shard_map/all_to_all | solution.py:290
  72.2 0.1 broadcast_in_dim.6
  72.2 22.0 %all_to_all.36 = f32[32,16,256]{2,1,0:T(8,128)S(1)} all-to-all(f32[32,16,256]{2,1,0:T(8,128)S(1)} %broadcast_in_dim.6), channel_id=1, replica_groups=mesh['y'=8,'x'=4,'core'=2,'z'=8] {'x','z'}, dimensions={0} | all-to-all | bytes 1048576 | tf_op jit(solution)/shard_map/all_to_all | solution.py:290
  94.2 0.6 shard_map.64
  94.8 5.9 %collective-permute-start.4 = (f32[136,896]{1,0:T(8,128)S(1)}, f32[136,896]{1,0:T(8,128)S(1)}, u32[]{:S(2)}, u32[]{:S(2)}) collective-permute-start(f32[136,896]{1,0:T(8,128)S(1)} %shard_map.64), channel_id=1, source_target_pairs={{0,8},{8,0},{1,9},{9,1},{2,10},{10,2},{3,11},{11,3},{4,12},{12,4},... | collective-permute-start | bytes 1462280 | tf_op jit(solution)/shard_map/ppermute | solution.py:321
  100.8 0.6 shard_map.63
  101.4 0.8 collective-permute-done.4
  102.3 0.1 add.13
  102.3 0.8 slice.36
  103.1 3.5 %all-to-all-start.3 = ((f32[8,16,896]{2,1,0:T(8,128)}), f32[8,16,896]{2,1,0:T(8,128)S(1)}, u32[]{:S(2)}, u32[]{:S(2)}) async-start(f32[8,16,896]{2,1,0:T(8,128)} %bitcast.2), calls=%async_computation.3 | async-start | bytes 917504 | tf_op jit(solution)/shard_map/all_to_all | solution.py:290
  106.6 16.5 %all-to-all-done.3 = f32[8,16,896]{2,1,0:T(8,128)S(1)} async-done(((f32[8,16,896]{2,1,0:T(8,128)}), f32[8,16,896]{2,1,0:T(8,128)S(1)}, u32[]{:S(2)}, u32[]{:S(2)}) %all-to-all-start.3) | async-done | bytes 458784 | tf_op jit(solution)/shard_map/all_to_all | solution.py:290
  123.2 20.3 %all_to_all.37 = f32[8,16,1024]{2,1,0:T(8,128)S(1)} all-to-all(f32[8,16,1024]{2,1,0:T(8,128)S(1)} %broadcast_in_dim.7), channel_id=1, replica_groups=mesh['y'=8,'x'=4,'core'=2,'z'=8] {'y'}, dimensions={0} | all-to-all | bytes 1048576 | tf_op jit(solution)/shard_map/all_to_all | solution.py:290
  143.5 0.6 broadcast_add_fusion.square_ref
  144.1 0.1 broadcast_in_dim.8
  144.2 25.2 %all_to_all.38.own_ref = f32[4,128,896]{2,1,0:T(8,128)S(1)} all-to-all(f32[4,128,896]{2,1,0:T(8,128)S(1)} %broadcast_in_dim.8), channel_id=1, replica_groups=mesh['y'=8,'x'=4,'core'=2,'z'=8] {'x'}, dimensions={0} | all-to-all | bytes 3670016 | tf_op jit(solution)/shard_map/all_to_all | solution.py:290
  169.4 3.8 %collective-permute-start.5 = (f32[4,128,896]{2,1,0:T(8,128)S(1)}, f32[4,128,896]{2,1,0:T(8,128)S(1)}, u32[]{:S(2)}, u32[]{:S(2)}) collective-permute-start(f32[4,128,896]{2,1,0:T(8,128)S(1)} %all_to_all.38.own_ref), channel_id=1, source_target_pairs={{0,8},{8,0},{1,9},{9,1},{2,10},{10,2},{3,11},{11,3},{4,12},{12,4},... | collective-permute-start | bytes 5505032 | tf_op jit(solution)/shard_map/ppermute | solution.py:333
  173.2 3.4 %collective-permute-done.5.oth_ref = f32[4,128,896]{2,1,0:T(8,128)S(1)} collective-permute-done((f32[4,128,896]{2,1,0:T(8,128)S(1)}, f32[4,128,896]{2,1,0:T(8,128)S(1)}, u32[]{:S(2)}, u32[]{:S(2)}) %collective-permute-start.5) | collective-permute-done | bytes 1835040 | tf_op jit(solution)/shard_map/ppermute | solution.py:333
  176.6 1.1 shard_map.66
  177.6 1.3 copy-done
  178.9 0.6 copy-done.7
  179.5 4.0 %all-to-all-start.6 = ((f32[8,8,256]{2,1,0:T(8,128)}), f32[8,8,256]{2,1,0:T(8,128)}, u32[]{:S(2)}, u32[]{:S(2)}) async-start(f32[8,8,256]{2,1,0:T(8,128)} %copy-done.7), calls=%async_computation.6 | async-start | bytes 131072 | tf_op jit(solution)/shard_map/all_to_all | solution.py:290
  183.5 1.5 copy-done.1
  185.0 1.1 copy-done.6
  186.2 0.7 copy-done.8
  186.9 2.7 %shard_map.65 = f32[112,3584]{1,0:T(8,128)} custom-call(f32[112,256]{1,0:T(8,128)S(1)} %get-tuple-element.41.mine_ref, f32[2,128]{1,0:T(2,128)S(1)} %copy-done.8, f32[112,3584]{1,0:T(8,128)S(1)} %copy-done.4, bf16[112,3584]{1,0:T(8,128)(2,1)S(1)} %copy-done.6, f32[4,128,896]{2,1,0:T(8,128)S(1)} %all_to_all.38.own_ref, f32[4,128,896]{2,1,0:T(8,128)S(1)} %copy-done.1), custom_call_target="tpu_custom_call" | custom-call | flops 616562688 | bytes 8486912 | tf_op jit(solution)/shard_map/pallas_call | solution.py:231
  189.6 1.1 all-to-all-done.6
  190.7 0.9 reduce_sum.39
  191.6 1.5 copy-done.2
  193.1 0.7 copy-done.9
  193.8 1.7 shard_map.67
  (22 shorter events, 0.2 us)
Async XLA Ops:
  0.6 1.4 copy-start.3
  2.1 1.1 copy-start.5
  3.2 11.9 %copy-start.10 = (f32[4,3584]{1,0:T(4,128)S(1)}, f32[4,3584]{1,0:T(4,128)}, u32[]{:S(2)}) copy-start(f32[4,3584]{1,0:T(4,128)} %basis_ref.1) | copy-start | bytes 172036
  3.7 19.6 %collective-permute-start = (f32[112,896]{1,0:T(8,128)S(1)}, f32[112,896]{1,0:T(8,128)S(1)}, u32[]{:S(2)}, u32[]{:S(2)}) collective-permute-start(f32[112,896]{1,0:T(8,128)S(1)} %get-tuple-element.33), channel_id=1, source_target_pairs={{0,16},{16,32},{32,48},{48,0},{1,17},{17,33},{33,49},{49,1},{2,18}... | collective-permute-start | bytes 1204232 | tf_op jit(solution)/shard_map/ppermute | solution.py:308
  7.7 19.8 %collective-permute-start.1 = (f32[112,896]{1,0:T(8,128)S(1)}, f32[112,896]{1,0:T(8,128)S(1)}, u32[]{:S(2)}, u32[]{:S(2)}) collective-permute-start(f32[112,896]{1,0:T(8,128)S(1)} %get-tuple-element.34), channel_id=1, source_target_pairs={{0,32},{16,48},{32,0},{48,16},{1,33},{17,49},{33,1},{49,17},{2,34}... | collective-permute-start | bytes 1204232 | tf_op jit(solution)/shard_map/ppermute | solution.py:308
  12.1 15.4 %collective-permute-start.2 = (f32[112,896]{1,0:T(8,128)S(1)}, f32[112,896]{1,0:T(8,128)S(1)}, u32[]{:S(2)}, u32[]{:S(2)}) collective-permute-start(f32[112,896]{1,0:T(8,128)S(1)} %get-tuple-element.35), channel_id=1, source_target_pairs={{0,48},{16,0},{32,16},{48,32},{1,49},{17,1},{33,17},{49,33},{2,50}... | collective-permute-start | bytes 1204232 | tf_op jit(solution)/shard_map/ppermute | solution.py:308
  15.9 21.3 %all-to-all-start = ((f32[32,4,896]{2,1,0:T(4,128)}), f32[32,4,896]{2,1,0:T(4,128)}, u32[]{:S(2)}, u32[]{:S(2)}) async-start(f32[32,4,896]{2,1,0:T(4,128)} %shard_map.59), calls=%async_computation | async-start | bytes 917504 | tf_op jit(solution)/shard_map/all_to_all | solution.py:290
  38.4 7.0 %collective-permute-start.3 = (f32[128,896]{1,0:T(8,128)S(1)}, f32[128,896]{1,0:T(8,128)S(1)}, u32[]{:S(2)}, u32[]{:S(2)}) collective-permute-start(f32[128,896]{1,0:T(8,128)S(1)} %reshape.52.basis_ref), channel_id=1, source_target_pairs={{0,8},{8,0},{1,9},{9,1},{2,10},{10,2},{3,11},{11,3},{4,12},{12,4},... | collective-permute-start | bytes 1376264 | tf_op jit(solution)/shard_map/ppermute | solution.py:313
  94.8 7.4 %collective-permute-start.4 = (f32[136,896]{1,0:T(8,128)S(1)}, f32[136,896]{1,0:T(8,128)S(1)}, u32[]{:S(2)}, u32[]{:S(2)}) collective-permute-start(f32[136,896]{1,0:T(8,128)S(1)} %shard_map.64), channel_id=1, source_target_pairs={{0,8},{8,0},{1,9},{9,1},{2,10},{10,2},{3,11},{11,3},{4,12},{12,4},... | collective-permute-start | bytes 1462280 | tf_op jit(solution)/shard_map/ppermute | solution.py:321
  103.1 20.0 %all-to-all-start.3 = ((f32[8,16,896]{2,1,0:T(8,128)}), f32[8,16,896]{2,1,0:T(8,128)S(1)}, u32[]{:S(2)}, u32[]{:S(2)}) async-start(f32[8,16,896]{2,1,0:T(8,128)} %bitcast.2), calls=%async_computation.3 | async-start | bytes 917504 | tf_op jit(solution)/shard_map/all_to_all | solution.py:290
  169.4 14.2 %copy-start.4 = (f32[112,3584]{1,0:T(8,128)S(1)}, f32[112,3584]{1,0:T(8,128)}, u32[]{:S(2)}) copy-start(f32[112,3584]{1,0:T(8,128)} %m_ref.3) | copy-start | bytes 4816900
  169.4 7.2 %collective-permute-start.5 = (f32[4,128,896]{2,1,0:T(8,128)S(1)}, f32[4,128,896]{2,1,0:T(8,128)S(1)}, u32[]{:S(2)}, u32[]{:S(2)}) collective-permute-start(f32[4,128,896]{2,1,0:T(8,128)S(1)} %all_to_all.38.own_ref), channel_id=1, source_target_pairs={{0,8},{8,0},{1,9},{9,1},{2,10},{10,2},{3,11},{11,3},{4,12},{12,4},... | collective-permute-start | bytes 5505032 | tf_op jit(solution)/shard_map/ppermute | solution.py:333
  177.6 1.3 copy-start
  178.9 0.6 copy-start.7
  179.5 11.2 %all-to-all-start.6 = ((f32[8,8,256]{2,1,0:T(8,128)}), f32[8,8,256]{2,1,0:T(8,128)}, u32[]{:S(2)}, u32[]{:S(2)}) async-start(f32[8,8,256]{2,1,0:T(8,128)} %copy-done.7), calls=%async_computation.6 | async-start | bytes 131072 | tf_op jit(solution)/shard_map/all_to_all | solution.py:290
  183.5 1.5 copy-start.1
  185.0 1.1 copy-start.6
  186.2 0.7 copy-start.8
  191.6 1.5 copy-start.2
  193.1 0.7 copy-start.9

commit v5 on v4

--- a/solution.py
+++ b/solution.py
@@ -3,6 +3,7 @@
 
 import jax
 import jax.numpy as jnp
+import numpy as np
 from jax import lax
 from jax.experimental import pallas as pl
 from jax.experimental.pallas import tpu as pltpu
@@ -17,7 +18,7 @@
 norm_eps = 1e-06
 carry_keep = 0.9
 SWAP = [(0, 1), (1, 0)]
-PARAMS = pltpu.CompilerParams(vmem_limit_bytes=10 * 1024 * 1024)
+PARAMS = pltpu.CompilerParams(vmem_limit_bytes=12 * 1024 * 1024)
 VMEM = pl.BlockSpec(memory_space=pltpu.VMEM)
 ANY = pl.BlockSpec(memory_space=pl.ANY)
 HBM = pl.BlockSpec(memory_space=pltpu.HBM)
@@ -174,78 +175,54 @@
     )(*tall, panel)
 
 
-def product(left, own_ref, oth_ref, at=0):
-    rows = left.shape[0] // 2
-    high, low = split(jnp.concatenate([own_ref[at], oth_ref[at]], axis=0))
-    dot = functools.partial(jnp.dot, preferred_element_type=jnp.float32)
-    sums = dot(left, high)
-    return sums[:rows] + sums[rows:] + dot(left[:rows], low)
-
-
-def scaled(mine_ref, factor):
-    return jnp.concatenate(split(mine_ref[...] * factor), axis=0)
-
-
 def row(pair):
     return jnp.concatenate([pair[:1], pair[1:2]], axis=1)
 
 
-def squares_kernel(own_ref, oth_ref, out_ref):
+def squares_kernel(own_ref, out_ref):
     nz, lines, _ = out_ref.shape
     part = own_ref.shape[2]
     ones = jnp.ones((lines, part), jnp.bfloat16)
     total = 0.0
     for j in range(NX):
-        block = jnp.concatenate([own_ref[j], oth_ref[j]], axis=0)
-        for piece in split(block * block):
+        for piece in split(own_ref[j] * own_ref[j]):
             dims = (((1,), (1,)), ((), ()))
             total += lax.dot_general(ones, piece, dims, preferred_element_type=jnp.float32)
     for z in range(nz):
         out_ref[z] = total
 
 
-def row_squares(own, oth):
+def row_squares(own):
     nx, half, part = own.shape
-    shape = (NZ, 8, 2 * half)
     return pl.pallas_call(
         squares_kernel,
-        in_specs=[VMEM] * 2,
+        in_specs=[VMEM],
         out_specs=VMEM,
-        out_shape=jax.ShapeDtypeStruct(shape, jnp.float32),
-        compiler_params=PARAMS,
-        cost_estimate=cost(4 * nx * half * part, 8 * nx * half * part),
-    )(own, oth)
-
-
-def momentum_kernel(mine_ref, square_ref, m_ref, g_ref, own_ref, oth_ref, out_ref):
-    left = scaled(mine_ref, row((1.0 - carry_keep) / square_ref[...]))
-    out_ref[...] = m_ref[...] + g_ref[...].astype(jnp.float32) - product(left, own_ref, oth_ref)
-
-
-def momentum_out(mine, square, momentum, gradient, own, oth):
-    rows, cols = momentum.shape
-    half, part = own.shape[1:]
-    block = pl.BlockSpec((rows, part), lambda j: (0, j))
-    right = pl.BlockSpec((1, half, part), lambda j: (j, 0, 0))
-    whole = [pl.BlockSpec(array.shape, lambda j: (0, 0)) for array in (mine, square)]
-    return pl.pallas_call(
-        momentum_kernel,
-        grid=(NX,),
-        in_specs=[*whole, block, block, right, right],
-        out_specs=block,
-        out_shape=jax.ShapeDtypeStruct((rows, cols), jnp.float32),
-        compiler_params=PARAMS,
-        cost_estimate=cost(12 * rows * cols * half, 4 * (3 * rows + 2 * half) * cols),
-    )(mine, square, momentum, gradient, own, oth)
-
-
-def update_kernel(
-    mine_ref, square_ref, sums_ref, own_ref, oth_ref, u_out, b_out, u_buf, b_buf, sems
+        out_shape=jax.ShapeDtypeStruct((NC * NZ, 8, half), jnp.float32),
+        compiler_params=PARAMS,
+        cost_estimate=cost(4 * nx * half * part, 4 * nx * half * part),
+    )(own)
+
+
+def last_kernel(
+    mine_ref, square_ref, sums_ref, m_ref, g_ref, own_ref, oth_ref,
+    m_out, u_out, b_out, m_buf, u_buf, b_buf, sems,
 ):
-    (ranks, _), (half, part) = b_buf.shape, own_ref.shape[1:]
+    rows, (ranks, _), (half, part) = mine_ref.shape[0], b_buf.shape, own_ref.shape[1:]
+    core = lax.axis_index("core")
     square = square_ref[...]
-    right_scale = jnp.sqrt(sums_ref[...] / square + norm_eps)
-    left = scaled(mine_ref, row(math.sqrt(ROWS * COLS / RANK) / (square * right_scale)))
+    sums = []
+    for side in (core, 1 - core):
+        total = sums_ref[side * NZ]
+        for z in range(1, NZ):
+            total = total + sums_ref[side * NZ + z]
+        sums.append(total[:1])
+    right_scale = jnp.sqrt(jnp.concatenate(sums, axis=0) / square + norm_eps)
+    panel = mine_ref[...]
+    m_left = split(panel * row((1.0 - carry_keep) / square))
+    u_left = split(panel * row(math.sqrt(ROWS * COLS / RANK) / (square * right_scale)))
+    left = jnp.concatenate([*m_left, *u_left], axis=0)
+    left_high = jnp.concatenate([m_left[0], u_left[0]], axis=0)
     first = (lax.axis_index("y") * NX + lax.axis_index("x")) * ranks
     group = pl.multiple_of(first // 8 * 8, 8)
     lane = lax.broadcasted_iota(jnp.int32, (8, half), 1)
@@ -253,45 +230,64 @@
     scale = 1.0 / (jnp.sqrt(square[:1]) * right_scale[:1])
     scale = jnp.sum(jnp.where(lane == rank, scale, 0.0), axis=1, keepdims=True)
 
+    dot = functools.partial(jnp.dot, preferred_element_type=jnp.float32)
     copies = []
     for j in range(NX):
-        columns = pl.ds(j * part, part)
-        eight = own_ref[j, pl.ds(group, 8), :] * scale
+        own_at = jnp.where(core == 0, j, NX - 1 - j)
+        own, columns = own_ref[own_at], pl.ds(j * part, part)
+        high, low = split(jnp.concatenate([own, oth_ref[NX - 1 - own_at]], axis=0))
+        sums, rest = dot(left, high), dot(left_high, low)
+        feedback = sums[:rows] + sums[rows : 2 * rows] + rest[:rows]
+        update = sums[2 * rows : 3 * rows] + sums[3 * rows :] + rest[rows:]
+        combined = m_ref[:, columns] + g_ref[:, columns].astype(jnp.float32)
+        m_buf[:, columns] = combined - feedback
+        u_buf[:, columns] = update.astype(jnp.bfloat16)
+        eight = own_ref[own_at, pl.ds(group, 8), :] * scale
         b_buf[:, columns] = jnp.where(first > group, eight[8 - ranks :], eight[:ranks])
-    copies.append(pltpu.make_async_copy(b_buf, b_out, sems.at[NX]))
+        at = (slice(None), columns)
+        for i, (buf, out) in enumerate(((m_buf, m_out), (u_buf, u_out))):
+            copies.append(pltpu.make_async_copy(buf.at[at], out.at[at], sems.at[j, i]))
+            copies[-1].start()
+    copies.append(pltpu.make_async_copy(b_buf, b_out, sems.at[NX, 0]))
     copies[-1].start()
-    for j in range(NX):
-        columns = pl.ds(j * part, part)
-        u_buf[:, columns] = product(left, own_ref, oth_ref, j).astype(jnp.bfloat16)
-        at = (slice(None), columns)
-        copies.append(pltpu.make_async_copy(u_buf.at[at], u_out.at[at], sems.at[j]))
-        copies[-1].start()
     for copy in copies:
         copy.wait()
 
 
-def update_out(mine, square, sums, own, oth, ranks):
-    rows, (half, part) = mine.shape[0], own.shape[1:]
-    cols = NX * part
-    shapes = [((rows, cols), jnp.bfloat16), ((ranks, cols), jnp.float32)]
-    return pl.pallas_call(
-        update_kernel,
-        in_specs=[VMEM] * 5,
-        out_specs=[HBM] * 2,
+def last_out(mine, square, sums, momentum, gradient, own, oth, ranks):
+    rows, cols = momentum.shape
+    half = own.shape[1]
+    shapes = [
+        ((rows, cols), jnp.float32),
+        ((rows, cols), jnp.bfloat16),
+        ((ranks, cols), jnp.float32),
+    ]
+    return pl.pallas_call(
+        last_kernel,
+        in_specs=[VMEM] * 7,
+        out_specs=[HBM] * 3,
         out_shape=[jax.ShapeDtypeStruct(*shape) for shape in shapes],
         scratch_shapes=[pltpu.VMEM(*shape) for shape in shapes]
-        + [pltpu.SemaphoreType.DMA((NX + 1,))],
-        compiler_params=PARAMS,
-        cost_estimate=cost(12 * rows * cols * half, 4 * (rows + 2 * half) * cols),
-    )(mine, square, sums, own, oth)
+        + [pltpu.SemaphoreType.DMA((NX + 1, 2))],
+        compiler_params=PARAMS,
+        cost_estimate=cost(24 * rows * cols * half, 4 * (4 * rows + 2 * half) * cols),
+    )(mine, square, sums, momentum, gradient, own, oth)
 
 
 def exchange(blocks, axes):
     return lax.all_to_all(blocks, axes, 0, 0, tiled=True)
 
 
+def opposed(blocks, axes):
+    sizes = {"y": NY, "x": NX, "core": NC, "z": NZ}
+    at = np.arange(math.prod(sizes[axis] for axis in axes)).reshape([sizes[axis] for axis in axes])
+    at = np.moveaxis(at, axes.index("core"), 0).reshape(NC, -1)
+    groups = [at[0].tolist(), at[1, ::-1].tolist()]
+    return lax.all_to_all(blocks, axes, 0, 0, axis_index_groups=groups, tiled=True)
+
+
 def spread(block, axes, n):
-    return exchange(jnp.broadcast_to(block[None], (n, *block.shape)), axes)
+    return opposed(jnp.broadcast_to(block[None], (n, *block.shape)), axes)
 
 
 def shards(momentum, gradient, basis_panel):
@@ -314,27 +310,28 @@
 
     panel = [panel_part(tall, basis, padded) for basis in (basis_own, basis_oth)]
     panel = jnp.concatenate(panel, axis=2)
-    panel = exchange(panel.reshape(NX * NZ, padded // NZ, 2 * half), ("x", "z"))
-    panel = spread(jnp.sum(panel, axis=0), ("x", "z"), NX * NZ)
+    panel = opposed(panel.reshape(NX * NZ, padded // NZ, 2 * half), ("x", "core", "z"))
+    panel = spread(jnp.sum(panel, axis=0), ("x", "core", "z"), NX * NZ)
     panel = panel.reshape(NX, padded, 2 * half)
 
     right_oth = lax.ppermute(right_part(1, tall, panel)[0], "core", SWAP)
     right_sum, mine = right_part(0, tall, panel)
     right_sum = right_sum + right_oth
     square = right_sum[half, : 2 * half].reshape(2, half)
-    right_sum = exchange(right_sum[:half].reshape(NY, own_ranks, part), "y")
+    right_sum, square = lax.optimization_barrier((right_sum[:half], square))
+    right_sum = opposed(right_sum.reshape(NY, own_ranks, part), ("y", "core"))
     right_sum = jnp.sum(right_sum, axis=0)
     beside = jnp.zeros((own_ranks, 128), jnp.float32).at[:2, :half].set(square)
-    got = spread(jnp.concatenate([right_sum, beside], axis=1), "y", NY)
+    got = spread(jnp.concatenate([right_sum, beside], axis=1), ("y", "core"), NY)
     square = jnp.sum(got[:, :2, part : part + half], axis=0) + norm_eps
 
     own, square = lax.optimization_barrier((got[:, :, :part].reshape(half, part), square))
-    own = spread(own, "x", NX)
-    own, oth = lax.optimization_barrier((own, lax.ppermute(own, "core", SWAP)))
-    sums = jnp.sum(exchange(row_squares(own, oth), "z"), axis=0)[0].reshape(2, half)
-
-    momentum_new = momentum_out(mine, square, momentum, gradient, own, oth)
-    update, basis_new = update_out(mine, square, sums, own, oth, rank_rows)
+    own = spread(own, ("x", "core"), NX)
+    oth = lax.ppermute(own, "core", SWAP)
+    sums = exchange(row_squares(own), ("core", "z"))
+    momentum_new, update, basis_new = last_out(
+        mine, square, sums, momentum, gradient, own, oth, rank_rows
+    )
     return momentum_new, basis_new, update
 
 

time: 196 us -> 181 us (0.923); the launches traced: 195 us -> 178 us
  blocking collectives: 93.3 us -> 116 us
  waiting for transfers between devices: 36.1 us -> 15.1 us
  local copies, waits for them, and re-layouts: 12.2 us -> 4.03 us
  starting transfers between devices: 41.5 us -> 33.9 us
  Pallas kernels: 9.94 us -> 7.73 us
    all_to_all x0 -> x5, blocking collectives: none -> 106 us  [opposed(): lax.all_to_all(blocks, axes, 0, 0, axis_index_groups=groups, tiled=True)]
    all_to_all x4 -> x1, blocking collectives: 93.3 us -> 10.2 us  [exchange(): return lax.all_to_all(blocks, axes, 0, 0, tiled=True)]
    all_to_all x3 -> x1, waiting for transfers between devices: 27.1 us -> 9.46 us  [exchange(): return lax.all_to_all(blocks, axes, 0, 0, tiled=True)]
    all_to_all x3 -> x1, starting transfers between devices: 14.8 us -> 7.35 us  [exchange(): return lax.all_to_all(blocks, axes, 0, 0, tiled=True)]
    unnamed x22 -> x10, local copies, waits for them, and re-layouts: 9.96 us -> 2.57 us
    ppermute x1, starting transfers between devices: 5.93 us -> 2.3 us  [shards(): right_oth = lax.ppermute(right_part(1, tall, panel)[0], 'core', SWAP)]
    ppermute x1, starting transfers between devices: 3.8 us -> 7.29 us  [shards(): oth = lax.ppermute(own, 'core', SWAP)]
    ppermute x1, waiting for transfers between devices: 3.39 us -> 0.01 us  [shards(): oth = lax.ppermute(own, 'core', SWAP)]
  transfers between devices with their start and end apart: 9 -> 7, of which waited for: 7 -> 4; matrix products, arithmetic and copies ran while one was open for 0% -> 0% of each run, Pallas kernels for 3% -> 2%
where the time goes in v5:
time: 181 us; the launch traced here: 178 us
  blocking collectives  116 us (64%)
  starting transfers between devices  33.9 us (19%)
  waiting for transfers between devices  15.1 us (8%)
  Pallas kernels  7.73 us (4%)
  local copies, waits for them, and re-layouts  4.03 us (2%)
    all_to_all x5, blocking collectives, opposed(): lax.all_to_all(blocks, axes, 0, 0, axis_index_groups=groups, tiled=True)  106 us
    ppermute x3, starting transfers between devices, shards(): lax.ppermute(blocks[j], 'x', [(i, (i + j) % NX) for i in range(NX)])  11.4 us
    all_to_all x1, blocking collectives, exchange(): return lax.all_to_all(blocks, axes, 0, 0, tiled=True)  10.2 us
    all_to_all x1, waiting for transfers between devices, exchange(): return lax.all_to_all(blocks, axes, 0, 0, tiled=True)  9.46 us
    all_to_all x1, starting transfers between devices, exchange(): return lax.all_to_all(blocks, axes, 0, 0, tiled=True)  7.35 us
    ppermute x1, starting transfers between devices, shards(): oth = lax.ppermute(own, 'core', SWAP)  7.29 us
    ppermute x1, starting transfers between devices, shards(): basis_oth = lax.ppermute(basis_own, 'core', SWAP)  5.57 us
    ppermute x3, waiting for transfers between devices, shards(): lax.ppermute(blocks[j], 'x', [(i, (i + j) % NX) for i in range(NX)])  4.15 us
  transfers between devices with their start and end apart: 7, of which 4 were waited for; matrix products, arithmetic and copies ran while one was open for 0% of the time, Pallas kernels for 2%

profile of v5, /device:TPU:1, one launch (start us, length us, event | category | flops | bytes accessed | tf_op | source)
XLA Modules:
  0.0 177.8 jit_solution(15284425364532706102)
XLA Ops:
  0.6 0.0 copy-start
  0.6 1.4 copy-done
  2.1 0.0 copy-start.2
  2.1 1.1 copy-done.2
  3.2 0.0 copy-start.4
  3.2 0.5 shard_map.58
  3.7 3.9 %collective-permute-start = (f32[112,896]{1,0:T(8,128)S(1)}, f32[112,896]{1,0:T(8,128)S(1)}, u32[]{:S(2)}, u32[]{:S(2)}) collective-permute-start(f32[112,896]{1,0:T(8,128)S(1)} %get-tuple-element.34), channel_id=1, source_target_pairs={{0,16},{16,32},{32,48},{48,0},{1,17},{17,33},{33,49},{49,1},{2,18}... | collective-permute-start | bytes 1204232 | tf_op jit(solution)/shard_map/ppermute | solution.py:304
  7.7 4.4 %collective-permute-start.1 = (f32[112,896]{1,0:T(8,128)S(1)}, f32[112,896]{1,0:T(8,128)S(1)}, u32[]{:S(2)}, u32[]{:S(2)}) collective-permute-start(f32[112,896]{1,0:T(8,128)S(1)} %get-tuple-element.35), channel_id=1, source_target_pairs={{0,32},{16,48},{32,0},{48,16},{1,33},{17,49},{33,1},{49,17},{2,34}... | collective-permute-start | bytes 1204232 | tf_op jit(solution)/shard_map/ppermute | solution.py:304
  12.1 3.1 %collective-permute-start.2 = (f32[112,896]{1,0:T(8,128)S(1)}, f32[112,896]{1,0:T(8,128)S(1)}, u32[]{:S(2)}, u32[]{:S(2)}) collective-permute-start(f32[112,896]{1,0:T(8,128)S(1)} %get-tuple-element.36), channel_id=1, source_target_pairs={{0,48},{16,0},{32,16},{48,32},{1,49},{17,1},{33,17},{49,33},{2,50}... | collective-permute-start | bytes 1204232 | tf_op jit(solution)/shard_map/ppermute | solution.py:304
  15.1 0.0 copy-done.4
  15.1 0.8 shard_map.59
  15.9 7.4 %all-to-all-start = ((f32[32,4,896]{2,1,0:T(4,128)}), f32[32,4,896]{2,1,0:T(4,128)}, u32[]{:S(2)}, u32[]{:S(2)}) async-start(f32[32,4,896]{2,1,0:T(4,128)} %shard_map.59), calls=%async_computation | async-start | bytes 917504 | tf_op jit(solution)/shard_map/all_to_all | solution.py:278
  23.3 0.0 collective-permute-done.refs_1_
  23.3 4.1 %collective-permute-done.1.refs_2_ = f32[112,896]{1,0:T(8,128)S(1)} collective-permute-done((f32[112,896]{1,0:T(8,128)S(1)}, f32[112,896]{1,0:T(8,128)S(1)}, u32[]{:S(2)}, u32[]{:S(2)}) %collective-permute-start.1) | collective-permute-done | bytes 401440 | tf_op jit(solution)/shard_map/ppermute | solution.py:304
  27.5 0.0 collective-permute-done.2.refs_3_
  27.5 0.3 shard_map.60
  27.8 9.5 %all-to-all-done = f32[32,4,896]{2,1,0:T(4,128)} async-done(((f32[32,4,896]{2,1,0:T(4,128)}), f32[32,4,896]{2,1,0:T(4,128)}, u32[]{:S(2)}, u32[]{:S(2)}) %all-to-all-start) | async-done | bytes 458784 | tf_op jit(solution)/shard_map/all_to_all | solution.py:278
  37.2 1.2 reshape.50.basis_ref
  38.4 5.6 %collective-permute-start.3 = (f32[128,896]{1,0:T(8,128)S(1)}, f32[128,896]{1,0:T(8,128)S(1)}, u32[]{:S(2)}, u32[]{:S(2)}) collective-permute-start(f32[128,896]{1,0:T(8,128)S(1)} %reshape.50.basis_ref), channel_id=1, source_target_pairs={{0,8},{8,0},{1,9},{9,1},{2,10},{10,2},{3,11},{11,3},{4,12},{12,4},... | collective-permute-start | bytes 1376264 | tf_op jit(solution)/shard_map/ppermute | solution.py:309
  44.0 0.8 shard_map.61
  44.8 0.6 collective-permute-done.3.basis_ref
  45.4 0.8 shard_map.62
  46.3 28.3 %all_to_all.35 = f32[32,16,256]{2,1,0:T(8,128)S(1)} all-to-all(f32[32,16,256]{2,1,0:T(8,128)S(1)} %bitcast.7), channel_id=1, replica_groups={{0,1,2,3,4,5,6,7,16,17,18,19,20,21,22,23,32,33,34,35,36,37,38,39,48,49,..., dimensions={0} | all-to-all | bytes 1048576 | tf_op jit(solution)/shard_map/all_to_all | solution.py:286
  74.6 0.1 broadcast_in_dim.6
  74.6 22.1 %all_to_all.36 = f32[32,16,256]{2,1,0:T(8,128)S(1)} all-to-all(f32[32,16,256]{2,1,0:T(8,128)S(1)} %broadcast_in_dim.6), channel_id=1, replica_groups={{0,1,2,3,4,5,6,7,16,17,18,19,20,21,22,23,32,33,34,35,36,37,38,39,48,49,..., dimensions={0} | all-to-all | bytes 1048576 | tf_op jit(solution)/shard_map/all_to_all | solution.py:286
  96.7 0.6 shard_map.64
  97.4 2.3 %collective-permute-start.4 = (f32[136,896]{1,0:T(8,128)S(1)}, f32[136,896]{1,0:T(8,128)S(1)}, u32[]{:S(2)}, u32[]{:S(2)}) collective-permute-start(f32[136,896]{1,0:T(8,128)S(1)} %shard_map.64), channel_id=1, source_target_pairs={{0,8},{8,0},{1,9},{9,1},{2,10},{10,2},{3,11},{11,3},{4,12},{12,4},... | collective-permute-start | bytes 1462280 | tf_op jit(solution)/shard_map/ppermute | solution.py:317
  99.7 0.6 shard_map.63
  100.3 0.8 collective-permute-done.4
  101.1 0.1 add.13
  101.3 15.5 %all_to_all.37 = f32[8,16,896]{2,1,0:T(8,128)S(1)} all-to-all(f32[8,16,896]{2,1,0:T(8,128)S(1)} %bitcast.8), channel_id=1, replica_groups={{0,64,128,192,256,320,384,448},{456,392,328,264,200,136,72,8},{1,65,129..., dimensions={0} | all-to-all | bytes 917504 | tf_op jit(solution)/shard_map/all_to_all | solution.py:286
  116.9 17.2 %all_to_all.38 = f32[8,16,1024]{2,1,0:T(8,128)S(1)} all-to-all(f32[8,16,1024]{2,1,0:T(8,128)S(1)} %broadcast_in_dim.7), channel_id=1, replica_groups={{0,64,128,192,256,320,384,448},{456,392,328,264,200,136,72,8},{1,65,129..., dimensions={0} | all-to-all | bytes 1048576 | tf_op jit(solution)/shard_map/all_to_all | solution.py:286
  134.2 0.1 broadcast_in_dim.8
  134.3 0.0 copy-start.3
  134.3 22.7 %all_to_all.39.own_ref = f32[4,128,896]{2,1,0:T(8,128)S(1)} all-to-all(f32[4,128,896]{2,1,0:T(8,128)S(1)} %broadcast_in_dim.8), channel_id=1, replica_groups={{0,16,32,48},{56,40,24,8},{1,17,33,49},{57,41,25,9},{2,18,34,50},{58,42..., dimensions={0} | all-to-all | bytes 3670016 | tf_op jit(solution)/shard_map/all_to_all | solution.py:286
  157.0 0.0 copy-start.1
  157.0 7.3 %collective-permute-start.5 = (f32[4,128,896]{2,1,0:T(8,128)S(1)}, f32[4,128,896]{2,1,0:T(8,128)S(1)}, u32[]{:S(2)}, u32[]{:S(2)}) collective-permute-start(f32[4,128,896]{2,1,0:T(8,128)S(1)} %all_to_all.39.own_ref), channel_id=1, source_target_pairs={{0,8},{8,0},{1,9},{9,1},{2,10},{10,2},{3,11},{11,3},{4,12},{12,4},... | collective-permute-start | bytes 5505032 | tf_op jit(solution)/shard_map/ppermute | solution.py:330
  164.3 0.6 shard_map.65
  165.0 10.2 %all_to_all.40.sums_ref = f32[16,8,128]{2,1,0:T(8,128)S(1)} all-to-all(f32[16,8,128]{2,1,0:T(8,128)S(1)} %shard_map.65), channel_id=1, replica_groups=mesh['y'=8,'x'=4,'core'=2,'z'=8] {'core','z'}, dimensions={0} | all-to-all | bytes 131072 | tf_op jit(solution)/shard_map/all_to_all | solution.py:278
  175.1 0.0 collective-permute-done.5.oth_ref
  175.1 0.0 copy-done.3
  175.2 0.0 copy-done.1
  175.2 2.6 %shard_map.66 = (f32[112,3584]{1,0:T(8,128)}, bf16[112,3584]{1,0:T(8,128)(2,1)}, f32[4,3584]{1,0:T(4,128)}) custom-call(f32[112,256]{1,0:T(8,128)S(1)} %get-tuple-element.42.mine_ref, f32[2,128]{1,0:T(2,128)S(1)} %broadcast_add_fusion.square_ref, f32[16,8,128]{2,1,0:T(8,128)S(1)} %all_to_all.40.sums_ref, f32[112,3584]{1,0:T(8,128)S(1)} %copy-done.1, ...), custom_call_target="tpu_custom_call" | custom-call | flops 1233125376 | bytes 10092544 | tf_op jit(solution)/shard_map/pallas_call | solution.py:265
  (10 shorter events, 0.3 us)
Async XLA Ops:
  0.6 1.4 copy-start
  2.1 1.1 copy-start.2
  3.2 11.9 %copy-start.4 = (f32[4,3584]{1,0:T(4,128)S(1)}, f32[4,3584]{1,0:T(4,128)}, u32[]{:S(2)}) copy-start(f32[4,3584]{1,0:T(4,128)} %basis_ref.1) | copy-start | bytes 172036
  3.7 19.6 %collective-permute-start = (f32[112,896]{1,0:T(8,128)S(1)}, f32[112,896]{1,0:T(8,128)S(1)}, u32[]{:S(2)}, u32[]{:S(2)}) collective-permute-start(f32[112,896]{1,0:T(8,128)S(1)} %get-tuple-element.34), channel_id=1, source_target_pairs={{0,16},{16,32},{32,48},{48,0},{1,17},{17,33},{33,49},{49,1},{2,18}... | collective-permute-start | bytes 1204232 | tf_op jit(solution)/shard_map/ppermute | solution.py:304
  7.7 19.8 %collective-permute-start.1 = (f32[112,896]{1,0:T(8,128)S(1)}, f32[112,896]{1,0:T(8,128)S(1)}, u32[]{:S(2)}, u32[]{:S(2)}) collective-permute-start(f32[112,896]{1,0:T(8,128)S(1)} %get-tuple-element.35), channel_id=1, source_target_pairs={{0,32},{16,48},{32,0},{48,16},{1,33},{17,49},{33,1},{49,17},{2,34}... | collective-permute-start | bytes 1204232 | tf_op jit(solution)/shard_map/ppermute | solution.py:304
  12.1 15.4 %collective-permute-start.2 = (f32[112,896]{1,0:T(8,128)S(1)}, f32[112,896]{1,0:T(8,128)S(1)}, u32[]{:S(2)}, u32[]{:S(2)}) collective-permute-start(f32[112,896]{1,0:T(8,128)S(1)} %get-tuple-element.36), channel_id=1, source_target_pairs={{0,48},{16,0},{32,16},{48,32},{1,49},{17,1},{33,17},{49,33},{2,50}... | collective-permute-start | bytes 1204232 | tf_op jit(solution)/shard_map/ppermute | solution.py:304
  15.9 21.3 %all-to-all-start = ((f32[32,4,896]{2,1,0:T(4,128)}), f32[32,4,896]{2,1,0:T(4,128)}, u32[]{:S(2)}, u32[]{:S(2)}) async-start(f32[32,4,896]{2,1,0:T(4,128)} %shard_map.59), calls=%async_computation | async-start | bytes 917504 | tf_op jit(solution)/shard_map/all_to_all | solution.py:278
  38.4 7.0 %collective-permute-start.3 = (f32[128,896]{1,0:T(8,128)S(1)}, f32[128,896]{1,0:T(8,128)S(1)}, u32[]{:S(2)}, u32[]{:S(2)}) collective-permute-start(f32[128,896]{1,0:T(8,128)S(1)} %reshape.50.basis_ref), channel_id=1, source_target_pairs={{0,8},{8,0},{1,9},{9,1},{2,10},{10,2},{3,11},{11,3},{4,12},{12,4},... | collective-permute-start | bytes 1376264 | tf_op jit(solution)/shard_map/ppermute | solution.py:309
  97.4 3.8 %collective-permute-start.4 = (f32[136,896]{1,0:T(8,128)S(1)}, f32[136,896]{1,0:T(8,128)S(1)}, u32[]{:S(2)}, u32[]{:S(2)}) collective-permute-start(f32[136,896]{1,0:T(8,128)S(1)} %shard_map.64), channel_id=1, source_target_pairs={{0,8},{8,0},{1,9},{9,1},{2,10},{10,2},{3,11},{11,3},{4,12},{12,4},... | collective-permute-start | bytes 1462280 | tf_op jit(solution)/shard_map/ppermute | solution.py:317
  134.3 40.9 %copy-start.3 = (bf16[112,3584]{1,0:T(8,128)(2,1)S(1)}, bf16[112,3584]{1,0:T(8,128)(2,1)}, u32[]{:S(2)}) copy-start(bf16[112,3584]{1,0:T(8,128)(2,1)} %g_ref.3) | copy-start | bytes 2408452
  157.0 18.1 %copy-start.1 = (f32[112,3584]{1,0:T(8,128)S(1)}, f32[112,3584]{1,0:T(8,128)}, u32[]{:S(2)}) copy-start(f32[112,3584]{1,0:T(8,128)} %m_ref.3) | copy-start | bytes 4816900
  157.0 18.1 %collective-permute-start.5 = (f32[4,128,896]{2,1,0:T(8,128)S(1)}, f32[4,128,896]{2,1,0:T(8,128)S(1)}, u32[]{:S(2)}, u32[]{:S(2)}) collective-permute-start(f32[4,128,896]{2,1,0:T(8,128)S(1)} %all_to_all.39.own_ref), channel_id=1, source_target_pairs={{0,8},{8,0},{1,9},{9,1},{2,10},{10,2},{3,11},{11,3},{4,12},{12,4},... | collective-permute-start | bytes 5505032 | tf_op jit(solution)/shard_map/ppermute | solution.py:330

commit v6 on v5

--- a/solution.py
+++ b/solution.py
@@ -40,44 +40,24 @@
     return pl.CostEstimate(flops=flops, bytes_accessed=nbytes, transcendentals=0)
 
 
-def deal_kernel(m_ref, g_ref, *refs):
-    blocks, (m_buf, g_buf, sems) = refs[:NX], refs[NX:]
+def deal_kernel(c_ref, *blocks):
     part = blocks[0].shape[1]
-    loads = []
-    for j in range(NX):
+    for j, ref in enumerate(blocks):
         at = lax.rem(lax.axis_index("x") + j, NX)
-        columns = (slice(None), pl.ds(pl.multiple_of(at * part, 128), part))
-        loads.append(
-            (
-                pltpu.make_async_copy(m_ref.at[columns], m_buf.at[j], sems.at[j, 0]),
-                pltpu.make_async_copy(g_ref.at[columns], g_buf.at[j], sems.at[j, 1]),
-            )
-        )
-    for j in (*range(1, NX), 0):
-        for load in loads[j]:
-            load.start()
-    for j in (*range(1, NX), 0):
-        for load in loads[j]:
-            load.wait()
-        blocks[j][...] = m_buf[j] + g_buf[j].astype(jnp.float32)
-
-
-def deal(momentum, gradient):
-    rows, cols = momentum.shape
+        ref[...] = c_ref[:, pl.ds(pl.multiple_of(at * part, 128), part)]
+
+
+def deal(combined):
+    rows, cols = combined.shape
     part = cols // NX
     return pl.pallas_call(
         deal_kernel,
-        in_specs=[HBM] * 2,
+        in_specs=[VMEM],
         out_specs=[VMEM] * NX,
         out_shape=[jax.ShapeDtypeStruct((rows, part), jnp.float32)] * NX,
-        scratch_shapes=[
-            pltpu.VMEM((NX, rows, part), jnp.float32),
-            pltpu.VMEM((NX, rows, part), jnp.bfloat16),
-            pltpu.SemaphoreType.DMA((NX, 2)),
-        ],
-        compiler_params=PARAMS,
-        cost_estimate=cost(rows * cols, 10 * rows * cols),
-    )(momentum, gradient)
+        compiler_params=PARAMS,
+        cost_estimate=cost(rows * cols, 8 * rows * cols),
+    )(combined)
 
 
 def pieces_kernel(basis_ref, after_ref, pieces_ref):
@@ -122,9 +102,12 @@
     )(*blocks)
 
 
-def panel_kernel(high_ref, low_ref, basis_ref, out_ref):
+def panel_kernel(high_ref, low_ref, basis_ref, out_ref, buf):
     rows = high_ref.shape[0] // NX
-    panel = dot3((high_ref[...], low_ref[...]), split(basis_ref[...]), ((1,), (1,)))
+    n, ranks, _ = basis_ref.shape
+    for i in range(n):
+        buf[i * ranks : (i + 1) * ranks] = basis_ref[i]
+    panel = dot3((high_ref[...], low_ref[...]), split(buf[...]), ((1,), (1,)))
     for j in range(NX):
         at = lax.rem(lax.axis_index("x") + (NX - j), NX)
         out_ref[at, :rows] = panel[j * rows : (j + 1) * rows]
@@ -135,12 +118,13 @@
 
 def panel_part(tall, basis, padded):
     rows, part = tall[0].shape
-    half = basis.shape[0]
+    half = basis.shape[0] * basis.shape[1]
     return pl.pallas_call(
         panel_kernel,
         in_specs=[VMEM] * 3,
         out_specs=VMEM,
         out_shape=jax.ShapeDtypeStruct((NX, padded, half), jnp.float32),
+        scratch_shapes=[pltpu.VMEM((half, part), jnp.float32)],
         compiler_params=PARAMS,
         cost_estimate=cost(6 * rows * part * half, 4 * (rows + half) * part),
     )(*tall, basis)
@@ -298,14 +282,13 @@
     own_ranks = NX * rank_rows
     padded = -(-rows // (8 * NZ)) * 8 * NZ
 
-    blocks = deal(momentum, gradient)
+    blocks = deal(momentum + gradient.astype(jnp.float32))
     pieces = basis_pieces(basis_panel, blocks[0])
     blocks = [blocks[0]] + [
         lax.ppermute(blocks[j], "x", [(i, (i + j) % NX) for i in range(NX)]) for j in range(1, NX)
     ]
     basis_own = exchange(pieces, ("y", "x"))
     basis_own, *tall = lax.optimization_barrier((basis_own, *tall_parts(blocks)))
-    basis_own = basis_own.reshape(half, part)
     basis_oth = lax.ppermute(basis_own, "core", SWAP)
 
     panel = [panel_part(tall, basis, padded) for basis in (basis_own, basis_oth)]

time: 181 us -> 177 us (0.978)
  local copies, waits for them, and re-layouts: 4.03 us -> 2.05 us
    all_to_all x1, waiting for transfers between devices: 9.46 us -> 7.6 us  [exchange(): return lax.all_to_all(blocks, axes, 0, 0, tiled=True)]
where the time goes in v6:
time: 177 us; the launch traced here: 175 us
  blocking collectives  116 us (66%)
  starting transfers between devices  33.7 us (19%)
  waiting for transfers between devices  13.3 us (8%)
  Pallas kernels  7.37 us (4%)
  local copies, waits for them, and re-layouts  2.05 us (1%)
  other arithmetic  1.98 us (1%)
    all_to_all x5, blocking collectives, opposed(): lax.all_to_all(blocks, axes, 0, 0, axis_index_groups=groups, tiled=True)  106 us
    ppermute x3, starting transfers between devices, shards(): lax.ppermute(blocks[j], 'x', [(i, (i + j) % NX) for i in range(NX)])  11.4 us
    all_to_all x1, blocking collectives, exchange(): return lax.all_to_all(blocks, axes, 0, 0, tiled=True)  10.4 us
    all_to_all x1, waiting for transfers between devices, exchange(): return lax.all_to_all(blocks, axes, 0, 0, tiled=True)  7.6 us
    all_to_all x1, starting transfers between devices, exchange(): return lax.all_to_all(blocks, axes, 0, 0, tiled=True)  7.24 us
    ppermute x1, starting transfers between devices, shards(): oth = lax.ppermute(own, 'core', SWAP)  7.24 us
    ppermute x1, starting transfers between devices, shards(): basis_oth = lax.ppermute(basis_own, 'core', SWAP)  5.56 us
    ppermute x3, waiting for transfers between devices, shards(): lax.ppermute(blocks[j], 'x', [(i, (i + j) % NX) for i in range(NX)])  4.27 us
  transfers between devices with their start and end apart: 7, of which 4 were waited for; matrix products, arithmetic and copies ran while one was open for 0% of the time, Pallas kernels for 2%

profile of v6, /device:TPU:1, one launch (start us, length us, event | category | flops | bytes accessed | tf_op | source)
XLA Modules:
  0.0 175.5 jit_solution(17383736060891978243)
XLA Ops:
  0.6 1.8 %convert_add_fusion.c_ref = f32[112,3584]{1,0:T(8,128)S(1)} fusion(f32[112,3584]{1,0:T(8,128)} %m_ref.1, bf16[112,3584]{1,0:T(8,128)(2,1)} %g_ref.1), kind=kLoop, calls=%fused_computation | loop fusion | flops 802816 | bytes 4014080 | tf_op jit(solution)/shard_map/add | solution.py:285
  2.4 0.0 copy-start.4
  2.4 0.1 shard_map.58
  2.5 3.9 %collective-permute-start = (f32[112,896]{1,0:T(8,128)S(1)}, f32[112,896]{1,0:T(8,128)S(1)}, u32[]{:S(2)}, u32[]{:S(2)}) collective-permute-start(f32[112,896]{1,0:T(8,128)S(1)} %get-tuple-element.34), channel_id=1, source_target_pairs={{0,16},{16,32},{32,48},{48,0},{1,17},{17,33},{33,49},{49,1},{2,18}... | collective-permute-start | bytes 1204232 | tf_op jit(solution)/shard_map/ppermute | solution.py:288
  6.5 4.4 %collective-permute-start.1 = (f32[112,896]{1,0:T(8,128)S(1)}, f32[112,896]{1,0:T(8,128)S(1)}, u32[]{:S(2)}, u32[]{:S(2)}) collective-permute-start(f32[112,896]{1,0:T(8,128)S(1)} %get-tuple-element.35), channel_id=1, source_target_pairs={{0,32},{16,48},{32,0},{48,16},{1,33},{17,49},{33,1},{49,17},{2,34}... | collective-permute-start | bytes 1204232 | tf_op jit(solution)/shard_map/ppermute | solution.py:288
  10.9 3.1 %collective-permute-start.2 = (f32[112,896]{1,0:T(8,128)S(1)}, f32[112,896]{1,0:T(8,128)S(1)}, u32[]{:S(2)}, u32[]{:S(2)}) collective-permute-start(f32[112,896]{1,0:T(8,128)S(1)} %get-tuple-element.36), channel_id=1, source_target_pairs={{0,48},{16,0},{32,16},{48,32},{1,49},{17,1},{33,17},{49,33},{2,50}... | collective-permute-start | bytes 1204232 | tf_op jit(solution)/shard_map/ppermute | solution.py:288
  13.9 0.0 copy-done.4
  13.9 0.8 shard_map.59
  14.8 7.2 %all-to-all-start = ((f32[32,4,896]{2,1,0:T(4,128)}), f32[32,4,896]{2,1,0:T(4,128)S(1)}, u32[]{:S(2)}, u32[]{:S(2)}) async-start(f32[32,4,896]{2,1,0:T(4,128)} %shard_map.59), calls=%async_computation | async-start | bytes 917504 | tf_op jit(solution)/shard_map/all_to_all | solution.py:262
  22.0 0.0 collective-permute-done.refs_1_
  22.0 4.3 %collective-permute-done.1.refs_2_ = f32[112,896]{1,0:T(8,128)S(1)} collective-permute-done((f32[112,896]{1,0:T(8,128)S(1)}, f32[112,896]{1,0:T(8,128)S(1)}, u32[]{:S(2)}, u32[]{:S(2)}) %collective-permute-start.1) | collective-permute-done | bytes 401440 | tf_op jit(solution)/shard_map/ppermute | solution.py:288
  26.3 0.0 collective-permute-done.2.refs_3_
  26.3 0.0 copy-start.2
  26.3 0.7 copy-done.2
  27.0 0.0 copy-start.3
  27.0 1.0 copy-done.3
  28.0 0.3 shard_map.60
  28.3 7.6 %all-to-all-done.basis_ref = f32[32,4,896]{2,1,0:T(4,128)S(1)} async-done(((f32[32,4,896]{2,1,0:T(4,128)}), f32[32,4,896]{2,1,0:T(4,128)S(1)}, u32[]{:S(2)}, u32[]{:S(2)}) %all-to-all-start) | async-done | bytes 458784 | tf_op jit(solution)/shard_map/all_to_all | solution.py:262
  35.9 5.6 %collective-permute-start.3 = (f32[32,4,896]{2,1,0:T(4,128)S(1)}, f32[32,4,896]{2,1,0:T(4,128)S(1)}, u32[]{:S(2)}, u32[]{:S(2)}) collective-permute-start(f32[32,4,896]{2,1,0:T(4,128)S(1)} %all-to-all-done.basis_ref), channel_id=1, source_target_pairs={{0,8},{8,0},{1,9},{9,1},{2,10},{10,2},{3,11},{11,3},{4,12},{12,4},... | collective-permute-start | bytes 1376264 | tf_op jit(solution)/shard_map/ppermute | solution.py:292
  41.5 0.8 shard_map.61
  42.3 0.6 collective-permute-done.3.basis_ref
  42.9 0.8 shard_map.62
  43.8 28.3 %all_to_all.35 = f32[32,16,256]{2,1,0:T(8,128)S(1)} all-to-all(f32[32,16,256]{2,1,0:T(8,128)S(1)} %bitcast.7), channel_id=1, replica_groups={{0,1,2,3,4,5,6,7,16,17,18,19,20,21,22,23,32,33,34,35,36,37,38,39,48,49,..., dimensions={0} | all-to-all | bytes 1048576 | tf_op jit(solution)/shard_map/all_to_all | solution.py:270
  72.1 0.1 broadcast_in_dim.6
  72.2 22.1 %all_to_all.36 = f32[32,16,256]{2,1,0:T(8,128)S(1)} all-to-all(f32[32,16,256]{2,1,0:T(8,128)S(1)} %broadcast_in_dim.6), channel_id=1, replica_groups={{0,1,2,3,4,5,6,7,16,17,18,19,20,21,22,23,32,33,34,35,36,37,38,39,48,49,..., dimensions={0} | all-to-all | bytes 1048576 | tf_op jit(solution)/shard_map/all_to_all | solution.py:270
  94.3 0.6 shard_map.64
  94.9 2.3 %collective-permute-start.4 = (f32[136,896]{1,0:T(8,128)S(1)}, f32[136,896]{1,0:T(8,128)S(1)}, u32[]{:S(2)}, u32[]{:S(2)}) collective-permute-start(f32[136,896]{1,0:T(8,128)S(1)} %shard_map.64), channel_id=1, source_target_pairs={{0,8},{8,0},{1,9},{9,1},{2,10},{10,2},{3,11},{11,3},{4,12},{12,4},... | collective-permute-start | bytes 1462280 | tf_op jit(solution)/shard_map/ppermute | solution.py:300
  97.2 0.6 shard_map.63
  97.8 0.8 collective-permute-done.4
  98.7 0.1 add.17
  98.8 14.3 %all_to_all.37 = f32[8,16,896]{2,1,0:T(8,128)S(1)} all-to-all(f32[8,16,896]{2,1,0:T(8,128)S(1)} %bitcast.8), channel_id=1, replica_groups={{0,64,128,192,256,320,384,448},{456,392,328,264,200,136,72,8},{1,65,129..., dimensions={0} | all-to-all | bytes 917504 | tf_op jit(solution)/shard_map/all_to_all | solution.py:270
  113.2 18.7 %all_to_all.38 = f32[8,16,1024]{2,1,0:T(8,128)S(1)} all-to-all(f32[8,16,1024]{2,1,0:T(8,128)S(1)} %broadcast_in_dim.7), channel_id=1, replica_groups={{0,64,128,192,256,320,384,448},{456,392,328,264,200,136,72,8},{1,65,129..., dimensions={0} | all-to-all | bytes 1048576 | tf_op jit(solution)/shard_map/all_to_all | solution.py:270
  132.0 0.1 broadcast_in_dim.8
  132.1 0.0 copy-start.1
  132.1 22.5 %all_to_all.39.own_ref = f32[4,128,896]{2,1,0:T(8,128)S(1)} all-to-all(f32[4,128,896]{2,1,0:T(8,128)S(1)} %broadcast_in_dim.8), channel_id=1, replica_groups={{0,16,32,48},{56,40,24,8},{1,17,33,49},{57,41,25,9},{2,18,34,50},{58,42..., dimensions={0} | all-to-all | bytes 3670016 | tf_op jit(solution)/shard_map/all_to_all | solution.py:270
  154.6 0.0 copy-start
  154.6 7.2 %collective-permute-start.5 = (f32[4,128,896]{2,1,0:T(8,128)S(1)}, f32[4,128,896]{2,1,0:T(8,128)S(1)}, u32[]{:S(2)}, u32[]{:S(2)}) collective-permute-start(f32[4,128,896]{2,1,0:T(8,128)S(1)} %all_to_all.39.own_ref), channel_id=1, source_target_pairs={{0,8},{8,0},{1,9},{9,1},{2,10},{10,2},{3,11},{11,3},{4,12},{12,4},... | collective-permute-start | bytes 5505032 | tf_op jit(solution)/shard_map/ppermute | solution.py:313
  161.8 0.6 shard_map.65
  162.5 10.4 %all_to_all.40.sums_ref = f32[16,8,128]{2,1,0:T(8,128)S(1)} all-to-all(f32[16,8,128]{2,1,0:T(8,128)S(1)} %shard_map.65), channel_id=1, replica_groups=mesh['y'=8,'x'=4,'core'=2,'z'=8] {'core','z'}, dimensions={0} | all-to-all | bytes 131072 | tf_op jit(solution)/shard_map/all_to_all | solution.py:262
  172.8 0.0 collective-permute-done.5.oth_ref
  172.8 0.0 copy-done.1
  172.9 0.0 copy-done
  172.9 2.6 %shard_map.66 = (f32[112,3584]{1,0:T(8,128)}, bf16[112,3584]{1,0:T(8,128)(2,1)}, f32[4,3584]{1,0:T(4,128)}) custom-call(f32[112,256]{1,0:T(8,128)S(1)} %get-tuple-element.42.mine_ref, f32[2,128]{1,0:T(2,128)S(1)} %broadcast_add_fusion.square_ref, f32[16,8,128]{2,1,0:T(8,128)S(1)} %all_to_all.40.sums_ref, f32[112,3584]{1,0:T(8,128)S(1)} %copy-done, ...), custom_call_target="tpu_custom_call" | custom-call | flops 1233125376 | bytes 10092544 | tf_op jit(solution)/shard_map/pallas_call | solution.py:249
  (10 shorter events, 0.2 us)
Async XLA Ops:
  2.4 11.5 %copy-start.4 = (f32[4,3584]{1,0:T(4,128)S(1)}, f32[4,3584]{1,0:T(4,128)}, u32[]{:S(2)}) copy-start(f32[4,3584]{1,0:T(4,128)} %basis_ref.1) | copy-start | bytes 172036
  2.5 19.5 %collective-permute-start = (f32[112,896]{1,0:T(8,128)S(1)}, f32[112,896]{1,0:T(8,128)S(1)}, u32[]{:S(2)}, u32[]{:S(2)}) collective-permute-start(f32[112,896]{1,0:T(8,128)S(1)} %get-tuple-element.34), channel_id=1, source_target_pairs={{0,16},{16,32},{32,48},{48,0},{1,17},{17,33},{33,49},{49,1},{2,18}... | collective-permute-start | bytes 1204232 | tf_op jit(solution)/shard_map/ppermute | solution.py:288
  6.5 19.8 %collective-permute-start.1 = (f32[112,896]{1,0:T(8,128)S(1)}, f32[112,896]{1,0:T(8,128)S(1)}, u32[]{:S(2)}, u32[]{:S(2)}) collective-permute-start(f32[112,896]{1,0:T(8,128)S(1)} %get-tuple-element.35), channel_id=1, source_target_pairs={{0,32},{16,48},{32,0},{48,16},{1,33},{17,49},{33,1},{49,17},{2,34}... | collective-permute-start | bytes 1204232 | tf_op jit(solution)/shard_map/ppermute | solution.py:288
  10.9 15.4 %collective-permute-start.2 = (f32[112,896]{1,0:T(8,128)S(1)}, f32[112,896]{1,0:T(8,128)S(1)}, u32[]{:S(2)}, u32[]{:S(2)}) collective-permute-start(f32[112,896]{1,0:T(8,128)S(1)} %get-tuple-element.36), channel_id=1, source_target_pairs={{0,48},{16,0},{32,16},{48,32},{1,49},{17,1},{33,17},{49,33},{2,50}... | collective-permute-start | bytes 1204232 | tf_op jit(solution)/shard_map/ppermute | solution.py:288
  14.8 21.2 %all-to-all-start = ((f32[32,4,896]{2,1,0:T(4,128)}), f32[32,4,896]{2,1,0:T(4,128)S(1)}, u32[]{:S(2)}, u32[]{:S(2)}) async-start(f32[32,4,896]{2,1,0:T(4,128)} %shard_map.59), calls=%async_computation | async-start | bytes 917504 | tf_op jit(solution)/shard_map/all_to_all | solution.py:262
  26.3 0.7 copy-start.2
  27.0 1.0 copy-start.3
  35.9 7.0 %collective-permute-start.3 = (f32[32,4,896]{2,1,0:T(4,128)S(1)}, f32[32,4,896]{2,1,0:T(4,128)S(1)}, u32[]{:S(2)}, u32[]{:S(2)}) collective-permute-start(f32[32,4,896]{2,1,0:T(4,128)S(1)} %all-to-all-done.basis_ref), channel_id=1, source_target_pairs={{0,8},{8,0},{1,9},{9,1},{2,10},{10,2},{3,11},{11,3},{4,12},{12,4},... | collective-permute-start | bytes 1376264 | tf_op jit(solution)/shard_map/ppermute | solution.py:292
  94.9 3.8 %collective-permute-start.4 = (f32[136,896]{1,0:T(8,128)S(1)}, f32[136,896]{1,0:T(8,128)S(1)}, u32[]{:S(2)}, u32[]{:S(2)}) collective-permute-start(f32[136,896]{1,0:T(8,128)S(1)} %shard_map.64), channel_id=1, source_target_pairs={{0,8},{8,0},{1,9},{9,1},{2,10},{10,2},{3,11},{11,3},{4,12},{12,4},... | collective-permute-start | bytes 1462280 | tf_op jit(solution)/shard_map/ppermute | solution.py:300
  132.1 40.7 %copy-start.1 = (bf16[112,3584]{1,0:T(8,128)(2,1)S(1)}, bf16[112,3584]{1,0:T(8,128)(2,1)}, u32[]{:S(2)}) copy-start(bf16[112,3584]{1,0:T(8,128)(2,1)} %g_ref.1) | copy-start | bytes 2408452
  154.6 18.3 %copy-start = (f32[112,3584]{1,0:T(8,128)S(1)}, f32[112,3584]{1,0:T(8,128)}, u32[]{:S(2)}) copy-start(f32[112,3584]{1,0:T(8,128)} %m_ref.1) | copy-start | bytes 4816900
  154.6 18.3 %collective-permute-start.5 = (f32[4,128,896]{2,1,0:T(8,128)S(1)}, f32[4,128,896]{2,1,0:T(8,128)S(1)}, u32[]{:S(2)}, u32[]{:S(2)}) collective-permute-start(f32[4,128,896]{2,1,0:T(8,128)S(1)} %all_to_all.39.own_ref), channel_id=1, source_target_pairs={{0,8},{8,0},{1,9},{9,1},{2,10},{10,2},{3,11},{11,3},{4,12},{12,4},... | collective-permute-start | bytes 5505032 | tf_op jit(solution)/shard_map/ppermute | solution.py:313

commit v7 on v6

--- a/solution.py
+++ b/solution.py
@@ -40,10 +40,15 @@
     return pl.CostEstimate(flops=flops, bytes_accessed=nbytes, transcendentals=0)
 
 
+def x_away(j):
+    steps = jnp.where(lax.axis_index("core") == 0, j, NX - j)
+    return lax.rem(lax.axis_index("x") + steps, NX)
+
+
 def deal_kernel(c_ref, *blocks):
     part = blocks[0].shape[1]
     for j, ref in enumerate(blocks):
-        at = lax.rem(lax.axis_index("x") + j, NX)
+        at = x_away(j)
         ref[...] = c_ref[:, pl.ds(pl.multiple_of(at * part, 128), part)]
 
 
@@ -63,7 +68,8 @@
 def pieces_kernel(basis_ref, after_ref, pieces_ref):
     part = pieces_ref.shape[2]
     for to in range(NX):
-        piece = basis_ref[:, to * part : (to + 1) * part]
+        at = jnp.where(lax.axis_index("core") == 0, to, NX - 1 - to)
+        piece = basis_ref[:, pl.ds(pl.multiple_of(at * part, 128), part)]
         for y in range(NY):
             pieces_ref[y * NX + to] = piece
 
@@ -109,7 +115,7 @@
         buf[i * ranks : (i + 1) * ranks] = basis_ref[i]
     panel = dot3((high_ref[...], low_ref[...]), split(buf[...]), ((1,), (1,)))
     for j in range(NX):
-        at = lax.rem(lax.axis_index("x") + (NX - j), NX)
+        at = x_away(NX - j)
         out_ref[at, :rows] = panel[j * rows : (j + 1) * rows]
         if out_ref.shape[1] > rows:
             spare = (out_ref.shape[1] - rows, out_ref.shape[2])
@@ -133,7 +139,7 @@
 def right_kernel(side, high_ref, low_ref, panel_ref, out_ref, mine_ref=None):
     rows, half = high_ref.shape[0] // NX, panel_ref.shape[2] // 2
     tall = (high_ref[...], low_ref[...])
-    panel = [panel_ref[lax.rem(lax.axis_index("x") + (NX - j), NX), :rows] for j in range(NX)]
+    panel = [panel_ref[x_away(NX - j), :rows] for j in range(NX)]
     if side == 0:
         mine_ref[...] = panel[0]
     panel = jnp.concatenate(panel, axis=0)
@@ -207,7 +213,8 @@
     u_left = split(panel * row(math.sqrt(ROWS * COLS / RANK) / (square * right_scale)))
     left = jnp.concatenate([*m_left, *u_left], axis=0)
     left_high = jnp.concatenate([m_left[0], u_left[0]], axis=0)
-    first = (lax.axis_index("y") * NX + lax.axis_index("x")) * ranks
+    place = lax.axis_index("y") * NX + lax.axis_index("x")
+    first = jnp.where(core == 0, place, NY * NX - 1 - place) * ranks
     group = pl.multiple_of(first // 8 * 8, 8)
     lane = lax.broadcasted_iota(jnp.int32, (8, half), 1)
     rank = lax.broadcasted_iota(jnp.int32, (8, half), 0) + group
@@ -262,6 +269,11 @@
     return lax.all_to_all(blocks, axes, 0, 0, tiled=True)
 
 
+def turn(j):
+    steps = [(x, core, (x + (j, -j)[core]) % NX) for x in range(NX) for core in range(NC)]
+    return [(x * NC + core, to * NC + core) for x, core, to in steps]
+
+
 def opposed(blocks, axes):
     sizes = {"y": NY, "x": NX, "core": NC, "z": NZ}
     at = np.arange(math.prod(sizes[axis] for axis in axes)).reshape([sizes[axis] for axis in axes])
@@ -285,9 +297,9 @@
     blocks = deal(momentum + gradient.astype(jnp.float32))
     pieces = basis_pieces(basis_panel, blocks[0])
     blocks = [blocks[0]] + [
-        lax.ppermute(blocks[j], "x", [(i, (i + j) % NX) for i in range(NX)]) for j in range(1, NX)
+        lax.ppermute(blocks[j], ("x", "core"), turn(j)) for j in range(1, NX)
     ]
-    basis_own = exchange(pieces, ("y", "x"))
+    basis_own = opposed(pieces, ("y", "x", "core"))
     basis_own, *tall = lax.optimization_barrier((basis_own, *tall_parts(blocks)))
     basis_oth = lax.ppermute(basis_own, "core", SWAP)
 

time: 177 us -> 178 us (level)
    ppermute x3, waiting for transfers between devices: 4.27 us -> 12.3 us  [shards(): lax.ppermute(blocks[j], ('x', 'core'), turn(j))]
    all_to_all x1, waiting for transfers between devices: 7.6 us -> 0.01 us  [opposed(): lax.all_to_all(blocks, axes, 0, 0, axis_index_groups=groups, tiled=True)]
    ppermute x1, starting transfers between devices: 5.56 us -> 1.93 us  [shards(): basis_oth = lax.ppermute(basis_own, 'core', SWAP)]
    all_to_all x1, starting transfers between devices: 7.24 us -> 10.7 us  [opposed(): lax.all_to_all(blocks, axes, 0, 0, axis_index_groups=groups, tiled=True)]
  transfers between devices with their start and end apart: 7 -> 7, of which waited for: 4 -> 3; matrix products, arithmetic and copies ran while one was open for 0% -> 0% of each run, Pallas kernels for 2% -> 2%
where the time goes in v7:
time: 178 us; the launch traced here: 175 us
  blocking collectives  116 us (65%)
  starting transfers between devices  32.6 us (18%)
  waiting for transfers between devices  14 us (8%)
  Pallas kernels  7.39 us (4%)
  local copies, waits for them, and re-layouts  2.05 us (1%)
  other arithmetic  1.98 us (1%)
    all_to_all x5, blocking collectives, opposed(): lax.all_to_all(blocks, axes, 0, 0, axis_index_groups=groups, tiled=True)  106 us
    ppermute x3, waiting for transfers between devices, shards(): lax.ppermute(blocks[j], ('x', 'core'), turn(j))  12.3 us
    all_to_all x1, blocking collectives, exchange(): return lax.all_to_all(blocks, axes, 0, 0, tiled=True)  10.8 us
    all_to_all x1, starting transfers between devices, opposed(): lax.all_to_all(blocks, axes, 0, 0, axis_index_groups=groups, tiled=True)  10.7 us
    ppermute x3, starting transfers between devices, shards(): lax.ppermute(blocks[j], ('x', 'core'), turn(j))  10.2 us
    ppermute x1, starting transfers between devices, shards(): oth = lax.ppermute(own, 'core', SWAP)  7.2 us
  transfers between devices with their start and end apart: 7, of which 3 were waited for; matrix products, arithmetic and copies ran while one was open for 0% of the time, Pallas kernels for 2%

profile of v7, /device:TPU:1, one launch (start us, length us, event | category | flops | bytes accessed | tf_op | source)
XLA Modules:
  0.0 175.3 jit_solution(6058057207379059341)
XLA Ops:
  0.6 1.8 %convert_add_fusion.c_ref = f32[112,3584]{1,0:T(8,128)S(1)} fusion(f32[112,3584]{1,0:T(8,128)} %m_ref.1, bf16[112,3584]{1,0:T(8,128)(2,1)} %g_ref.1), kind=kLoop, calls=%fused_computation | loop fusion | flops 802816 | bytes 4014080 | tf_op jit(solution)/shard_map/add | solution.py:297
  2.4 0.0 copy-start.4
  2.4 0.1 shard_map.58
  2.5 5.2 %collective-permute-start = (f32[112,896]{1,0:T(8,128)S(1)}, f32[112,896]{1,0:T(8,128)S(1)}, u32[]{:S(2)}, u32[]{:S(2)}) collective-permute-start(f32[112,896]{1,0:T(8,128)S(1)} %get-tuple-element.34), channel_id=1, source_target_pairs={{0,16},{8,56},{16,32},{24,8},{32,48},{40,24},{48,0},{56,40},{1,17}... | collective-permute-start | bytes 1204232 | tf_op jit(solution)/shard_map/ppermute | solution.py:300
  7.8 2.4 %collective-permute-start.1 = (f32[112,896]{1,0:T(8,128)S(1)}, f32[112,896]{1,0:T(8,128)S(1)}, u32[]{:S(2)}, u32[]{:S(2)}) collective-permute-start(f32[112,896]{1,0:T(8,128)S(1)} %get-tuple-element.35), channel_id=1, source_target_pairs={{0,32},{8,40},{16,48},{24,56},{32,0},{40,8},{48,16},{56,24},{1,33}... | collective-permute-start | bytes 1204232 | tf_op jit(solution)/shard_map/ppermute | solution.py:300
  10.2 2.5 %collective-permute-start.2 = (f32[112,896]{1,0:T(8,128)S(1)}, f32[112,896]{1,0:T(8,128)S(1)}, u32[]{:S(2)}, u32[]{:S(2)}) collective-permute-start(f32[112,896]{1,0:T(8,128)S(1)} %get-tuple-element.36), channel_id=1, source_target_pairs={{0,48},{8,24},{16,0},{24,40},{32,16},{40,56},{48,32},{56,8},{1,49}... | collective-permute-start | bytes 1204232 | tf_op jit(solution)/shard_map/ppermute | solution.py:300
  12.7 0.0 copy-done.4
  12.7 0.8 shard_map.59
  13.6 10.7 %all-to-all-start = ((f32[32,4,896]{2,1,0:T(4,128)}), f32[32,4,896]{2,1,0:T(4,128)S(1)}, u32[]{:S(2)}, u32[]{:S(2)}) async-start(f32[32,4,896]{2,1,0:T(4,128)} %shard_map.59), calls=%async_computation | async-start | bytes 917504 | tf_op jit(solution)/shard_map/all_to_all | solution.py:282
  24.3 0.0 collective-permute-done.refs_1_
  24.3 0.0 collective-permute-done.1.refs_2_
  24.3 12.3 %collective-permute-done.2.refs_3_ = f32[112,896]{1,0:T(8,128)S(1)} collective-permute-done((f32[112,896]{1,0:T(8,128)S(1)}, f32[112,896]{1,0:T(8,128)S(1)}, u32[]{:S(2)}, u32[]{:S(2)}) %collective-permute-start.2) | collective-permute-done | bytes 401440 | tf_op jit(solution)/shard_map/ppermute | solution.py:300
  36.5 0.0 copy-start.2
  36.5 0.7 copy-done.2
  37.3 0.0 copy-start.3
  37.3 1.0 copy-done.3
  38.3 0.3 shard_map.60
  38.6 0.0 all-to-all-done.basis_ref
  38.6 1.9 %collective-permute-start.3 = (f32[32,4,896]{2,1,0:T(4,128)S(1)}, f32[32,4,896]{2,1,0:T(4,128)S(1)}, u32[]{:S(2)}, u32[]{:S(2)}) collective-permute-start(f32[32,4,896]{2,1,0:T(4,128)S(1)} %all-to-all-done.basis_ref), channel_id=1, source_target_pairs={{0,8},{8,0},{1,9},{9,1},{2,10},{10,2},{3,11},{11,3},{4,12},{12,4},... | collective-permute-start | bytes 1376264 | tf_op jit(solution)/shard_map/ppermute | solution.py:304
  40.5 0.8 shard_map.61
  41.4 0.9 collective-permute-done.3.basis_ref
  42.3 0.8 shard_map.62
  43.2 27.8 %all_to_all.35 = f32[32,16,256]{2,1,0:T(8,128)S(1)} all-to-all(f32[32,16,256]{2,1,0:T(8,128)S(1)} %bitcast.7), channel_id=1, replica_groups={{0,1,2,3,4,5,6,7,16,17,18,19,20,21,22,23,32,33,34,35,36,37,38,39,48,49,..., dimensions={0} | all-to-all | bytes 1048576 | tf_op jit(solution)/shard_map/all_to_all | solution.py:282
  71.1 0.1 broadcast_in_dim.6
  71.1 22.0 %all_to_all.36 = f32[32,16,256]{2,1,0:T(8,128)S(1)} all-to-all(f32[32,16,256]{2,1,0:T(8,128)S(1)} %broadcast_in_dim.6), channel_id=1, replica_groups={{0,1,2,3,4,5,6,7,16,17,18,19,20,21,22,23,32,33,34,35,36,37,38,39,48,49,..., dimensions={0} | all-to-all | bytes 1048576 | tf_op jit(solution)/shard_map/all_to_all | solution.py:282
  93.1 0.6 shard_map.64
  93.7 2.6 %collective-permute-start.4 = (f32[136,896]{1,0:T(8,128)S(1)}, f32[136,896]{1,0:T(8,128)S(1)}, u32[]{:S(2)}, u32[]{:S(2)}) collective-permute-start(f32[136,896]{1,0:T(8,128)S(1)} %shard_map.64), channel_id=1, source_target_pairs={{0,8},{8,0},{1,9},{9,1},{2,10},{10,2},{3,11},{11,3},{4,12},{12,4},... | collective-permute-start | bytes 1462280 | tf_op jit(solution)/shard_map/ppermute | solution.py:312
  96.4 0.6 shard_map.63
  97.0 0.8 collective-permute-done.4
  97.8 0.1 add.17
  98.0 15.5 %all_to_all.37 = f32[8,16,896]{2,1,0:T(8,128)S(1)} all-to-all(f32[8,16,896]{2,1,0:T(8,128)S(1)} %bitcast.8), channel_id=1, replica_groups={{0,64,128,192,256,320,384,448},{456,392,328,264,200,136,72,8},{1,65,129..., dimensions={0} | all-to-all | bytes 917504 | tf_op jit(solution)/shard_map/all_to_all | solution.py:282
  113.5 18.3 %all_to_all.38 = f32[8,16,1024]{2,1,0:T(8,128)S(1)} all-to-all(f32[8,16,1024]{2,1,0:T(8,128)S(1)} %broadcast_in_dim.7), channel_id=1, replica_groups={{0,64,128,192,256,320,384,448},{456,392,328,264,200,136,72,8},{1,65,129..., dimensions={0} | all-to-all | bytes 1048576 | tf_op jit(solution)/shard_map/all_to_all | solution.py:282
  131.8 0.1 broadcast_in_dim.8
  132.0 0.0 copy-start.1
  132.0 22.1 %all_to_all.39.own_ref = f32[4,128,896]{2,1,0:T(8,128)S(1)} all-to-all(f32[4,128,896]{2,1,0:T(8,128)S(1)} %broadcast_in_dim.8), channel_id=1, replica_groups={{0,16,32,48},{56,40,24,8},{1,17,33,49},{57,41,25,9},{2,18,34,50},{58,42..., dimensions={0} | all-to-all | bytes 3670016 | tf_op jit(solution)/shard_map/all_to_all | solution.py:282
  154.1 0.0 copy-start
  154.1 7.2 %collective-permute-start.5 = (f32[4,128,896]{2,1,0:T(8,128)S(1)}, f32[4,128,896]{2,1,0:T(8,128)S(1)}, u32[]{:S(2)}, u32[]{:S(2)}) collective-permute-start(f32[4,128,896]{2,1,0:T(8,128)S(1)} %all_to_all.39.own_ref), channel_id=1, source_target_pairs={{0,8},{8,0},{1,9},{9,1},{2,10},{10,2},{3,11},{11,3},{4,12},{12,4},... | collective-permute-start | bytes 5505032 | tf_op jit(solution)/shard_map/ppermute | solution.py:325
  161.3 0.6 shard_map.65
  161.9 10.8 %all_to_all.40.sums_ref = f32[16,8,128]{2,1,0:T(8,128)S(1)} all-to-all(f32[16,8,128]{2,1,0:T(8,128)S(1)} %shard_map.65), channel_id=1, replica_groups=mesh['y'=8,'x'=4,'core'=2,'z'=8] {'core','z'}, dimensions={0} | all-to-all | bytes 131072 | tf_op jit(solution)/shard_map/all_to_all | solution.py:269
  172.7 0.0 collective-permute-done.5.oth_ref
  172.7 0.0 copy-done.1
  172.7 0.0 copy-done
  172.7 2.6 %shard_map.66 = (f32[112,3584]{1,0:T(8,128)}, bf16[112,3584]{1,0:T(8,128)(2,1)}, f32[4,3584]{1,0:T(4,128)}) custom-call(f32[112,256]{1,0:T(8,128)S(1)} %get-tuple-element.42.mine_ref, f32[2,128]{1,0:T(2,128)S(1)} %broadcast_add_fusion.square_ref, f32[16,8,128]{2,1,0:T(8,128)S(1)} %all_to_all.40.sums_ref, f32[112,3584]{1,0:T(8,128)S(1)} %copy-done, ...), custom_call_target="tpu_custom_call" | custom-call | flops 1233125376 | bytes 10092544 | tf_op jit(solution)/shard_map/pallas_call | solution.py:256
  (10 shorter events, 0.2 us)
Async XLA Ops:
  2.4 10.3 %copy-start.4 = (f32[4,3584]{1,0:T(4,128)S(1)}, f32[4,3584]{1,0:T(4,128)}, u32[]{:S(2)}) copy-start(f32[4,3584]{1,0:T(4,128)} %basis_ref.1) | copy-start | bytes 172036
  2.5 21.7 %collective-permute-start = (f32[112,896]{1,0:T(8,128)S(1)}, f32[112,896]{1,0:T(8,128)S(1)}, u32[]{:S(2)}, u32[]{:S(2)}) collective-permute-start(f32[112,896]{1,0:T(8,128)S(1)} %get-tuple-element.34), channel_id=1, source_target_pairs={{0,16},{8,56},{16,32},{24,8},{32,48},{40,24},{48,0},{56,40},{1,17}... | collective-permute-start | bytes 1204232 | tf_op jit(solution)/shard_map/ppermute | solution.py:300
  7.8 16.5 %collective-permute-start.1 = (f32[112,896]{1,0:T(8,128)S(1)}, f32[112,896]{1,0:T(8,128)S(1)}, u32[]{:S(2)}, u32[]{:S(2)}) collective-permute-start(f32[112,896]{1,0:T(8,128)S(1)} %get-tuple-element.35), channel_id=1, source_target_pairs={{0,32},{8,40},{16,48},{24,56},{32,0},{40,8},{48,16},{56,24},{1,33}... | collective-permute-start | bytes 1204232 | tf_op jit(solution)/shard_map/ppermute | solution.py:300
  10.2 26.3 %collective-permute-start.2 = (f32[112,896]{1,0:T(8,128)S(1)}, f32[112,896]{1,0:T(8,128)S(1)}, u32[]{:S(2)}, u32[]{:S(2)}) collective-permute-start(f32[112,896]{1,0:T(8,128)S(1)} %get-tuple-element.36), channel_id=1, source_target_pairs={{0,48},{8,24},{16,0},{24,40},{32,16},{40,56},{48,32},{56,8},{1,49}... | collective-permute-start | bytes 1204232 | tf_op jit(solution)/shard_map/ppermute | solution.py:300
  13.6 25.0 %all-to-all-start = ((f32[32,4,896]{2,1,0:T(4,128)}), f32[32,4,896]{2,1,0:T(4,128)S(1)}, u32[]{:S(2)}, u32[]{:S(2)}) async-start(f32[32,4,896]{2,1,0:T(4,128)} %shard_map.59), calls=%async_computation | async-start | bytes 917504 | tf_op jit(solution)/shard_map/all_to_all | solution.py:282
  36.5 0.7 copy-start.2
  37.3 1.0 copy-start.3
  38.6 3.7 %collective-permute-start.3 = (f32[32,4,896]{2,1,0:T(4,128)S(1)}, f32[32,4,896]{2,1,0:T(4,128)S(1)}, u32[]{:S(2)}, u32[]{:S(2)}) collective-permute-start(f32[32,4,896]{2,1,0:T(4,128)S(1)} %all-to-all-done.basis_ref), channel_id=1, source_target_pairs={{0,8},{8,0},{1,9},{9,1},{2,10},{10,2},{3,11},{11,3},{4,12},{12,4},... | collective-permute-start | bytes 1376264 | tf_op jit(solution)/shard_map/ppermute | solution.py:304
  93.7 4.1 %collective-permute-start.4 = (f32[136,896]{1,0:T(8,128)S(1)}, f32[136,896]{1,0:T(8,128)S(1)}, u32[]{:S(2)}, u32[]{:S(2)}) collective-permute-start(f32[136,896]{1,0:T(8,128)S(1)} %shard_map.64), channel_id=1, source_target_pairs={{0,8},{8,0},{1,9},{9,1},{2,10},{10,2},{3,11},{11,3},{4,12},{12,4},... | collective-permute-start | bytes 1462280 | tf_op jit(solution)/shard_map/ppermute | solution.py:312
  132.0 40.7 %copy-start.1 = (bf16[112,3584]{1,0:T(8,128)(2,1)S(1)}, bf16[112,3584]{1,0:T(8,128)(2,1)}, u32[]{:S(2)}) copy-start(bf16[112,3584]{1,0:T(8,128)(2,1)} %g_ref.1) | copy-start | bytes 2408452
  154.1 18.6 %copy-start = (f32[112,3584]{1,0:T(8,128)S(1)}, f32[112,3584]{1,0:T(8,128)}, u32[]{:S(2)}) copy-start(f32[112,3584]{1,0:T(8,128)} %m_ref.1) | copy-start | bytes 4816900
  154.1 18.6 %collective-permute-start.5 = (f32[4,128,896]{2,1,0:T(8,128)S(1)}, f32[4,128,896]{2,1,0:T(8,128)S(1)}, u32[]{:S(2)}, u32[]{:S(2)}) collective-permute-start(f32[4,128,896]{2,1,0:T(8,128)S(1)} %all_to_all.39.own_ref), channel_id=1, source_target_pairs={{0,8},{8,0},{1,9},{9,1},{2,10},{10,2},{3,11},{11,3},{4,12},{12,4},... | collective-permute-start | bytes 5505032 | tf_op jit(solution)/shard_map/ppermute | solution.py:325

commit v8 on v7

--- a/solution.py
+++ b/solution.py
@@ -83,7 +83,7 @@
         out_specs=VMEM,
         out_shape=jax.ShapeDtypeStruct(pieces, jnp.float32),
         compiler_params=PARAMS,
-        cost_estimate=cost(10**10, 10**8),
+        cost_estimate=cost(basis.size, 4 * NY * basis.size),
     )(basis, after)
 
 
@@ -300,7 +300,7 @@
         lax.ppermute(blocks[j], ("x", "core"), turn(j)) for j in range(1, NX)
     ]
     basis_own = opposed(pieces, ("y", "x", "core"))
-    basis_own, *tall = lax.optimization_barrier((basis_own, *tall_parts(blocks)))
+    tall = tall_parts(blocks)
     basis_oth = lax.ppermute(basis_own, "core", SWAP)
 
     panel = [panel_part(tall, basis, padded) for basis in (basis_own, basis_oth)]

time: 178 us -> 181 us (1.017)
  starting transfers between devices: 32.6 us -> 34.7 us
  blocking collectives: 116 us -> 118 us
    ppermute x1, starting transfers between devices: 1.93 us -> 5.61 us  [shards(): basis_oth = lax.ppermute(basis_own, 'core', SWAP)]
    all_to_all x1, waiting for transfers between devices: 0.01 us -> 2.56 us  [opposed(): lax.all_to_all(blocks, axes, 0, 0, axis_index_groups=groups, tiled=True)]
    ppermute x3, waiting for transfers between devices: 12.3 us -> 9.73 us  [shards(): lax.ppermute(blocks[j], ('x', 'core'), turn(j))]
    ppermute x3, starting transfers between devices: 10.2 us -> 8.1 us  [shards(): lax.ppermute(blocks[j], ('x', 'core'), turn(j))]
  transfers between devices with their start and end apart: 7 -> 7, of which waited for: 3 -> 4; matrix products, arithmetic and copies ran while one was open for 0% -> 0% of each run, Pallas kernels for 2% -> 1%
where the time goes in v8:
time: 181 us; the launch traced here: 179 us
  blocking collectives  118 us (65%)
  starting transfers between devices  34.7 us (19%)
  waiting for transfers between devices  13.1 us (7%)
  Pallas kernels  7.37 us (4%)
  local copies, waits for them, and re-layouts  2.72 us (2%)
  other arithmetic  1.98 us (1%)
    all_to_all x5, blocking collectives, opposed(): lax.all_to_all(blocks, axes, 0, 0, axis_index_groups=groups, tiled=True)  107 us
    all_to_all x1, blocking collectives, exchange(): return lax.all_to_all(blocks, axes, 0, 0, tiled=True)  11.4 us
    all_to_all x1, starting transfers between devices, opposed(): lax.all_to_all(blocks, axes, 0, 0, axis_index_groups=groups, tiled=True)  11.2 us
    ppermute x3, waiting for transfers between devices, shards(): lax.ppermute(blocks[j], ('x', 'core'), turn(j))  9.73 us
    ppermute x3, starting transfers between devices, shards(): lax.ppermute(blocks[j], ('x', 'core'), turn(j))  8.1 us
    ppermute x1, starting transfers between devices, shards(): oth = lax.ppermute(own, 'core', SWAP)  7.24 us
    ppermute x1, starting transfers between devices, shards(): basis_oth = lax.ppermute(basis_own, 'core', SWAP)  5.61 us
  transfers between devices with their start and end apart: 7, of which 4 were waited for; matrix products, arithmetic and copies ran while one was open for 0% of the time, Pallas kernels for 1%

profile of v8, /device:TPU:1, one launch (start us, length us, event | category | flops | bytes accessed | tf_op | source)
XLA Modules:
  0.0 178.7 jit_solution(391425443299452957)
XLA Ops:
  0.6 1.8 convert_add_fusion.c_ref
  2.4 0.0 copy-start.2
  2.4 0.1 shard_map.58
  2.5 0.7 copy-done.2
  3.2 0.8 shard_map.60
  4.0 11.2 %all-to-all-start = ((f32[32,4,896]{2,1,0:T(4,128)}), f32[32,4,896]{2,1,0:T(4,128)S(1)}, u32[]{:S(2)}, u32[]{:S(2)}) async-start(f32[32,4,896]{2,1,0:T(4,128)} %shard_map.60), calls=%async_computation | async-start | bytes 917504 | tf_op jit(solution)/shard_map/all_to_all | solution.py:282
  15.3 2.2 %collective-permute-start = (f32[112,896]{1,0:T(8,128)S(1)}, f32[112,896]{1,0:T(8,128)S(1)}, u32[]{:S(2)}, u32[]{:S(2)}) collective-permute-start(f32[112,896]{1,0:T(8,128)S(1)} %get-tuple-element.31), channel_id=1, source_target_pairs={{0,16},{8,56},{16,32},{24,8},{32,48},{40,24},{48,0},{56,40},{1,17}... | collective-permute-start | bytes 1204232 | tf_op jit(solution)/shard_map/ppermute | solution.py:300
  17.4 4.0 %collective-permute-start.1 = (f32[112,896]{1,0:T(8,128)S(1)}, f32[112,896]{1,0:T(8,128)S(1)}, u32[]{:S(2)}, u32[]{:S(2)}) collective-permute-start(f32[112,896]{1,0:T(8,128)S(1)} %get-tuple-element.32), channel_id=1, source_target_pairs={{0,32},{8,40},{16,48},{24,56},{32,0},{40,8},{48,16},{56,24},{1,33}... | collective-permute-start | bytes 1204232 | tf_op jit(solution)/shard_map/ppermute | solution.py:300
  21.4 1.9 %collective-permute-start.2 = (f32[112,896]{1,0:T(8,128)S(1)}, f32[112,896]{1,0:T(8,128)S(1)}, u32[]{:S(2)}, u32[]{:S(2)}) collective-permute-start(f32[112,896]{1,0:T(8,128)S(1)} %get-tuple-element.33), channel_id=1, source_target_pairs={{0,48},{8,24},{16,0},{24,40},{32,16},{40,56},{48,32},{56,8},{1,49}... | collective-permute-start | bytes 1204232 | tf_op jit(solution)/shard_map/ppermute | solution.py:300
  23.4 2.6 %all-to-all-done.basis_ref = f32[32,4,896]{2,1,0:T(4,128)S(1)} async-done(((f32[32,4,896]{2,1,0:T(4,128)}), f32[32,4,896]{2,1,0:T(4,128)S(1)}, u32[]{:S(2)}, u32[]{:S(2)}) %all-to-all-start) | async-done | bytes 458784 | tf_op jit(solution)/shard_map/all_to_all | solution.py:282
  25.9 5.6 %collective-permute-start.3 = (f32[32,4,896]{2,1,0:T(4,128)S(1)}, f32[32,4,896]{2,1,0:T(4,128)S(1)}, u32[]{:S(2)}, u32[]{:S(2)}) collective-permute-start(f32[32,4,896]{2,1,0:T(4,128)S(1)} %all-to-all-done.basis_ref), channel_id=1, source_target_pairs={{0,8},{8,0},{1,9},{9,1},{2,10},{10,2},{3,11},{11,3},{4,12},{12,4},... | collective-permute-start | bytes 1376264 | tf_op jit(solution)/shard_map/ppermute | solution.py:304
  31.6 0.0 collective-permute-done.refs_1_
  31.6 2.7 %collective-permute-done.1.refs_2_ = f32[112,896]{1,0:T(8,128)S(1)} collective-permute-done((f32[112,896]{1,0:T(8,128)S(1)}, f32[112,896]{1,0:T(8,128)S(1)}, u32[]{:S(2)}, u32[]{:S(2)}) %collective-permute-start.1) | collective-permute-done | bytes 401440 | tf_op jit(solution)/shard_map/ppermute | solution.py:300
  34.2 7.1 %collective-permute-done.2.refs_3_ = f32[112,896]{1,0:T(8,128)S(1)} collective-permute-done((f32[112,896]{1,0:T(8,128)S(1)}, f32[112,896]{1,0:T(8,128)S(1)}, u32[]{:S(2)}, u32[]{:S(2)}) %collective-permute-start.2) | collective-permute-done | bytes 401440 | tf_op jit(solution)/shard_map/ppermute | solution.py:300
  41.3 0.0 copy-start.3
  41.3 0.7 copy-done.3
  42.0 0.0 copy-start.4
  42.0 1.0 copy-done.4
  43.0 0.3 shard_map.59
  43.3 0.8 shard_map.61
  44.2 0.0 collective-permute-done.3.basis_ref
  44.2 0.8 shard_map.62
  45.1 28.0 %all_to_all.35 = f32[32,16,256]{2,1,0:T(8,128)S(1)} all-to-all(f32[32,16,256]{2,1,0:T(8,128)S(1)} %bitcast.7), channel_id=1, replica_groups={{0,1,2,3,4,5,6,7,16,17,18,19,20,21,22,23,32,33,34,35,36,37,38,39,48,49,..., dimensions={0} | all-to-all | bytes 1048576 | tf_op jit(solution)/shard_map/all_to_all | solution.py:282
  73.2 0.1 broadcast_in_dim.6
  73.2 22.0 %all_to_all.36 = f32[32,16,256]{2,1,0:T(8,128)S(1)} all-to-all(f32[32,16,256]{2,1,0:T(8,128)S(1)} %broadcast_in_dim.6), channel_id=1, replica_groups={{0,1,2,3,4,5,6,7,16,17,18,19,20,21,22,23,32,33,34,35,36,37,38,39,48,49,..., dimensions={0} | all-to-all | bytes 1048576 | tf_op jit(solution)/shard_map/all_to_all | solution.py:282
  95.3 0.6 shard_map.64
  95.9 2.5 %collective-permute-start.4 = (f32[136,896]{1,0:T(8,128)S(1)}, f32[136,896]{1,0:T(8,128)S(1)}, u32[]{:S(2)}, u32[]{:S(2)}) collective-permute-start(f32[136,896]{1,0:T(8,128)S(1)} %shard_map.64), channel_id=1, source_target_pairs={{0,8},{8,0},{1,9},{9,1},{2,10},{10,2},{3,11},{11,3},{4,12},{12,4},... | collective-permute-start | bytes 1462280 | tf_op jit(solution)/shard_map/ppermute | solution.py:312
  98.4 0.6 shard_map.63
  99.1 0.8 collective-permute-done.4
  99.9 0.1 add.17
  100.0 16.8 %all_to_all.37 = f32[8,16,896]{2,1,0:T(8,128)S(1)} all-to-all(f32[8,16,896]{2,1,0:T(8,128)S(1)} %bitcast.8), channel_id=1, replica_groups={{0,64,128,192,256,320,384,448},{456,392,328,264,200,136,72,8},{1,65,129..., dimensions={0} | all-to-all | bytes 917504 | tf_op jit(solution)/shard_map/all_to_all | solution.py:282
  117.0 18.3 %all_to_all.38 = f32[8,16,1024]{2,1,0:T(8,128)S(1)} all-to-all(f32[8,16,1024]{2,1,0:T(8,128)S(1)} %broadcast_in_dim.7), channel_id=1, replica_groups={{0,64,128,192,256,320,384,448},{456,392,328,264,200,136,72,8},{1,65,129..., dimensions={0} | all-to-all | bytes 1048576 | tf_op jit(solution)/shard_map/all_to_all | solution.py:282
  135.3 0.1 broadcast_in_dim.8
  135.4 0.0 copy-start.1
  135.4 21.4 %all_to_all.39.own_ref = f32[4,128,896]{2,1,0:T(8,128)S(1)} all-to-all(f32[4,128,896]{2,1,0:T(8,128)S(1)} %broadcast_in_dim.8), channel_id=1, replica_groups={{0,16,32,48},{56,40,24,8},{1,17,33,49},{57,41,25,9},{2,18,34,50},{58,42..., dimensions={0} | all-to-all | bytes 3670016 | tf_op jit(solution)/shard_map/all_to_all | solution.py:282
  156.8 0.0 copy-start
  156.8 7.2 %collective-permute-start.5 = (f32[4,128,896]{2,1,0:T(8,128)S(1)}, f32[4,128,896]{2,1,0:T(8,128)S(1)}, u32[]{:S(2)}, u32[]{:S(2)}) collective-permute-start(f32[4,128,896]{2,1,0:T(8,128)S(1)} %all_to_all.39.own_ref), channel_id=1, source_target_pairs={{0,8},{8,0},{1,9},{9,1},{2,10},{10,2},{3,11},{11,3},{4,12},{12,4},... | collective-permute-start | bytes 5505032 | tf_op jit(solution)/shard_map/ppermute | solution.py:325
  164.0 0.6 shard_map.65
  164.7 11.4 %all_to_all.40.sums_ref = f32[16,8,128]{2,1,0:T(8,128)S(1)} all-to-all(f32[16,8,128]{2,1,0:T(8,128)S(1)} %shard_map.65), channel_id=1, replica_groups=mesh['y'=8,'x'=4,'core'=2,'z'=8] {'core','z'}, dimensions={0} | all-to-all | bytes 131072 | tf_op jit(solution)/shard_map/all_to_all | solution.py:269
  176.0 0.0 collective-permute-done.5.oth_ref
  176.1 0.0 copy-done.1
  176.1 0.0 copy-done
  176.1 2.6 %shard_map.66 = (f32[112,3584]{1,0:T(8,128)}, bf16[112,3584]{1,0:T(8,128)(2,1)}, f32[4,3584]{1,0:T(4,128)}) custom-call(f32[112,256]{1,0:T(8,128)S(1)} %get-tuple-element.36.mine_ref, f32[2,128]{1,0:T(2,128)S(1)} %broadcast_add_fusion.square_ref, f32[16,8,128]{2,1,0:T(8,128)S(1)} %all_to_all.40.sums_ref, f32[112,3584]{1,0:T(8,128)S(1)} %copy-done, ...), custom_call_target="tpu_custom_call" | custom-call | flops 1233125376 | bytes 10092544 | tf_op jit(solution)/shard_map/pallas_call | solution.py:256
  (10 shorter events, 0.2 us)
Async XLA Ops:
  2.4 0.8 copy-start.2
  4.0 21.9 %all-to-all-start = ((f32[32,4,896]{2,1,0:T(4,128)}), f32[32,4,896]{2,1,0:T(4,128)S(1)}, u32[]{:S(2)}, u32[]{:S(2)}) async-start(f32[32,4,896]{2,1,0:T(4,128)} %shard_map.60), calls=%async_computation | async-start | bytes 917504 | tf_op jit(solution)/shard_map/all_to_all | solution.py:282
  15.3 16.3 %collective-permute-start = (f32[112,896]{1,0:T(8,128)S(1)}, f32[112,896]{1,0:T(8,128)S(1)}, u32[]{:S(2)}, u32[]{:S(2)}) collective-permute-start(f32[112,896]{1,0:T(8,128)S(1)} %get-tuple-element.31), channel_id=1, source_target_pairs={{0,16},{8,56},{16,32},{24,8},{32,48},{40,24},{48,0},{56,40},{1,17}... | collective-permute-start | bytes 1204232 | tf_op jit(solution)/shard_map/ppermute | solution.py:300
  17.4 16.8 %collective-permute-start.1 = (f32[112,896]{1,0:T(8,128)S(1)}, f32[112,896]{1,0:T(8,128)S(1)}, u32[]{:S(2)}, u32[]{:S(2)}) collective-permute-start(f32[112,896]{1,0:T(8,128)S(1)} %get-tuple-element.32), channel_id=1, source_target_pairs={{0,32},{8,40},{16,48},{24,56},{32,0},{40,8},{48,16},{56,24},{1,33}... | collective-permute-start | bytes 1204232 | tf_op jit(solution)/shard_map/ppermute | solution.py:300
  21.4 19.8 %collective-permute-start.2 = (f32[112,896]{1,0:T(8,128)S(1)}, f32[112,896]{1,0:T(8,128)S(1)}, u32[]{:S(2)}, u32[]{:S(2)}) collective-permute-start(f32[112,896]{1,0:T(8,128)S(1)} %get-tuple-element.33), channel_id=1, source_target_pairs={{0,48},{8,24},{16,0},{24,40},{32,16},{40,56},{48,32},{56,8},{1,49}... | collective-permute-start | bytes 1204232 | tf_op jit(solution)/shard_map/ppermute | solution.py:300
  25.9 18.2 %collective-permute-start.3 = (f32[32,4,896]{2,1,0:T(4,128)S(1)}, f32[32,4,896]{2,1,0:T(4,128)S(1)}, u32[]{:S(2)}, u32[]{:S(2)}) collective-permute-start(f32[32,4,896]{2,1,0:T(4,128)S(1)} %all-to-all-done.basis_ref), channel_id=1, source_target_pairs={{0,8},{8,0},{1,9},{9,1},{2,10},{10,2},{3,11},{11,3},{4,12},{12,4},... | collective-permute-start | bytes 1376264 | tf_op jit(solution)/shard_map/ppermute | solution.py:304
  41.3 0.7 copy-start.3
  42.0 1.0 copy-start.4
  95.9 4.0 %collective-permute-start.4 = (f32[136,896]{1,0:T(8,128)S(1)}, f32[136,896]{1,0:T(8,128)S(1)}, u32[]{:S(2)}, u32[]{:S(2)}) collective-permute-start(f32[136,896]{1,0:T(8,128)S(1)} %shard_map.64), channel_id=1, source_target_pairs={{0,8},{8,0},{1,9},{9,1},{2,10},{10,2},{3,11},{11,3},{4,12},{12,4},... | collective-permute-start | bytes 1462280 | tf_op jit(solution)/shard_map/ppermute | solution.py:312
  135.4 40.6 %copy-start.1 = (bf16[112,3584]{1,0:T(8,128)(2,1)S(1)}, bf16[112,3584]{1,0:T(8,128)(2,1)}, u32[]{:S(2)}) copy-start(bf16[112,3584]{1,0:T(8,128)(2,1)} %g_ref.1) | copy-start | bytes 2408452
  156.8 19.3 %copy-start = (f32[112,3584]{1,0:T(8,128)S(1)}, f32[112,3584]{1,0:T(8,128)}, u32[]{:S(2)}) copy-start(f32[112,3584]{1,0:T(8,128)} %m_ref.1) | copy-start | bytes 4816900
  156.8 19.3 %collective-permute-start.5 = (f32[4,128,896]{2,1,0:T(8,128)S(1)}, f32[4,128,896]{2,1,0:T(8,128)S(1)}, u32[]{:S(2)}, u32[]{:S(2)}) collective-permute-start(f32[4,128,896]{2,1,0:T(8,128)S(1)} %all_to_all.39.own_ref), channel_id=1, source_target_pairs={{0,8},{8,0},{1,9},{9,1},{2,10},{10,2},{3,11},{11,3},{4,12},{12,4},... | collective-permute-start | bytes 5505032 | tf_op jit(solution)/shard_map/ppermute | solution.py:325

commit v9 on v7

--- a/solution.py
+++ b/solution.py
@@ -167,6 +167,23 @@
 
 def row(pair):
     return jnp.concatenate([pair[:1], pair[1:2]], axis=1)
+
+
+def stack_kernel(*refs):
+    for j, ref in enumerate(refs[:-1]):
+        refs[-1][j] = ref[...]
+
+
+def stack(blocks):
+    rows, part = blocks[0].shape
+    return pl.pallas_call(
+        stack_kernel,
+        in_specs=[VMEM] * NX,
+        out_specs=VMEM,
+        out_shape=jax.ShapeDtypeStruct((NX, rows, part), jnp.float32),
+        compiler_params=PARAMS,
+        cost_estimate=cost(NX * rows * part, 8 * NX * rows * part),
+    )(*blocks)
 
 
 def squares_kernel(own_ref, out_ref):
@@ -224,9 +241,11 @@
     dot = functools.partial(jnp.dot, preferred_element_type=jnp.float32)
     copies = []
     for j in range(NX):
-        own_at = jnp.where(core == 0, j, NX - 1 - j)
+        ahead = lax.rem(NX + j - lax.axis_index("x"), NX)
+        behind = lax.rem(NX - j + lax.axis_index("x"), NX)
+        own_at, oth_at = jnp.where(core == 0, behind, ahead), jnp.where(core == 0, ahead, behind)
         own, columns = own_ref[own_at], pl.ds(j * part, part)
-        high, low = split(jnp.concatenate([own, oth_ref[NX - 1 - own_at]], axis=0))
+        high, low = split(jnp.concatenate([own, oth_ref[oth_at]], axis=0))
         sums, rest = dot(left, high), dot(left_high, low)
         feedback = sums[:rows] + sums[rows : 2 * rows] + rest[:rows]
         update = sums[2 * rows : 3 * rows] + sums[3 * rows :] + rest[rows:]
@@ -321,7 +340,7 @@
     square = jnp.sum(got[:, :2, part : part + half], axis=0) + norm_eps
 
     own, square = lax.optimization_barrier((got[:, :, :part].reshape(half, part), square))
-    own = spread(own, ("x", "core"), NX)
+    own = stack([own] + [lax.ppermute(own, ("x", "core"), turn(j)) for j in range(1, NX)])
     oth = lax.ppermute(own, "core", SWAP)
     sums = exchange(row_squares(own), ("core", "z"))
     momentum_new, update, basis_new = last_out(

time: 178 us -> 178 us (level)
  blocking collectives: 116 us -> 94.9 us
  waiting for transfers between devices: 14 us -> 32.5 us
  starting transfers between devices: 32.6 us -> 36.3 us
    all_to_all x5 -> x4, blocking collectives: 106 us -> 83.5 us  [opposed(): lax.all_to_all(blocks, axes, 0, 0, axis_index_groups=groups, tiled=True)]
    ppermute x0 -> x3, waiting for transfers between devices: none -> 18.4 us  [shards(): lax.ppermute(own, ('x', 'core'), turn(j))]
    ppermute x0 -> x3, starting transfers between devices: none -> 8.9 us  [shards(): lax.ppermute(own, ('x', 'core'), turn(j))]
    ppermute x1, starting transfers between devices: 7.2 us -> 2.05 us  [shards(): oth = lax.ppermute(own, 'core', SWAP)]
  transfers between devices with their start and end apart: 7 -> 10, of which waited for: 3 -> 6; matrix products, arithmetic and copies ran while one was open for 0% -> 0% of each run, Pallas kernels for 2% -> 2%
where the time goes in v9:
time: 178 us; the launch traced here: 176 us
  blocking collectives  94.9 us (53%)
  starting transfers between devices  36.3 us (20%)
  waiting for transfers between devices  32.5 us (18%)
  Pallas kernels  7.5 us (4%)
  other arithmetic  1.98 us (1%)
  local copies, waits for them, and re-layouts  1.93 us (1%)
    all_to_all x4, blocking collectives, opposed(): lax.all_to_all(blocks, axes, 0, 0, axis_index_groups=groups, tiled=True)  83.5 us
    ppermute x3, waiting for transfers between devices, shards(): lax.ppermute(own, ('x', 'core'), turn(j))  18.4 us
    ppermute x3, waiting for transfers between devices, shards(): lax.ppermute(blocks[j], ('x', 'core'), turn(j))  12.3 us
    all_to_all x1, blocking collectives, exchange(): return lax.all_to_all(blocks, axes, 0, 0, tiled=True)  11.4 us
    all_to_all x1, starting transfers between devices, opposed(): lax.all_to_all(blocks, axes, 0, 0, axis_index_groups=groups, tiled=True)  10.7 us
    ppermute x3, starting transfers between devices, shards(): lax.ppermute(blocks[j], ('x', 'core'), turn(j))  10.2 us
    ppermute x3, starting transfers between devices, shards(): lax.ppermute(own, ('x', 'core'), turn(j))  8.9 us
  transfers between devices with their start and end apart: 10, of which 6 were waited for; matrix products, arithmetic and copies ran while one was open for 0% of the time, Pallas kernels for 2%

profile of v9, /device:TPU:1, one launch (start us, length us, event | category | flops | bytes accessed | tf_op | source)
XLA Modules:
  0.0 176.0 jit_solution(11683683501909062602)
XLA Ops:
  0.6 1.8 %convert_add_fusion.c_ref = f32[112,3584]{1,0:T(8,128)S(1)} fusion(f32[112,3584]{1,0:T(8,128)} %m_ref.1, bf16[112,3584]{1,0:T(8,128)(2,1)} %g_ref.1), kind=kLoop, calls=%fused_computation | loop fusion | flops 802816 | bytes 4014080 | tf_op jit(solution)/shard_map/add | solution.py:316
  2.4 0.0 copy-start.4
  2.4 0.1 shard_map.58
  2.5 5.2 %collective-permute-start = (f32[112,896]{1,0:T(8,128)S(1)}, f32[112,896]{1,0:T(8,128)S(1)}, u32[]{:S(2)}, u32[]{:S(2)}) collective-permute-start(f32[112,896]{1,0:T(8,128)S(1)} %get-tuple-element.34), channel_id=1, source_target_pairs={{0,16},{8,56},{16,32},{24,8},{32,48},{40,24},{48,0},{56,40},{1,17}... | collective-permute-start | bytes 1204232 | tf_op jit(solution)/shard_map/ppermute | solution.py:319
  7.8 2.4 %collective-permute-start.1 = (f32[112,896]{1,0:T(8,128)S(1)}, f32[112,896]{1,0:T(8,128)S(1)}, u32[]{:S(2)}, u32[]{:S(2)}) collective-permute-start(f32[112,896]{1,0:T(8,128)S(1)} %get-tuple-element.35), channel_id=1, source_target_pairs={{0,32},{8,40},{16,48},{24,56},{32,0},{40,8},{48,16},{56,24},{1,33}... | collective-permute-start | bytes 1204232 | tf_op jit(solution)/shard_map/ppermute | solution.py:319
  10.2 2.5 %collective-permute-start.2 = (f32[112,896]{1,0:T(8,128)S(1)}, f32[112,896]{1,0:T(8,128)S(1)}, u32[]{:S(2)}, u32[]{:S(2)}) collective-permute-start(f32[112,896]{1,0:T(8,128)S(1)} %get-tuple-element.36), channel_id=1, source_target_pairs={{0,48},{8,24},{16,0},{24,40},{32,16},{40,56},{48,32},{56,8},{1,49}... | collective-permute-start | bytes 1204232 | tf_op jit(solution)/shard_map/ppermute | solution.py:319
  12.7 0.0 copy-done.4
  12.7 0.8 shard_map.59
  13.6 10.7 %all-to-all-start = ((f32[32,4,896]{2,1,0:T(4,128)}), f32[32,4,896]{2,1,0:T(4,128)S(1)}, u32[]{:S(2)}, u32[]{:S(2)}) async-start(f32[32,4,896]{2,1,0:T(4,128)} %shard_map.59), calls=%async_computation | async-start | bytes 917504 | tf_op jit(solution)/shard_map/all_to_all | solution.py:301
  24.3 0.0 collective-permute-done.refs_1_
  24.3 0.0 collective-permute-done.1.refs_2_
  24.3 12.3 %collective-permute-done.2.refs_3_ = f32[112,896]{1,0:T(8,128)S(1)} collective-permute-done((f32[112,896]{1,0:T(8,128)S(1)}, f32[112,896]{1,0:T(8,128)S(1)}, u32[]{:S(2)}, u32[]{:S(2)}) %collective-permute-start.2) | collective-permute-done | bytes 401440 | tf_op jit(solution)/shard_map/ppermute | solution.py:319
  36.5 0.0 copy-start.2
  36.5 0.7 copy-done.2
  37.3 0.0 copy-start.3
  37.3 1.0 copy-done.3
  38.3 0.3 shard_map.60
  38.6 0.0 all-to-all-done.basis_ref
  38.6 1.9 %collective-permute-start.3 = (f32[32,4,896]{2,1,0:T(4,128)S(1)}, f32[32,4,896]{2,1,0:T(4,128)S(1)}, u32[]{:S(2)}, u32[]{:S(2)}) collective-permute-start(f32[32,4,896]{2,1,0:T(4,128)S(1)} %all-to-all-done.basis_ref), channel_id=1, source_target_pairs={{0,8},{8,0},{1,9},{9,1},{2,10},{10,2},{3,11},{11,3},{4,12},{12,4},... | collective-permute-start | bytes 1376264 | tf_op jit(solution)/shard_map/ppermute | solution.py:323
  40.5 0.8 shard_map.61
  41.4 0.9 collective-permute-done.3.basis_ref
  42.3 0.8 shard_map.62
  43.2 27.8 %all_to_all.30 = f32[32,16,256]{2,1,0:T(8,128)S(1)} all-to-all(f32[32,16,256]{2,1,0:T(8,128)S(1)} %bitcast.11), channel_id=1, replica_groups={{0,1,2,3,4,5,6,7,16,17,18,19,20,21,22,23,32,33,34,35,36,37,38,39,48,49,..., dimensions={0} | all-to-all | bytes 1048576 | tf_op jit(solution)/shard_map/all_to_all | solution.py:301
  71.1 0.1 broadcast_in_dim.4
  71.1 22.0 %all_to_all.31 = f32[32,16,256]{2,1,0:T(8,128)S(1)} all-to-all(f32[32,16,256]{2,1,0:T(8,128)S(1)} %broadcast_in_dim.4), channel_id=1, replica_groups={{0,1,2,3,4,5,6,7,16,17,18,19,20,21,22,23,32,33,34,35,36,37,38,39,48,49,..., dimensions={0} | all-to-all | bytes 1048576 | tf_op jit(solution)/shard_map/all_to_all | solution.py:301
  93.1 0.6 shard_map.64
  93.7 2.6 %collective-permute-start.4 = (f32[136,896]{1,0:T(8,128)S(1)}, f32[136,896]{1,0:T(8,128)S(1)}, u32[]{:S(2)}, u32[]{:S(2)}) collective-permute-start(f32[136,896]{1,0:T(8,128)S(1)} %shard_map.64), channel_id=1, source_target_pairs={{0,8},{8,0},{1,9},{9,1},{2,10},{10,2},{3,11},{11,3},{4,12},{12,4},... | collective-permute-start | bytes 1462280 | tf_op jit(solution)/shard_map/ppermute | solution.py:331
  96.4 0.6 shard_map.63
  97.0 0.8 collective-permute-done.4
  97.8 0.1 add.17
  98.0 15.5 %all_to_all.32 = f32[8,16,896]{2,1,0:T(8,128)S(1)} all-to-all(f32[8,16,896]{2,1,0:T(8,128)S(1)} %bitcast.12), channel_id=1, replica_groups={{0,64,128,192,256,320,384,448},{456,392,328,264,200,136,72,8},{1,65,129..., dimensions={0} | all-to-all | bytes 917504 | tf_op jit(solution)/shard_map/all_to_all | solution.py:301
  113.5 18.3 %all_to_all.33 = f32[8,16,1024]{2,1,0:T(8,128)S(1)} all-to-all(f32[8,16,1024]{2,1,0:T(8,128)S(1)} %broadcast_in_dim.5), channel_id=1, replica_groups={{0,64,128,192,256,320,384,448},{456,392,328,264,200,136,72,8},{1,65,129..., dimensions={0} | all-to-all | bytes 1048576 | tf_op jit(solution)/shard_map/all_to_all | solution.py:301
  131.8 1.9 %collective-permute-start.7 = (f32[128,896]{1,0:T(8,128)S(1)}, f32[128,896]{1,0:T(8,128)S(1)}, u32[]{:S(2)}, u32[]{:S(2)}) collective-permute-start(f32[128,896]{1,0:T(8,128)S(1)} %bitcast.7), channel_id=1, source_target_pairs={{0,48},{8,24},{16,0},{24,40},{32,16},{40,56},{48,32},{56,8},{1,49}... | collective-permute-start | bytes 1376264 | tf_op jit(solution)/shard_map/ppermute | solution.py:343
  133.8 5.1 %collective-permute-start.6 = (f32[128,896]{1,0:T(8,128)S(1)}, f32[128,896]{1,0:T(8,128)S(1)}, u32[]{:S(2)}, u32[]{:S(2)}) collective-permute-start(f32[128,896]{1,0:T(8,128)S(1)} %bitcast.8), channel_id=1, source_target_pairs={{0,32},{8,40},{16,48},{24,56},{32,0},{40,8},{48,16},{56,24},{1,33}... | collective-permute-start | bytes 1376264 | tf_op jit(solution)/shard_map/ppermute | solution.py:343
  138.8 1.9 %collective-permute-start.5 = (f32[128,896]{1,0:T(8,128)S(1)}, f32[128,896]{1,0:T(8,128)S(1)}, u32[]{:S(2)}, u32[]{:S(2)}) collective-permute-start(f32[128,896]{1,0:T(8,128)S(1)} %bitcast.9), channel_id=1, source_target_pairs={{0,16},{8,56},{16,32},{24,8},{32,48},{40,24},{48,0},{56,40},{1,17}... | collective-permute-start | bytes 1376264 | tf_op jit(solution)/shard_map/ppermute | solution.py:343
  140.8 1.5 collective-permute-done.7.refs_3_
  142.3 7.3 %collective-permute-done.6.refs_2_ = f32[128,896]{1,0:T(8,128)S(1)} collective-permute-done((f32[128,896]{1,0:T(8,128)S(1)}, f32[128,896]{1,0:T(8,128)S(1)}, u32[]{:S(2)}, u32[]{:S(2)}) %collective-permute-start.6) | collective-permute-done | bytes 458784 | tf_op jit(solution)/shard_map/ppermute | solution.py:343
  149.6 9.6 %collective-permute-done.5.refs_1_ = f32[128,896]{1,0:T(8,128)S(1)} collective-permute-done((f32[128,896]{1,0:T(8,128)S(1)}, f32[128,896]{1,0:T(8,128)S(1)}, u32[]{:S(2)}, u32[]{:S(2)}) %collective-permute-start.5) | collective-permute-done | bytes 458784 | tf_op jit(solution)/shard_map/ppermute | solution.py:343
  159.2 0.0 copy-start.1
  159.2 0.1 shard_map.65.own_ref
  159.3 0.0 copy-start
  159.3 2.1 %collective-permute-start.8 = (f32[4,128,896]{2,1,0:T(8,128)S(1)}, f32[4,128,896]{2,1,0:T(8,128)S(1)}, u32[]{:S(2)}, u32[]{:S(2)}) collective-permute-start(f32[4,128,896]{2,1,0:T(8,128)S(1)} %shard_map.65.own_ref), channel_id=1, source_target_pairs={{0,8},{8,0},{1,9},{9,1},{2,10},{10,2},{3,11},{11,3},{4,12},{12,4},... | collective-permute-start | bytes 5505032 | tf_op jit(solution)/shard_map/ppermute | solution.py:344
  161.4 0.6 shard_map.66
  162.0 11.4 %all_to_all.34.sums_ref = f32[16,8,128]{2,1,0:T(8,128)S(1)} all-to-all(f32[16,8,128]{2,1,0:T(8,128)S(1)} %shard_map.66), channel_id=1, replica_groups=mesh['y'=8,'x'=4,'core'=2,'z'=8] {'core','z'}, dimensions={0} | all-to-all | bytes 131072 | tf_op jit(solution)/shard_map/all_to_all | solution.py:288
  173.4 0.0 collective-permute-done.8.oth_ref
  173.4 0.0 copy-done.1
  173.4 0.0 copy-done
  173.4 2.6 %shard_map.67 = (f32[112,3584]{1,0:T(8,128)}, bf16[112,3584]{1,0:T(8,128)(2,1)}, f32[4,3584]{1,0:T(4,128)}) custom-call(f32[112,256]{1,0:T(8,128)S(1)} %get-tuple-element.42.mine_ref, f32[2,128]{1,0:T(2,128)S(1)} %broadcast_add_fusion.square_ref, f32[16,8,128]{2,1,0:T(8,128)S(1)} %all_to_all.34.sums_ref, f32[112,3584]{1,0:T(8,128)S(1)} %copy-done, ...), custom_call_target="tpu_custom_call" | custom-call | flops 1233125376 | bytes 10092544 | tf_op jit(solution)/shard_map/pallas_call | solution.py:275
  (10 shorter events, 0.2 us)
Async XLA Ops:
  2.4 10.3 %copy-start.4 = (f32[4,3584]{1,0:T(4,128)S(1)}, f32[4,3584]{1,0:T(4,128)}, u32[]{:S(2)}) copy-start(f32[4,3584]{1,0:T(4,128)} %basis_ref.1) | copy-start | bytes 172036
  2.5 21.7 %collective-permute-start = (f32[112,896]{1,0:T(8,128)S(1)}, f32[112,896]{1,0:T(8,128)S(1)}, u32[]{:S(2)}, u32[]{:S(2)}) collective-permute-start(f32[112,896]{1,0:T(8,128)S(1)} %get-tuple-element.34), channel_id=1, source_target_pairs={{0,16},{8,56},{16,32},{24,8},{32,48},{40,24},{48,0},{56,40},{1,17}... | collective-permute-start | bytes 1204232 | tf_op jit(solution)/shard_map/ppermute | solution.py:319
  7.8 16.5 %collective-permute-start.1 = (f32[112,896]{1,0:T(8,128)S(1)}, f32[112,896]{1,0:T(8,128)S(1)}, u32[]{:S(2)}, u32[]{:S(2)}) collective-permute-start(f32[112,896]{1,0:T(8,128)S(1)} %get-tuple-element.35), channel_id=1, source_target_pairs={{0,32},{8,40},{16,48},{24,56},{32,0},{40,8},{48,16},{56,24},{1,33}... | collective-permute-start | bytes 1204232 | tf_op jit(solution)/shard_map/ppermute | solution.py:319
  10.2 26.3 %collective-permute-start.2 = (f32[112,896]{1,0:T(8,128)S(1)}, f32[112,896]{1,0:T(8,128)S(1)}, u32[]{:S(2)}, u32[]{:S(2)}) collective-permute-start(f32[112,896]{1,0:T(8,128)S(1)} %get-tuple-element.36), channel_id=1, source_target_pairs={{0,48},{8,24},{16,0},{24,40},{32,16},{40,56},{48,32},{56,8},{1,49}... | collective-permute-start | bytes 1204232 | tf_op jit(solution)/shard_map/ppermute | solution.py:319
  13.6 25.0 %all-to-all-start = ((f32[32,4,896]{2,1,0:T(4,128)}), f32[32,4,896]{2,1,0:T(4,128)S(1)}, u32[]{:S(2)}, u32[]{:S(2)}) async-start(f32[32,4,896]{2,1,0:T(4,128)} %shard_map.59), calls=%async_computation | async-start | bytes 917504 | tf_op jit(solution)/shard_map/all_to_all | solution.py:301
  36.5 0.7 copy-start.2
  37.3 1.0 copy-start.3
  38.6 3.7 %collective-permute-start.3 = (f32[32,4,896]{2,1,0:T(4,128)S(1)}, f32[32,4,896]{2,1,0:T(4,128)S(1)}, u32[]{:S(2)}, u32[]{:S(2)}) collective-permute-start(f32[32,4,896]{2,1,0:T(4,128)S(1)} %all-to-all-done.basis_ref), channel_id=1, source_target_pairs={{0,8},{8,0},{1,9},{9,1},{2,10},{10,2},{3,11},{11,3},{4,12},{12,4},... | collective-permute-start | bytes 1376264 | tf_op jit(solution)/shard_map/ppermute | solution.py:323
  93.7 4.1 %collective-permute-start.4 = (f32[136,896]{1,0:T(8,128)S(1)}, f32[136,896]{1,0:T(8,128)S(1)}, u32[]{:S(2)}, u32[]{:S(2)}) collective-permute-start(f32[136,896]{1,0:T(8,128)S(1)} %shard_map.64), channel_id=1, source_target_pairs={{0,8},{8,0},{1,9},{9,1},{2,10},{10,2},{3,11},{11,3},{4,12},{12,4},... | collective-permute-start | bytes 1462280 | tf_op jit(solution)/shard_map/ppermute | solution.py:331
  131.8 10.4 %collective-permute-start.7 = (f32[128,896]{1,0:T(8,128)S(1)}, f32[128,896]{1,0:T(8,128)S(1)}, u32[]{:S(2)}, u32[]{:S(2)}) collective-permute-start(f32[128,896]{1,0:T(8,128)S(1)} %bitcast.7), channel_id=1, source_target_pairs={{0,48},{8,24},{16,0},{24,40},{32,16},{40,56},{48,32},{56,8},{1,49}... | collective-permute-start | bytes 1376264 | tf_op jit(solution)/shard_map/ppermute | solution.py:343
  133.8 15.8 %collective-permute-start.6 = (f32[128,896]{1,0:T(8,128)S(1)}, f32[128,896]{1,0:T(8,128)S(1)}, u32[]{:S(2)}, u32[]{:S(2)}) collective-permute-start(f32[128,896]{1,0:T(8,128)S(1)} %bitcast.8), channel_id=1, source_target_pairs={{0,32},{8,40},{16,48},{24,56},{32,0},{40,8},{48,16},{56,24},{1,33}... | collective-permute-start | bytes 1376264 | tf_op jit(solution)/shard_map/ppermute | solution.py:343
  138.8 20.3 %collective-permute-start.5 = (f32[128,896]{1,0:T(8,128)S(1)}, f32[128,896]{1,0:T(8,128)S(1)}, u32[]{:S(2)}, u32[]{:S(2)}) collective-permute-start(f32[128,896]{1,0:T(8,128)S(1)} %bitcast.9), channel_id=1, source_target_pairs={{0,16},{8,56},{16,32},{24,8},{32,48},{40,24},{48,0},{56,40},{1,17}... | collective-permute-start | bytes 1376264 | tf_op jit(solution)/shard_map/ppermute | solution.py:343
  159.2 14.2 %copy-start.1 = (bf16[112,3584]{1,0:T(8,128)(2,1)S(1)}, bf16[112,3584]{1,0:T(8,128)(2,1)}, u32[]{:S(2)}) copy-start(bf16[112,3584]{1,0:T(8,128)(2,1)} %g_ref.1) | copy-start | bytes 2408452
  159.3 14.1 %copy-start = (f32[112,3584]{1,0:T(8,128)S(1)}, f32[112,3584]{1,0:T(8,128)}, u32[]{:S(2)}) copy-start(f32[112,3584]{1,0:T(8,128)} %m_ref.1) | copy-start | bytes 4816900
  159.3 14.1 %collective-permute-start.8 = (f32[4,128,896]{2,1,0:T(8,128)S(1)}, f32[4,128,896]{2,1,0:T(8,128)S(1)}, u32[]{:S(2)}, u32[]{:S(2)}) collective-permute-start(f32[4,128,896]{2,1,0:T(8,128)S(1)} %shard_map.65.own_ref), channel_id=1, source_target_pairs={{0,8},{8,0},{1,9},{9,1},{2,10},{10,2},{3,11},{11,3},{4,12},{12,4},... | collective-permute-start | bytes 5505032 | tf_op jit(solution)/shard_map/ppermute | solution.py:344

commit v10 on v7

--- a/solution.py
+++ b/solution.py
@@ -45,28 +45,11 @@
     return lax.rem(lax.axis_index("x") + steps, NX)
 
 
-def deal_kernel(c_ref, *blocks):
+def deal_kernel(c_ref, basis_ref, *refs):
+    blocks, pieces_ref = refs[:NX], refs[NX]
     part = blocks[0].shape[1]
     for j, ref in enumerate(blocks):
-        at = x_away(j)
-        ref[...] = c_ref[:, pl.ds(pl.multiple_of(at * part, 128), part)]
-
-
-def deal(combined):
-    rows, cols = combined.shape
-    part = cols // NX
-    return pl.pallas_call(
-        deal_kernel,
-        in_specs=[VMEM],
-        out_specs=[VMEM] * NX,
-        out_shape=[jax.ShapeDtypeStruct((rows, part), jnp.float32)] * NX,
-        compiler_params=PARAMS,
-        cost_estimate=cost(rows * cols, 8 * rows * cols),
-    )(combined)
-
-
-def pieces_kernel(basis_ref, after_ref, pieces_ref):
-    part = pieces_ref.shape[2]
+        ref[...] = c_ref[:, pl.ds(pl.multiple_of(x_away(j) * part, 128), part)]
     for to in range(NX):
         at = jnp.where(lax.axis_index("core") == 0, to, NX - 1 - to)
         piece = basis_ref[:, pl.ds(pl.multiple_of(at * part, 128), part)]
@@ -74,17 +57,18 @@
             pieces_ref[y * NX + to] = piece
 
 
-def basis_pieces(basis, after):
-    ranks, cols = basis.shape
-    pieces = (NY * NX, ranks, cols // NX)
-    return pl.pallas_call(
-        pieces_kernel,
-        in_specs=[VMEM, ANY],
-        out_specs=VMEM,
-        out_shape=jax.ShapeDtypeStruct(pieces, jnp.float32),
-        compiler_params=PARAMS,
-        cost_estimate=cost(10**10, 10**8),
-    )(basis, after)
+def deal(combined, basis):
+    rows, cols = combined.shape
+    ranks, part = basis.shape[0], cols // NX
+    shapes = [(rows, part)] * NX + [(NY * NX, ranks, part)]
+    return pl.pallas_call(
+        deal_kernel,
+        in_specs=[VMEM] * 2,
+        out_specs=[VMEM] * (NX + 1),
+        out_shape=[jax.ShapeDtypeStruct(shape, jnp.float32) for shape in shapes],
+        compiler_params=PARAMS,
+        cost_estimate=cost(rows * cols, 8 * rows * cols),
+    )(combined, basis)
 
 
 def tall_kernel(*refs):
@@ -294,8 +278,7 @@
     own_ranks = NX * rank_rows
     padded = -(-rows // (8 * NZ)) * 8 * NZ
 
-    blocks = deal(momentum + gradient.astype(jnp.float32))
-    pieces = basis_pieces(basis_panel, blocks[0])
+    *blocks, pieces = deal(momentum + gradient.astype(jnp.float32), basis_panel)
     blocks = [blocks[0]] + [
         lax.ppermute(blocks[j], ("x", "core"), turn(j)) for j in range(1, NX)
     ]

time: 178 us -> 178 us (level)
  transfers between devices with their start and end apart: 7 -> 7, of which waited for: 3 -> 3; matrix products, arithmetic and copies ran while one was open for 0% -> 0% of each run, Pallas kernels for 2% -> 1%
where the time goes in v10:
time: 178 us; the launch traced here: 175 us
  blocking collectives  116 us (65%)
  starting transfers between devices  32.6 us (18%)
  waiting for transfers between devices  14.9 us (8%)
  Pallas kernels  7.37 us (4%)
  local copies, waits for them, and re-layouts  2.04 us (1%)
  other arithmetic  2 us (1%)
    all_to_all x5, blocking collectives, opposed(): lax.all_to_all(blocks, axes, 0, 0, axis_index_groups=groups, tiled=True)  105 us
    ppermute x3, waiting for transfers between devices, shards(): lax.ppermute(blocks[j], ('x', 'core'), turn(j))  13.2 us
    all_to_all x1, blocking collectives, exchange(): return lax.all_to_all(blocks, axes, 0, 0, tiled=True)  10.8 us
    all_to_all x1, starting transfers between devices, opposed(): lax.all_to_all(blocks, axes, 0, 0, axis_index_groups=groups, tiled=True)  10.7 us
    ppermute x3, starting transfers between devices, shards(): lax.ppermute(blocks[j], ('x', 'core'), turn(j))  10.1 us
    ppermute x1, starting transfers between devices, shards(): oth = lax.ppermute(own, 'core', SWAP)  7.19 us
  transfers between devices with their start and end apart: 7, of which 3 were waited for; matrix products, arithmetic and copies ran while one was open for 0% of the time, Pallas kernels for 1%

profile of v10, /device:TPU:1, one launch (start us, length us, event | category | flops | bytes accessed | tf_op | source)
XLA Modules:
  0.0 175.3 jit_solution(3452456213387898452)
XLA Ops:
  0.6 0.0 copy-start.2
  0.6 1.8 %convert_add_fusion.c_ref = f32[112,3584]{1,0:T(8,128)S(1)} fusion(f32[112,3584]{1,0:T(8,128)} %m_ref.1, bf16[112,3584]{1,0:T(8,128)(2,1)} %g_ref.1), kind=kLoop, calls=%fused_computation | loop fusion | flops 802816 | bytes 4014080 | tf_op jit(solution)/shard_map/add | solution.py:281
  2.4 0.0 copy-done.2
  2.4 0.9 shard_map.58
  3.4 5.2 %collective-permute-start = (f32[112,896]{1,0:T(8,128)S(1)}, f32[112,896]{1,0:T(8,128)S(1)}, u32[]{:S(2)}, u32[]{:S(2)}) collective-permute-start(f32[112,896]{1,0:T(8,128)S(1)} %get-tuple-element.36), channel_id=1, source_target_pairs={{0,16},{8,56},{16,32},{24,8},{32,48},{40,24},{48,0},{56,40},{1,17}... | collective-permute-start | bytes 1204232 | tf_op jit(solution)/shard_map/ppermute | solution.py:283
  8.6 2.4 %collective-permute-start.1 = (f32[112,896]{1,0:T(8,128)S(1)}, f32[112,896]{1,0:T(8,128)S(1)}, u32[]{:S(2)}, u32[]{:S(2)}) collective-permute-start(f32[112,896]{1,0:T(8,128)S(1)} %get-tuple-element.37), channel_id=1, source_target_pairs={{0,32},{8,40},{16,48},{24,56},{32,0},{40,8},{48,16},{56,24},{1,33}... | collective-permute-start | bytes 1204232 | tf_op jit(solution)/shard_map/ppermute | solution.py:283
  11.0 2.5 %collective-permute-start.2 = (f32[112,896]{1,0:T(8,128)S(1)}, f32[112,896]{1,0:T(8,128)S(1)}, u32[]{:S(2)}, u32[]{:S(2)}) collective-permute-start(f32[112,896]{1,0:T(8,128)S(1)} %get-tuple-element.38), channel_id=1, source_target_pairs={{0,48},{8,24},{16,0},{24,40},{32,16},{40,56},{48,32},{56,8},{1,49}... | collective-permute-start | bytes 1204232 | tf_op jit(solution)/shard_map/ppermute | solution.py:283
  13.5 10.7 %all-to-all-start = ((f32[32,4,896]{2,1,0:T(4,128)}), f32[32,4,896]{2,1,0:T(4,128)S(1)}, u32[]{:S(2)}, u32[]{:S(2)}) async-start(f32[32,4,896]{2,1,0:T(4,128)} %get-tuple-element.34), calls=%async_computation | async-start | bytes 917504 | tf_op jit(solution)/shard_map/all_to_all | solution.py:266
  24.3 0.0 collective-permute-done.refs_1_
  24.3 0.0 collective-permute-done.1.refs_2_
  24.3 13.2 %collective-permute-done.2.refs_3_ = f32[112,896]{1,0:T(8,128)S(1)} collective-permute-done((f32[112,896]{1,0:T(8,128)S(1)}, f32[112,896]{1,0:T(8,128)S(1)}, u32[]{:S(2)}, u32[]{:S(2)}) %collective-permute-start.2) | collective-permute-done | bytes 401440 | tf_op jit(solution)/shard_map/ppermute | solution.py:283
  37.4 0.0 copy-start.3
  37.4 0.7 copy-done.3
  38.2 0.0 copy-start.4
  38.2 1.0 copy-done.4
  39.2 0.3 shard_map.59
  39.5 0.0 all-to-all-done.basis_ref
  39.5 1.9 %collective-permute-start.3 = (f32[32,4,896]{2,1,0:T(4,128)S(1)}, f32[32,4,896]{2,1,0:T(4,128)S(1)}, u32[]{:S(2)}, u32[]{:S(2)}) collective-permute-start(f32[32,4,896]{2,1,0:T(4,128)S(1)} %all-to-all-done.basis_ref), channel_id=1, source_target_pairs={{0,8},{8,0},{1,9},{9,1},{2,10},{10,2},{3,11},{11,3},{4,12},{12,4},... | collective-permute-start | bytes 1376264 | tf_op jit(solution)/shard_map/ppermute | solution.py:287
  41.4 0.8 shard_map.60
  42.3 0.9 collective-permute-done.3.basis_ref
  43.2 0.8 shard_map.61
  44.1 26.9 %all_to_all.35 = f32[32,16,256]{2,1,0:T(8,128)S(1)} all-to-all(f32[32,16,256]{2,1,0:T(8,128)S(1)} %bitcast.7), channel_id=1, replica_groups={{0,1,2,3,4,5,6,7,16,17,18,19,20,21,22,23,32,33,34,35,36,37,38,39,48,49,..., dimensions={0} | all-to-all | bytes 1048576 | tf_op jit(solution)/shard_map/all_to_all | solution.py:266
  71.1 0.1 broadcast_in_dim.6
  71.1 22.0 %all_to_all.36 = f32[32,16,256]{2,1,0:T(8,128)S(1)} all-to-all(f32[32,16,256]{2,1,0:T(8,128)S(1)} %broadcast_in_dim.6), channel_id=1, replica_groups={{0,1,2,3,4,5,6,7,16,17,18,19,20,21,22,23,32,33,34,35,36,37,38,39,48,49,..., dimensions={0} | all-to-all | bytes 1048576 | tf_op jit(solution)/shard_map/all_to_all | solution.py:266
  93.1 0.6 shard_map.63
  93.7 2.6 %collective-permute-start.4 = (f32[136,896]{1,0:T(8,128)S(1)}, f32[136,896]{1,0:T(8,128)S(1)}, u32[]{:S(2)}, u32[]{:S(2)}) collective-permute-start(f32[136,896]{1,0:T(8,128)S(1)} %shard_map.63), channel_id=1, source_target_pairs={{0,8},{8,0},{1,9},{9,1},{2,10},{10,2},{3,11},{11,3},{4,12},{12,4},... | collective-permute-start | bytes 1462280 | tf_op jit(solution)/shard_map/ppermute | solution.py:295
  96.4 0.6 shard_map.62
  97.0 0.8 collective-permute-done.4
  97.8 0.1 add.17
  97.9 15.5 %all_to_all.37 = f32[8,16,896]{2,1,0:T(8,128)S(1)} all-to-all(f32[8,16,896]{2,1,0:T(8,128)S(1)} %bitcast.8), channel_id=1, replica_groups={{0,64,128,192,256,320,384,448},{456,392,328,264,200,136,72,8},{1,65,129..., dimensions={0} | all-to-all | bytes 917504 | tf_op jit(solution)/shard_map/all_to_all | solution.py:266
  113.5 18.3 %all_to_all.38 = f32[8,16,1024]{2,1,0:T(8,128)S(1)} all-to-all(f32[8,16,1024]{2,1,0:T(8,128)S(1)} %broadcast_in_dim.7), channel_id=1, replica_groups={{0,64,128,192,256,320,384,448},{456,392,328,264,200,136,72,8},{1,65,129..., dimensions={0} | all-to-all | bytes 1048576 | tf_op jit(solution)/shard_map/all_to_all | solution.py:266
  131.8 0.1 broadcast_in_dim.8
  132.0 0.0 copy-start.1
  132.0 22.1 %all_to_all.39.own_ref = f32[4,128,896]{2,1,0:T(8,128)S(1)} all-to-all(f32[4,128,896]{2,1,0:T(8,128)S(1)} %broadcast_in_dim.8), channel_id=1, replica_groups={{0,16,32,48},{56,40,24,8},{1,17,33,49},{57,41,25,9},{2,18,34,50},{58,42..., dimensions={0} | all-to-all | bytes 3670016 | tf_op jit(solution)/shard_map/all_to_all | solution.py:266
  154.1 0.0 copy-start
  154.1 7.2 %collective-permute-start.5 = (f32[4,128,896]{2,1,0:T(8,128)S(1)}, f32[4,128,896]{2,1,0:T(8,128)S(1)}, u32[]{:S(2)}, u32[]{:S(2)}) collective-permute-start(f32[4,128,896]{2,1,0:T(8,128)S(1)} %all_to_all.39.own_ref), channel_id=1, source_target_pairs={{0,8},{8,0},{1,9},{9,1},{2,10},{10,2},{3,11},{11,3},{4,12},{12,4},... | collective-permute-start | bytes 5505032 | tf_op jit(solution)/shard_map/ppermute | solution.py:308
  161.3 0.6 shard_map.64
  161.9 10.8 %all_to_all.40.sums_ref = f32[16,8,128]{2,1,0:T(8,128)S(1)} all-to-all(f32[16,8,128]{2,1,0:T(8,128)S(1)} %shard_map.64), channel_id=1, replica_groups=mesh['y'=8,'x'=4,'core'=2,'z'=8] {'core','z'}, dimensions={0} | all-to-all | bytes 131072 | tf_op jit(solution)/shard_map/all_to_all | solution.py:253
  172.7 0.0 collective-permute-done.5.oth_ref
  172.7 0.0 copy-done.1
  172.7 0.0 copy-done
  172.7 2.6 %shard_map.65 = (f32[112,3584]{1,0:T(8,128)}, bf16[112,3584]{1,0:T(8,128)(2,1)}, f32[4,3584]{1,0:T(4,128)}) custom-call(f32[112,256]{1,0:T(8,128)S(1)} %get-tuple-element.44.mine_ref, f32[2,128]{1,0:T(2,128)S(1)} %broadcast_add_fusion.square_ref, f32[16,8,128]{2,1,0:T(8,128)S(1)} %all_to_all.40.sums_ref, f32[112,3584]{1,0:T(8,128)S(1)} %copy-done, ...), custom_call_target="tpu_custom_call" | custom-call | flops 1233125376 | bytes 10092544 | tf_op jit(solution)/shard_map/pallas_call | solution.py:240
  (10 shorter events, 0.3 us)
Async XLA Ops:
  0.6 1.8 %copy-start.2 = (f32[4,3584]{1,0:T(4,128)S(1)}, f32[4,3584]{1,0:T(4,128)}, u32[]{:S(2)}) copy-start(f32[4,3584]{1,0:T(4,128)} %basis_ref.1) | copy-start | bytes 172036
  3.4 20.9 %collective-permute-start = (f32[112,896]{1,0:T(8,128)S(1)}, f32[112,896]{1,0:T(8,128)S(1)}, u32[]{:S(2)}, u32[]{:S(2)}) collective-permute-start(f32[112,896]{1,0:T(8,128)S(1)} %get-tuple-element.36), channel_id=1, source_target_pairs={{0,16},{8,56},{16,32},{24,8},{32,48},{40,24},{48,0},{56,40},{1,17}... | collective-permute-start | bytes 1204232 | tf_op jit(solution)/shard_map/ppermute | solution.py:283
  8.6 15.7 %collective-permute-start.1 = (f32[112,896]{1,0:T(8,128)S(1)}, f32[112,896]{1,0:T(8,128)S(1)}, u32[]{:S(2)}, u32[]{:S(2)}) collective-permute-start(f32[112,896]{1,0:T(8,128)S(1)} %get-tuple-element.37), channel_id=1, source_target_pairs={{0,32},{8,40},{16,48},{24,56},{32,0},{40,8},{48,16},{56,24},{1,33}... | collective-permute-start | bytes 1204232 | tf_op jit(solution)/shard_map/ppermute | solution.py:283
  11.0 26.4 %collective-permute-start.2 = (f32[112,896]{1,0:T(8,128)S(1)}, f32[112,896]{1,0:T(8,128)S(1)}, u32[]{:S(2)}, u32[]{:S(2)}) collective-permute-start(f32[112,896]{1,0:T(8,128)S(1)} %get-tuple-element.38), channel_id=1, source_target_pairs={{0,48},{8,24},{16,0},{24,40},{32,16},{40,56},{48,32},{56,8},{1,49}... | collective-permute-start | bytes 1204232 | tf_op jit(solution)/shard_map/ppermute | solution.py:283
  13.5 25.9 %all-to-all-start = ((f32[32,4,896]{2,1,0:T(4,128)}), f32[32,4,896]{2,1,0:T(4,128)S(1)}, u32[]{:S(2)}, u32[]{:S(2)}) async-start(f32[32,4,896]{2,1,0:T(4,128)} %get-tuple-element.34), calls=%async_computation | async-start | bytes 917504 | tf_op jit(solution)/shard_map/all_to_all | solution.py:266
  37.4 0.7 copy-start.3
  38.2 1.0 copy-start.4
  39.5 3.7 %collective-permute-start.3 = (f32[32,4,896]{2,1,0:T(4,128)S(1)}, f32[32,4,896]{2,1,0:T(4,128)S(1)}, u32[]{:S(2)}, u32[]{:S(2)}) collective-permute-start(f32[32,4,896]{2,1,0:T(4,128)S(1)} %all-to-all-done.basis_ref), channel_id=1, source_target_pairs={{0,8},{8,0},{1,9},{9,1},{2,10},{10,2},{3,11},{11,3},{4,12},{12,4},... | collective-permute-start | bytes 1376264 | tf_op jit(solution)/shard_map/ppermute | solution.py:287
  93.7 4.1 %collective-permute-start.4 = (f32[136,896]{1,0:T(8,128)S(1)}, f32[136,896]{1,0:T(8,128)S(1)}, u32[]{:S(2)}, u32[]{:S(2)}) collective-permute-start(f32[136,896]{1,0:T(8,128)S(1)} %shard_map.63), channel_id=1, source_target_pairs={{0,8},{8,0},{1,9},{9,1},{2,10},{10,2},{3,11},{11,3},{4,12},{12,4},... | collective-permute-start | bytes 1462280 | tf_op jit(solution)/shard_map/ppermute | solution.py:295
  132.0 40.7 %copy-start.1 = (bf16[112,3584]{1,0:T(8,128)(2,1)S(1)}, bf16[112,3584]{1,0:T(8,128)(2,1)}, u32[]{:S(2)}) copy-start(bf16[112,3584]{1,0:T(8,128)(2,1)} %g_ref.1) | copy-start | bytes 2408452
  154.1 18.6 %copy-start = (f32[112,3584]{1,0:T(8,128)S(1)}, f32[112,3584]{1,0:T(8,128)}, u32[]{:S(2)}) copy-start(f32[112,3584]{1,0:T(8,128)} %m_ref.1) | copy-start | bytes 4816900
  154.1 18.6 %collective-permute-start.5 = (f32[4,128,896]{2,1,0:T(8,128)S(1)}, f32[4,128,896]{2,1,0:T(8,128)S(1)}, u32[]{:S(2)}, u32[]{:S(2)}) collective-permute-start(f32[4,128,896]{2,1,0:T(8,128)S(1)} %all_to_all.39.own_ref), channel_id=1, source_target_pairs={{0,8},{8,0},{1,9},{9,1},{2,10},{10,2},{3,11},{11,3},{4,12},{12,4},... | collective-permute-start | bytes 5505032 | tf_op jit(solution)/shard_map/ppermute | solution.py:308
